TPU v7x, 32 devices: a whole 2x2x4 slice. The times are simulated.
32 devices in a mesh: occ: 16 (over z, y, x), vir: 2 (over core).
Axes of the slice: x: 2, y: 2, z: 4, core: 2. Of those that a mesh axis runs over, the one named last changes fastest.
Arguments:
- amplitudes: float32 [2304, 384, 384], P('occ', 'vir'), may hold values from -6 to 6
- integrals: float32 [384, 384, 1536], P('vir', 'occ'), may hold values from -0.015625 to 0.015625
Outputs:
- ladder: float32 [2304, 1536], P('occ', 'vir')
All inputs are finite; a program needn't handle non-finite values.
Results may differ from a plain program's by a relative error of at most 0.000071.
Values sent between devices are 32-bit elements; how exact they have to be, the bound alone decides.
No kernel may reach another device: no remote copies, remote signals or barrier semaphores. Data moves between devices by JAX's collectives and lax.ppermute only.
A program may use at most 384 MiB of HBM per device.

v0:
```python
import jax
import jax.numpy as jnp
from jax import lax
from jax.sharding import PartitionSpec as P

O = 48


def on_device(amplitudes, integrals):
    regrouped = lax.all_to_all(amplitudes, "occ", split_axis=2, concat_axis=0, tiled=True)
    pair_count = regrouped.shape[0]
    col_count = regrouped.shape[1] * regrouped.shape[2]
    flattened = regrouped.reshape(pair_count, col_count)
    grouped = flattened.reshape(O, O, col_count)
    summed = (grouped + jnp.transpose(grouped, (1, 0, 2))).reshape(pair_count, col_count)
    slab_matrix = integrals.reshape(col_count, integrals.shape[2])
    pair_share = lax.psum_scatter(
        jnp.dot(
            summed, slab_matrix, precision=lax.Precision.HIGHEST, preferred_element_type=jnp.float32
        ),
        "occ",
        scatter_dimension=0,
        tiled=True,
    )
    finished = lax.psum_scatter(pair_share, "vir", scatter_dimension=1, tiled=True)
    return finished


def solution(mesh):
    in_specs = (P("occ", "vir", None), P("vir", "occ", None))
    out_specs = P("occ", "vir")
    return jax.shard_map(
        on_device, mesh=mesh, in_specs=in_specs, out_specs=out_specs, check_vma=False
    )
```

profile of v0, /device:TPU:0, one launch (start us, length us, event | category | flops | bytes accessed | tf_op | source)
XLA Modules:
  0.0 2215.8 jit_solution(1910519170207545517)
XLA Ops:
  6.5 0.0 reduce-scatter.3.cloned.1.call-start
  6.5 55.8 %copy.11 = f32[144,192,384]{1,0,2:T(8,128)} copy(f32[144,192,384]{2,1,0:T(8,128)} %param.2) | data formatting | bytes 84934656 | tf_op args[0]
  62.3 1229.1 %all_to_all.15 = f32[144,192,384]{1,0,2:T(8,128)} all-to-all(f32[144,192,384]{1,0,2:T(8,128)} %copy.11), channel_id=1, replica_groups=mesh['occ'=16,'vir'=2] {'occ'}, dimensions={2} | all-to-all | bytes 84934656 | tf_op jit(solution)/shard_map/all_to_all | solution.py:10
  1291.4 69.5 %copy.13 = f32[16,144,192,24]{1,0,3,2:T(8,128)} copy(f32[16,144,192,24]{2,1,3,0:T(8,128)} %bitcast.13) | data formatting | bytes 84934656 | tf_op jit(solution)/shard_map/all_to_all | solution.py:10
  1360.9 109.2 %reshape_reshape.3 = f32[48,48,4608]{1,0,2:T(8,128)} reshape(f32[16,144,192,24]{1,0,3,2:T(8,128)} %copy.13) | data formatting | bytes 84934656 | tf_op jit(solution)/shard_map/reshape;reshape | solution.py:14
  1470.1 109.1 %copy.14 = f32[48,48,4608]{0,1,2:T(8,128)} copy(f32[48,48,4608]{1,0,2:T(8,128)} %reshape_reshape.3) | data formatting | bytes 84934656 | tf_op jit(solution)/shard_map/reshape;reshape | solution.py:14
  1579.2 108.6 %bitcast_add_fusion = f32[48,48,4608]{1,0,2:T(8,128)} fusion(f32[48,48,4608]{1,0,2:T(8,128)} %reshape_reshape.3, f32[48,48,4608]{0,1,2:T(8,128)} %copy.14), kind=kLoop, calls=%fused_computation | loop fusion | flops 10616832 | bytes 127401984 | tf_op jit(solution)/shard_map/add | solution.py:15
  1687.8 76.0 %copy.15 = f32[48,48,4608]{2,1,0:T(8,128)} copy(f32[48,48,4608]{1,0,2:T(8,128)} %bitcast_add_fusion) | data formatting | bytes 84934656 | tf_op jit(solution)/shard_map/add | solution.py:15
  1763.8 209.4 %fusion = f32[2304,1536]{1,0:T(8,128)} fusion(f32[2304,4608]{1,0:T(8,128)} %bitcast.14, f32[4608,1536]{1,0:T(8,128)} %bitcast.15), kind=kOutput, calls=%fused_computation.1 | convolution fusion | flops 195689447424 | bytes 84934656 | tf_op jit(solution)/shard_map/dot_general | solution.py:18
  1973.2 0.0 reduce-scatter.3.cloned.1.call-update
  1973.3 0.0 reduce-scatter.5.cloned.1.call-start
  1973.3 225.3 %reduce-scatter.3.cloned.1.call-done = f32[144,1536]{1,0:T(8,128)} async-done(((f32[2304,1536]{1,0:T(8,128)}), f32[144,1536]{1,0:T(8,128)}) %reduce-scatter.3.cloned.1.call-update) | async-done | bytes 884752 | tf_op jit(solution)/shard_map/reduce_scatter | solution.py:17
  2198.6 0.0 reduce-scatter.5.cloned.1.call-update
  2198.6 10.3 reduce-scatter.5.cloned.1.call-done
Async XLA Ops:
  6.5 2192.1 %reduce-scatter.3.cloned.1.call-start = ((), (), s32[]{:S(2)}) async-start(), calls=%async_computation.3 | async-start | bytes 15040512 | tf_op jit(solution)/shard_map/reduce_scatter | solution.py:17
  1973.3 235.7 %reduce-scatter.5.cloned.1.call-start = ((), (), s32[]{:S(2)}) async-start(), calls=%async_computation.4 | async-start | bytes 1327104 | tf_op jit(solution)/shard_map/reduce_scatter | solution.py:25
Sparse Core Ops, SparseCore 0:
  1973.4 225.1 reduce-scatter.2
  2201.0 7.9 reduce-scatter.4
where the time goes:
time: 2220 us
  blocking collectives  1230 us (55%)
  local copies, waits for them, and re-layouts  420 us (19%)
  waiting for transfers between devices  236 us (11%)
  matrix products  209 us (9%)
  other arithmetic  109 us (5%)
    all_to_all x1, blocking collectives, on_device(): lax.all_to_all(amplitudes, 'occ', split_axis=2, concat_axis=0, tiled=True)  1230 us
    reduce_scatter x1, waiting for transfers between devices, on_device(): lax.psum_scatter(jnp.dot(summed, slab_matrix, precision=lax.Precision.HIG...  225 us
    another operation x2, local copies, waits for them, and re-layouts, on_device(): grouped = flattened.reshape(O, O, col_count)  218 us
    dot_general x1, matrix products, on_device(): jnp.dot(summed, slab_matrix, precision=lax.Precision.HIGHEST, preferred_e...  209 us
    add x1, other arithmetic, on_device(): grouped + jnp.transpose(grouped, (1, 0, 2))  109 us
    add x1, local copies, waits for them, and re-layouts, on_device(): grouped + jnp.transpose(grouped, (1, 0, 2))  76 us
    all_to_all x1, local copies, waits for them, and re-layouts, on_device(): lax.all_to_all(amplitudes, 'occ', split_axis=2, concat_axis=0, tiled=True)  69.5 us
    unnamed x1, local copies, waits for them, and re-layouts  55.8 us
  transfers between devices with their start and end apart: 2, of which 2 were waited for; matrix products, arithmetic and copies ran while one was open for 0% of the time, Pallas kernels for 0%

commit v1 on v0

v1 whole, which is shorter than its diff:
```python
import numpy as np
import jax
import jax.numpy as jnp
from jax import lax
from jax.experimental import pallas as pl
from jax.experimental.pallas import tpu as pltpu
from jax.sharding import PartitionSpec as P

O = 48
PLANES = 4
SPOTS = 4
OWNERS = PLANES * SPOTS
SHARE = O // OWNERS
CG = 16
SUB = 8
CHUNK = 2 * CG
VMEM = 56 * 1024 * 1024

CLASSES = ((0, 0), (1, 1), (0, 1), (0, 2), (1, 2), (2, 2))
BATCH_ENDS = ((0, 1), (0, 2), (1, 2), (2, 2))


def pack_kernel(where_ref, *refs):
    z, q = where_ref[0], where_ref[1]
    a_refs, x_refs, turned = refs[:3], refs[-SPOTS - 1 : -1], refs[-1]
    rows, cs, _ = a_refs[0].shape
    lanes = 128 * len(a_refs)
    width = lanes // OWNERS
    flat = [a_ref.reshape(rows * cs, 128) for a_ref in a_refs]
    lane = lax.broadcasted_iota(jnp.int32, (SUB, lanes), 1)
    block = (lane * (65536 // width + 1)) >> 16
    low = lax.broadcasted_iota(jnp.int32, (SUB, lanes), 0) < 4

    def step(half, carry):
        for cg in range(2):
            first = half * SUB * cs + cg * CG
            t = [
                jnp.concatenate([ref[pl.ds(first + c, SUB, stride=cs), :] for ref in flat], axis=1)
                for c in range(CG)
            ]
            for bit in (8, 4, 2, 1):
                keep = (block & bit) == 0
                for c in range(CG):
                    if c & bit == 0:
                        a, b = t[c], t[c + bit]
                        t[c] = jnp.where(keep, a, pltpu.roll(b, bit * width, 1))
                        t[c + bit] = jnp.where(keep, pltpu.roll(a, lanes - bit * width, 1), b)
            for o in range(OWNERS):
                turned[cg, o] = t[o]
        for m, x_ref in enumerate(x_refs):
            for dr in range(PLANES):
                o = (z ^ dr) * SPOTS + (q ^ m)
                t0, t1 = turned[0, o], turned[1, o]
                x_ref[dr, z ^ (2 * half)] = jnp.where(low, t0, pltpu.roll(t1, 4, 0))
                x_ref[dr, z ^ (2 * half + 1)] = jnp.where(low, pltpu.roll(t0, 4, 0), t1)
        return carry

    lax.fori_loop(0, 2, step, 0)


def pack(where, amplitudes, pair, span, after):
    r, s = pair
    both = 1 if r == s else 2
    rows, cs, lanes = amplitudes.shape
    begin, deep = span[0], span[1] - span[0]
    view = amplitudes.reshape(SHARE, OWNERS, SHARE, cs, lanes)
    shape = (PLANES, PLANES, both, deep, SUB, lanes)
    block = pl.BlockSpec(
        (PLANES, PLANES, None, None, SUB, lanes), lambda u, k, w: (0, 0, u, k, 0, 0)
    )
    in_specs = [
        pl.BlockSpec(
            (None, OWNERS, None, CHUNK, 128),
            lambda u, k, w, at=at: (r + u * (s - r), 0, s + u * (r - s), begin + k, at),
        )
        for at in range(lanes // 128)
    ]
    operands = [view] * len(in_specs) + after
    in_specs += [pl.BlockSpec(memory_space=pl.ANY)] * len(after)
    return pl.pallas_call(
        pack_kernel,
        out_shape=[jax.ShapeDtypeStruct(shape, jnp.float32)] * SPOTS,
        grid_spec=pltpu.PrefetchScalarGridSpec(
            num_scalar_prefetch=1,
            grid=(both, deep),
            in_specs=in_specs,
            out_specs=[block] * SPOTS,
            scratch_shapes=[pltpu.VMEM((2, OWNERS, SUB, lanes), jnp.float32)],
        ),
        compiler_params=pltpu.CompilerParams(vmem_limit_bytes=VMEM),
        cost_estimate=pl.CostEstimate(
            flops=0, transcendentals=0, bytes_accessed=0
        ),
        name="pack",
    )(where, *operands)


def hold(arrays, after):
    def kernel(*refs):
        pass

    return pl.pallas_call(
        kernel,
        out_shape=[jax.ShapeDtypeStruct(x.shape, x.dtype) for x in arrays],
        in_specs=[pl.BlockSpec(memory_space=pl.ANY)] * (len(arrays) + len(after)),
        out_specs=[pl.BlockSpec(memory_space=pl.ANY)] * len(arrays),
        input_output_aliases={n: n for n in range(len(arrays))},
        cost_estimate=pl.CostEstimate(flops=0, transcendentals=0, bytes_accessed=0),
        name="hold",
    )(*arrays, *after)


def turn(tiles, odd1, odd2):
    tiles = list(tiles)
    for bit, odd in ((1, odd1), (2, odd2)):
        for n in range(SPOTS):
            if n & bit == 0:
                a, b = tiles[n], tiles[n + bit]
                tiles[n] = jnp.where(odd, pltpu.roll(b, bit, a.ndim - 2), a)
                tiles[n + bit] = jnp.where(odd, b, pltpu.roll(a, SUB - bit, a.ndim - 2))
    return tiles


class Sizes:
    def __init__(self, both, deep):
        self.both, self.deep = both, deep
        self.own = SPOTS * deep
        self.cross = SPOTS * both * deep
        self.full = self.own + 3 * self.cross
        self.part = self.own + 2 * self.cross
        self.near = 2 * self.full
        self.far = 2 * self.part + self.cross
        self.own_rows = SPOTS * SPOTS
        self.cross_rows = SPOTS * SPOTS * both
        self.rows = PLANES * self.own_rows + 6 * self.cross_rows

    def cross_row(self, a, b):
        at = a * PLANES - a * (a + 1) // 2 + b - a - 1
        return PLANES * self.own_rows + self.cross_rows * at


def orient_kernel(sizes, where_ref, *refs):
    z, q = where_ref[0], where_ref[1]
    y_refs = refs[:SPOTS]
    kept, near, far, held = refs[-4:]
    both, deep, lanes = sizes.both, sizes.deep, y_refs[0].shape[-1]
    own, cross = sizes.own, sizes.cross
    spot = lax.broadcasted_iota(jnp.int32, (deep, SUB, lanes), 1)
    odd1, odd2 = (spot & 1) != 0, (spot & 2) != 0
    full = [0, own, own + cross, own + 2 * cross]
    places = {
        0: (kept, full),
        1: (near, [sizes.full + n for n in full]),
        2: (far, [0, 2 * sizes.part, own, own + cross]),
        3: (near, [0, sizes.part, own, own + cross]),
    }
    for dr in range(PLANES):
        out, firsts = places[dr]
        for br in range(PLANES):
            first = firsts[br]
            for m, y_ref in enumerate(y_refs):
                held[q ^ m] = y_ref[dr, br]

            def turned(u):
                return turn([held[n, u] for n in range(SPOTS)], odd1, odd2)

            if br == 0:
                other = turned(both - 1)
                for n in range(SPOTS):
                    out[first + n * deep : first + (n + 1) * deep] = held[n, 0] + other[n]
            else:
                lower = (z & (1 if br == 1 else 2)) == 0

                @pl.when(lower)
                def _():
                    for n in range(SPOTS):
                        for u in range(both):
                            at = first + (n * both + u) * deep
                            out[at : at + deep] = held[n, u]

                @pl.when(jnp.logical_not(lower))
                def _():
                    for u in range(both):
                        tiles = turned(both - 1 - u)
                        for n in range(SPOTS):
                            at = first + (n * both + u) * deep
                            out[at : at + deep] = tiles[n]


def orient(where, ys, sizes, after):
    lanes = ys[0].shape[-1]
    counts = (sizes.full, sizes.near, sizes.far)

    def kernel(*refs):
        orient_kernel(sizes, *refs)

    return pl.pallas_call(
        kernel,
        out_shape=[jax.ShapeDtypeStruct((n, SUB, lanes), jnp.float32) for n in counts],
        grid_spec=pltpu.PrefetchScalarGridSpec(
            num_scalar_prefetch=1,
            grid=(lanes // 128,),
            in_specs=[pl.BlockSpec(ys[0].shape[:-1] + (128,), lambda l, w: (0, 0, 0, 0, 0, l))]
            * SPOTS
            + [pl.BlockSpec(memory_space=pl.ANY)] * len(after),
            out_specs=[pl.BlockSpec((n, SUB, 128), lambda l, w: (0, 0, l)) for n in counts],
            scratch_shapes=[pltpu.VMEM((SPOTS, sizes.both, sizes.deep, SUB, 128), jnp.float32)],
        ),
        compiler_params=pltpu.CompilerParams(vmem_limit_bytes=VMEM),
        cost_estimate=pl.CostEstimate(
            flops=0, transcendentals=0, bytes_accessed=0
        ),
        name="orient",
    )(where, *ys, *after)


def merge(far, arrived, sizes, after):
    own, lanes = sizes.own, far.shape[-1]
    relayed = sizes.part // own

    def kernel(far_ref, arrived_ref, *rest):
        out_ref, token_ref = rest[-2:]
        n = pl.program_id(0)

        @pl.when(n < relayed)
        def _():
            out_ref[...] = arrived_ref[...]

        @pl.when(n >= relayed)
        def _():
            out_ref[...] = arrived_ref[...] + far_ref[...]

        token_ref[...] = jnp.zeros_like(token_ref)

    return pl.pallas_call(
        kernel,
        out_shape=[
            jax.ShapeDtypeStruct(far.shape, jnp.float32),
            jax.ShapeDtypeStruct((SUB, 128), jnp.float32),
        ],
        grid=(sizes.full // own,),
        in_specs=[
            pl.BlockSpec((own, SUB, lanes), lambda n: (jnp.maximum(n, relayed) + relayed, 0, 0)),
            pl.BlockSpec((own, SUB, lanes), lambda n: (n, 0, 0)),
        ]
        + [pl.BlockSpec(memory_space=pl.ANY)] * len(after),
        out_specs=[
            pl.BlockSpec((own, SUB, lanes), lambda n: (n + relayed, 0, 0)),
            pl.BlockSpec((SUB, 128), lambda n: (0, 0)),
        ],
        input_output_aliases={0: 0},
        compiler_params=pltpu.CompilerParams(vmem_limit_bytes=VMEM),
        cost_estimate=pl.CostEstimate(
            flops=0, transcendentals=0, bytes_accessed=0
        ),
        name="merge",
    )(far, arrived, *after)


def place_of(z, sizes):
    def cross(m, n):
        a, b = z ^ m, z ^ n
        return sizes.cross_row(jnp.minimum(a, b), jnp.maximum(a, b))

    own = [(z ^ n) * sizes.own_rows for n in range(PLANES)]
    pairs = [cross(0, 1), cross(0, 2), cross(0, 3), cross(1, 3), cross(1, 2), cross(2, 3)]
    return jnp.stack(own + pairs + [lax.axis_index("vir")]).astype(jnp.int32)


def multiply_kernel(spans, place_ref, *refs):
    b_ref, mine, theirs, hi, lo = refs[3 * len(spans)], *refs[-4:]
    lanes = refs[0].shape[-1]

    def gather(sizes, begin, kept, near, far):
        deep, own, cross, part = sizes.deep, sizes.own, sizes.cross, sizes.part
        pieces = [
            (kept, 0, None, 0, 1),
            (near, 0, None, 0, 1),
            (far, 0, None, 0, 1),
            (far, part, None, 0, 1),
            (kept, own, near, own, sizes.both),
            (kept, own + cross, far, own, sizes.both),
            (kept, own + 2 * cross, far, part + own + cross, sizes.both),
            (near, own + cross, far, part + own, sizes.both),
            (near, own + 2 * cross, far, own + cross, sizes.both),
            (far, 2 * part, None, 0, sizes.both),
        ]
        low = lax.broadcasted_iota(jnp.int32, (SUB, lanes), 0) < 4

        def step(k, carry):
            for at, (one, first, two, second, groups) in enumerate(pieces):
                for n in range(groups):
                    t = []
                    for m in range(4 * n, 4 * n + 4):
                        tile = one[first + m * deep + k]
                        if two is not None:
                            tile = tile + two[second + m * deep + k]
                        t.append(tile)
                    row = pl.multiple_of(place_ref[at] + 16 * n, 16)
                    x0 = [jnp.where(low, t[m], pltpu.roll(t[m + 1], 4, 0)) for m in (0, 2)]
                    x1 = [jnp.where(low, pltpu.roll(t[m], 4, 0), t[m + 1]) for m in (0, 2)]
                    for cg, x in enumerate((x0, x1)):
                        x = jnp.concatenate(x, axis=0)
                        top = x.astype(jnp.bfloat16)
                        column = pl.multiple_of((2 * (begin + k) + cg) * lanes, 128)
                        hi[pl.ds(row, 16), pl.ds(column, lanes)] = top
                        lo[pl.ds(row, 16), pl.ds(column, lanes)] = (
                            x - top.astype(jnp.float32)
                        ).astype(jnp.bfloat16)
            return carry

        lax.fori_loop(0, deep, step, 0)

    @pl.when(pl.program_id(0) == 0)
    def _():
        for at, (sizes, begin) in enumerate(spans):
            gather(sizes, begin, *refs[3 * at : 3 * at + 3])

    b = b_ref[...].reshape(b_ref.shape[0] * b_ref.shape[1], b_ref.shape[2])
    b_hi = b.astype(jnp.bfloat16)
    b_lo = (b - b_hi.astype(jnp.float32)).astype(jnp.bfloat16)
    dot = lambda x, y: jnp.dot(x, y, preferred_element_type=jnp.float32)
    c = dot(lo[...], b_hi) + dot(hi[...], b_lo) + dot(hi[...], b_hi)
    half = pl.num_programs(0) // 2

    @pl.when(pl.program_id(0) < half)
    def _():
        theirs[...] = c

    @pl.when(pl.program_id(0) >= half)
    def _():
        mine[...] = c


def multiply(place, parts, integrals, after):
    cs, ds, columns = integrals.shape
    rows = parts[0][0].rows
    wide = 256
    half = columns // wide // 2
    arrays = [x for _, _, three in parts for x in three]
    lanes = arrays[0].shape[-1]
    in_specs = []
    for sizes, _, _ in parts:
        in_specs += [
            pl.BlockSpec((sizes.full, SUB, lanes), lambda n, w: (0, 0, 0)),
            pl.BlockSpec((sizes.full, SUB, lanes), lambda n, w: (1, 0, 0)),
            pl.BlockSpec((sizes.far, SUB, lanes), lambda n, w: (0, 0, 0)),
        ]

    def kernel(*refs):
        multiply_kernel([(sizes, begin) for sizes, begin, _ in parts], *refs)

    def column(n, w):
        return lax.rem(n + (1 - w[PLANES + 6]) * half, 2 * half)

    return pl.pallas_call(
        kernel,
        out_shape=[jax.ShapeDtypeStruct((rows, columns // 2), jnp.float32)] * 2,
        grid_spec=pltpu.PrefetchScalarGridSpec(
            num_scalar_prefetch=1,
            grid=(2 * half,),
            in_specs=in_specs
            + [pl.BlockSpec((cs, ds, wide), lambda n, w: (0, 0, column(n, w)))]
            + [pl.BlockSpec(memory_space=pl.ANY)] * len(after),
            out_specs=[
                pl.BlockSpec((rows, wide), lambda n, w: (0, jnp.maximum(n - half, 0))),
                pl.BlockSpec((rows, wide), lambda n, w: (0, jnp.minimum(n, half - 1))),
            ],
            scratch_shapes=[pltpu.VMEM((rows, cs * ds), jnp.bfloat16)] * 2,
        ),
        compiler_params=pltpu.CompilerParams(vmem_limit_bytes=VMEM),
        cost_estimate=pl.CostEstimate(
            flops=0,
            transcendentals=0,
            bytes_accessed=0
        ),
        name="multiply",
    )(place, *arrays, integrals, *after)


def row_table(sizes):
    table = []
    for owner in range(OWNERS):
        for u in range(sizes.both):
            for partner in range(OWNERS):
                (za, qa), (zb, qb) = divmod(owner, SPOTS), divmod(partner, SPOTS)
                if (za, u) > (zb, 0) if za == zb else za > zb:
                    za, qa, zb, qb, v = zb, qb, za, qa, sizes.both - 1 - u
                else:
                    v = u
                if za == zb:
                    table.append(za * sizes.own_rows + qa * SPOTS + qb)
                else:
                    table.append(sizes.cross_row(za, zb) + (qa * sizes.both + v) * SPOTS + qb)
    return np.array(table, np.int32)


def spread(where, batch, after):
    classes = [sizes for sizes, _, _ in batch]
    table = np.concatenate([row_table(sizes) for sizes in classes])
    columns = batch[0][1].shape[1]
    rows = OWNERS * sum(sizes.both for sizes in classes)

    def kernel(where_ref, table_ref, *refs):
        z, q = where_ref[0], where_ref[1]
        outs = refs[-SPOTS:]
        begin = put = 0
        for at, sizes in enumerate(classes):
            one, two = refs[2 * at], refs[2 * at + 1]
            count = OWNERS * sizes.both
            for m, out in enumerate(outs):

                def step(n, carry):
                    dr, k = n // (count // 8), n % (count // 8)
                    first = begin + ((z ^ dr) * SPOTS + (q ^ m)) * count + k * 8
                    found = [pl.ds(table_ref[first + j], 1) for j in range(8)]
                    out[dr, pl.ds(pl.multiple_of(put + k * 8, 8), 8), :] = jnp.concatenate(
                        [one[row, :] + two[row, :] for row in found], axis=0
                    )
                    return carry

                lax.fori_loop(0, PLANES * count // 8, step, 0)
            begin += OWNERS * count
            put += count

    halves = [x for _, one, two in batch for x in (one, two)]
    return pl.pallas_call(
        kernel,
        out_shape=[jax.ShapeDtypeStruct((PLANES, rows, columns), jnp.float32)] * SPOTS,
        grid_spec=pltpu.PrefetchScalarGridSpec(
            num_scalar_prefetch=2,
            grid=(1,),
            in_specs=[pl.BlockSpec(x.shape, lambda n, w, t: (0, 0)) for x in halves]
            + [pl.BlockSpec(memory_space=pl.ANY)] * len(after),
            out_specs=[pl.BlockSpec((PLANES, rows, columns), lambda n, w, t: (0, 0, 0))] * SPOTS,
        ),
        compiler_params=pltpu.CompilerParams(vmem_limit_bytes=VMEM),
        cost_estimate=pl.CostEstimate(
            flops=0,
            transcendentals=0,
            bytes_accessed=0
        ),
        name="spread",
    )(where, jnp.asarray(table), *halves, *after)


def collect(batches):
    columns = batches[0][1][0].shape[1]
    arrays = [x for _, parts in batches for x in parts]

    def kernel(*refs):
        out = refs[-1]
        for at, (pairs, _) in enumerate(batches):
            a, b, c, d = refs[PLANES * at : PLANES * (at + 1)]
            for n, (r, s) in enumerate(pairs):
                rows = pl.ds(n * OWNERS, OWNERS)
                total = (a[rows, :] + b[rows, :]) + (c[rows, :] + d[rows, :])
                out[pl.ds(r * O + s, OWNERS, stride=SHARE), :] = total

    return pl.pallas_call(
        kernel,
        out_shape=jax.ShapeDtypeStruct((SHARE * O, columns), jnp.float32),
        grid=(columns // 128,),
        in_specs=[pl.BlockSpec((x.shape[0], 128), lambda n: (0, n)) for x in arrays],
        out_specs=pl.BlockSpec((SHARE * O, 128), lambda n: (0, n)),
        name="collect",
    )(*arrays)


def exchange(x, bits):
    return lax.ppermute(x, "occ", [(n, n ^ bits) for n in range(OWNERS)])


def in_planes(amplitudes, integrals):
    here = lax.axis_index("occ")
    z, q = here // SPOTS, here % SPOTS
    where = jnp.stack([z, q]).astype(jnp.int32)
    deep = amplitudes.shape[1] // CHUNK
    chunks = []
    for pair in CLASSES:
        chunks += [(pair, (0, deep // 2), False), (pair, (deep // 2, deep), True)]
    kepts, nears, tokens, fars, products = [], [], [], [], []
    parts, batch, batches, ready = [], [], [], []

    def last(arrays, back=1):
        return arrays[-back:][:1] if len(arrays) >= back else []

    def packed(at):
        pair, span, _ = chunks[at]
        return pack(where, amplitudes, pair, span, last(kepts))

    def first_half(at):
        own, *others = coming
        if kepts:
            others = hold(others, last(tokens, 1) + last(kepts))
        ys = [own] + [exchange(x, m) for m, x in enumerate(others, 1)]
        upcoming = packed(at + 1) if at + 1 < len(chunks) else []
        kept, near, far = orient(where, ys, sizes_of(at), list(upcoming[:1]))
        kepts.append(kept)
        nears.append((exchange(near, SPOTS), far))
        return upcoming

    def sizes_of(at):
        (r, s), span, _ = chunks[at]
        return Sizes(1 if r == s else 2, span[1] - span[0])

    def second_half(at, after):
        nonlocal parts, batch, ready
        (r, s), span, ends = chunks[at]
        parts.append((sizes_of(at), span[0], (kepts[at], nears[at][0], fars[at])))
        if not ends:
            return
        mine, theirs = multiply(place_of(z, sizes_of(at)), parts, integrals, ready + after)
        products.append(mine)
        theirs = lax.ppermute(theirs, "vir", [(0, 1), (1, 0)])
        batch.append((sizes_of(at), mine, theirs, [(r, s)] if r == s else [(r, s), (s, r)]))
        parts = []
        if (r, s) not in BATCH_ENDS:
            return
        before = nears[-1][:1] if batches else kepts[-1:]
        rows = spread(where, [x[:3] for x in batch], list(before))
        rows = [rows[0]] + [exchange(rows[m], m) for m in range(1, SPOTS)]
        plane = [rows[0][dr] + rows[1][dr] + rows[2][dr] + rows[3][dr] for dr in range(PLANES)]
        ready = plane[:1]
        batches.append(([pair for x in batch for pair in x[3]], plane))
        batch = []

    def over_planes(plane):
        return plane[:1] + [exchange(plane[dr], dr * SPOTS) for dr in range(1, PLANES)]

    coming = packed(0)
    coming = first_half(0)
    count = len(chunks)
    for at in range(count):
        if at + 1 < count:
            coming = first_half(at + 1)
        if at >= 2:
            second_half(at - 2, kepts[-1:] + (tokens[-1:] if at + 1 == count else []))
        before = last(fars, 2 if at + 2 == count else 1)
        if at >= 4:
            before = before + last(kepts) + last(products)
        near, far = nears[at]
        far, token = merge(far, near, sizes_of(at), before)
        tokens.append(token)
        fars.append(exchange(far, 2 * SPOTS))
    second_half(count - 2, [])
    early = [pair for pairs, _ in batches for pair in pairs]
    plane = [jnp.concatenate([x[dr] for _, x in batches]) for dr in range(PLANES)]
    second_half(count - 1, plane)
    return collect([(pairs, over_planes(x)) for pairs, x in [(early, plane), batches[-1]]])


def regrouped(amplitudes, integrals):
    moved = lax.all_to_all(amplitudes, "occ", split_axis=2, concat_axis=0, tiled=True)
    pair_count = moved.shape[0]
    col_count = moved.shape[1] * moved.shape[2]
    grouped = moved.reshape(O, O, col_count)
    summed = (grouped + jnp.transpose(grouped, (1, 0, 2))).reshape(pair_count, col_count)
    product = jnp.dot(
        summed,
        integrals.reshape(col_count, integrals.shape[2]),
        precision=lax.Precision.HIGHEST,
        preferred_element_type=jnp.float32,
    )
    half = lax.psum_scatter(product, "vir", scatter_dimension=1, tiled=True)
    return lax.psum_scatter(half, "occ", scatter_dimension=0, tiled=True)


def solution(mesh):
    def on_device(amplitudes, integrals):
        rows, cs, ds = amplitudes.shape
        fits = (
            mesh.shape["occ"] == OWNERS
            and mesh.shape["vir"] == 2
            and rows * OWNERS == O * O
            and cs % (2 * CHUNK) == 0
            and ds == 128 * 3
            and O == OWNERS * SHARE
            and integrals.shape[2] % 512 == 0
        )
        return in_planes(amplitudes, integrals) if fits else regrouped(amplitudes, integrals)

    in_specs = (P("occ", "vir", None), P("vir", "occ", None))
    out_specs = P("occ", "vir")
    return jax.shard_map(
        on_device, mesh=mesh, in_specs=in_specs, out_specs=out_specs, check_vma=False
    )
```

time: 2220 us -> 989 us (0.45)
  blocking collectives: 1230 us -> 0 us
  local copies, waits for them, and re-layouts: 420 us -> 30.1 us
  Pallas kernels: 0 us -> 383 us
  waiting for transfers between devices: 236 us -> 452 us
  matrix products: 209 us -> 0 us
  starting transfers between devices: 0.04 us -> 113 us
  other arithmetic: 109 us -> 6.92 us
    all_to_all x1 -> x0, blocking collectives: 1230 us -> none  [on_device(): lax.all_to_all(amplitudes, 'occ', split_axis=2, concat_axis=0, tiled=True)]
    ppermute x0 -> x84, waiting for transfers between devices: none -> 452 us  [the longest x78 448 us: exchange(): return lax.ppermute(x, 'occ', [(n, n ^ bits) for n in range(OWNERS)])]
    pallas_call x0 -> x58, Pallas kernels: none -> 383 us  [the longest x12 123 us: pack(): pl.pallas_call(pack_kernel, out_shape=[jax.ShapeDtypeStruct(shape, jnp.fl...]
    reduce_scatter x2 -> x0, waiting for transfers between devices: 236 us -> none  [the longest x1 225 us: on_device(): lax.psum_scatter(jnp.dot(summed, slab_matrix, precision=lax.Precision.HIG...]
    another operation x2, local copies, waits for them, and re-layouts: 218 us -> 1.3 us  [place_of(): return jnp.stack(own + pairs + [lax.axis_index('vir')]).astype(jnp.int32)]
    dot_general x1 -> x0, matrix products: 209 us -> none  [on_device(): jnp.dot(summed, slab_matrix, precision=lax.Precision.HIGHEST, preferred_e...]
    ppermute x0 -> x84, starting transfers between devices: none -> 113 us  [the longest x78 113 us: exchange(): return lax.ppermute(x, 'occ', [(n, n ^ bits) for n in range(OWNERS)])]
    add x1 -> x4, other arithmetic: 109 us -> 3.19 us  [second_half(): rows[0][dr] + rows[1][dr] + rows[2][dr] + rows[3][dr]]
  transfers between devices with their start and end apart: 2 -> 84, of which waited for: 2 -> 42; matrix products, arithmetic and copies ran while one was open for 0% -> 1% of each run, Pallas kernels for 0% -> 35%
where the time goes in v1:
time: 989 us; the launch traced here: 985 us
  waiting for transfers between devices  452 us (46%)
  Pallas kernels  383 us (39%)
  starting transfers between devices  113 us (11%)
  local copies, waits for them, and re-layouts  30.1 us (3%)
    ppermute x78, waiting for transfers between devices, exchange(): return lax.ppermute(x, 'occ', [(n, n ^ bits) for n in range(OWNERS)])  448 us
    pallas_call x12, Pallas kernels, pack(): pl.pallas_call(pack_kernel, out_shape=[jax.ShapeDtypeStruct(shape, jnp.fl...  123 us
    ppermute x78, starting transfers between devices, exchange(): return lax.ppermute(x, 'occ', [(n, n ^ bits) for n in range(OWNERS)])  113 us
    pallas_call x6, Pallas kernels, multiply(): pl.pallas_call(kernel, out_shape=[jax.ShapeDtypeStruct((rows, columns //...  111 us
    pallas_call x12, Pallas kernels, orient(): pl.pallas_call(kernel, out_shape=[jax.ShapeDtypeStruct((n, SUB, lanes), j...  70.4 us
    pallas_call x12, Pallas kernels, merge(): pl.pallas_call(kernel, out_shape=[jax.ShapeDtypeStruct(far.shape, jnp.flo...  49.1 us
    unnamed x142, local copies, waits for them, and re-layouts  28.8 us
    pallas_call x4, Pallas kernels, spread(): pl.pallas_call(kernel, out_shape=[jax.ShapeDtypeStruct((PLANES, rows, col...  25.2 us
  transfers between devices with their start and end apart: 84, of which 42 were waited for; matrix products, arithmetic and copies ran while one was open for 1% of the time, Pallas kernels for 35%

profile of v1, /device:TPU:0, one launch (start us, length us, event | category | flops | bytes accessed | tf_op | source)
XLA Modules:
  0.0 985.3 jit_solution(17136556435049481425)
XLA Ops:
  0.6 7.7 pack.12
  12.7 7.7 pack.13
  25.6 13.3 %collective-permute-done.1.refs_3_ = f32[4,4,1,3,8,384]{5,4,3,2,1,0:T(8,128)S(1)} collective-permute-done((f32[4,4,1,3,8,384]{5,4,3,2,1,0:T(8,128)}, f32[4,4,1,3,8,384]{5,4,3,2,1,0:T(8,128)S(1)}, u32[]{:S(2)}, u32[]{:S(2)}) %collective-permute-start.1) | collective-permute-done | bytes 589856 | tf_op jit(solution)/shard_map/ppermute | solution.py:471
  50.2 7.7 pack.14
  63.1 11.0 %collective-permute-done.6.refs_3_ = f32[4,4,1,3,8,384]{5,4,3,2,1,0:T(8,128)S(1)} collective-permute-done((f32[4,4,1,3,8,384]{5,4,3,2,1,0:T(8,128)}, f32[4,4,1,3,8,384]{5,4,3,2,1,0:T(8,128)S(1)}, u32[]{:S(2)}, u32[]{:S(2)}) %collective-permute-start.6) | collective-permute-done | bytes 589856 | tf_op jit(solution)/shard_map/ppermute | solution.py:471
  91.4 7.7 pack.15
  104.4 8.3 collective-permute-done.11.refs_3_
  120.6 22.1 %collective-permute-done.8.arrived_ref.refs_5_ = f32[96,8,384]{2,1,0:T(8,128)S(1)} collective-permute-done((f32[96,8,384]{2,1,0:T(8,128)}, f32[96,8,384]{2,1,0:T(8,128)S(1)}, u32[]{:S(2)}, u32[]{:S(2)}) %collective-permute-start.8) | collective-permute-done | bytes 1179680 | tf_op jit(solution)/shard_map/ppermute | solution.py:471
  151.3 12.8 %pack.16 = (f32[4,4,2,3,8,384]{5,4,3,2,1,0:T(8,128)}, f32[4,4,2,3,8,384]{5,4,3,2,1,0:T(8,128)}, f32[4,4,2,3,8,384]{5,4,3,2,1,0:T(8,128)}, f32[4,4,2,3,8,384]{5,4,3,2,1,0:T(8,128)}) custom-call(s32[2]{0:T(128)} %pad_add_fusion.where_ref.refs_0_, f32[3,16,3,192,384]{4,3,2,1,0:T(8,128)} %bitcast.64, f32[3,16,3,192,384]{4,3,2,1,0:T(8,128)} %bitcast.65, ...), custom_call_target="tpu_custom_call" | custom-call | tf_op jit(solution)/shard_map/pack/pallas_call | solution.py:80
  170.9 12.2 %collective-permute-done.9.rest_0_.refs_6_ = f32[84,8,384]{2,1,0:T(8,128)S(1)} collective-permute-done((f32[84,8,384]{2,1,0:T(8,128)}, f32[84,8,384]{2,1,0:T(8,128)S(1)}, u32[]{:S(2)}, u32[]{:S(2)}) %collective-permute-start.9) | collective-permute-done | bytes 1032224 | tf_op jit(solution)/shard_map/ppermute | solution.py:471
  193.5 12.8 %pack.17 = (f32[4,4,2,3,8,384]{5,4,3,2,1,0:T(8,128)}, f32[4,4,2,3,8,384]{5,4,3,2,1,0:T(8,128)}, f32[4,4,2,3,8,384]{5,4,3,2,1,0:T(8,128)}, f32[4,4,2,3,8,384]{5,4,3,2,1,0:T(8,128)}) custom-call(s32[2]{0:T(128)} %pad_add_fusion.where_ref.refs_0_, f32[3,16,3,192,384]{4,3,2,1,0:T(8,128)} %bitcast.69, f32[3,16,3,192,384]{4,3,2,1,0:T(8,128)} %bitcast.68, ...), custom_call_target="tpu_custom_call" | custom-call | tf_op jit(solution)/shard_map/pack/pallas_call | solution.py:80
  212.7 17.4 %collective-permute-done.18.refs_3_ = f32[4,4,2,3,8,384]{5,4,3,2,1,0:T(8,128)S(1)} collective-permute-done((f32[4,4,2,3,8,384]{5,4,3,2,1,0:T(8,128)}, f32[4,4,2,3,8,384]{5,4,3,2,1,0:T(8,128)S(1)}, u32[]{:S(2)}, u32[]{:S(2)}) %collective-permute-start.18) | collective-permute-done | bytes 1179680 | tf_op jit(solution)/shard_map/ppermute | solution.py:471
  248.8 12.8 %pack.18 = (f32[4,4,2,3,8,384]{5,4,3,2,1,0:T(8,128)}, f32[4,4,2,3,8,384]{5,4,3,2,1,0:T(8,128)}, f32[4,4,2,3,8,384]{5,4,3,2,1,0:T(8,128)}, f32[4,4,2,3,8,384]{5,4,3,2,1,0:T(8,128)}) custom-call(s32[2]{0:T(128)} %pad_add_fusion.where_ref.refs_0_, f32[3,16,3,192,384]{4,3,2,1,0:T(8,128)} %bitcast.70, f32[3,16,3,192,384]{4,3,2,1,0:T(8,128)} %bitcast.71, ...), custom_call_target="tpu_custom_call" | custom-call | tf_op jit(solution)/shard_map/pack/pallas_call | solution.py:80
  261.5 12.9 %collective-permute-done.25.refs_2_ = f32[4,4,2,3,8,384]{5,4,3,2,1,0:T(8,128)S(1)} collective-permute-done((f32[4,4,2,3,8,384]{5,4,3,2,1,0:T(8,128)}, f32[4,4,2,3,8,384]{5,4,3,2,1,0:T(8,128)S(1)}, u32[]{:S(2)}, u32[]{:S(2)}) %collective-permute-start.25) | collective-permute-done | bytes 1179680 | tf_op jit(solution)/shard_map/ppermute | solution.py:471
  274.4 16.4 %collective-permute-done.26.refs_3_ = f32[4,4,2,3,8,384]{5,4,3,2,1,0:T(8,128)S(1)} collective-permute-done((f32[4,4,2,3,8,384]{5,4,3,2,1,0:T(8,128)}, f32[4,4,2,3,8,384]{5,4,3,2,1,0:T(8,128)S(1)}, u32[]{:S(2)}, u32[]{:S(2)}) %collective-permute-start.26) | collective-permute-done | bytes 1179680 | tf_op jit(solution)/shard_map/ppermute | solution.py:471
  299.7 16.7 %multiply.6 = (f32[160,768]{1,0:T(8,128)}, f32[160,768]{1,0:T(8,128)}) custom-call(s32[11]{0:T(128)} %stack.58.refs_0_, f32[48,8,384]{2,1,0:T(8,128)} %get-tuple-element.178.refs_3_.refs_1_, f32[96,8,384]{2,1,0:T(8,128)} %copy-done.10, f32[84,8,384]{2,1,0:T(8,128)} %collective-permute-done.4.rest_0_.refs_3_, ...), custom_call_target="tpu_custom_call" | custom-call | tf_op jit(solution)/shard_map/multiply/pallas_call | solution.py:356
  327.1 12.8 %pack.19 = (f32[4,4,2,3,8,384]{5,4,3,2,1,0:T(8,128)}, f32[4,4,2,3,8,384]{5,4,3,2,1,0:T(8,128)}, f32[4,4,2,3,8,384]{5,4,3,2,1,0:T(8,128)}, f32[4,4,2,3,8,384]{5,4,3,2,1,0:T(8,128)}) custom-call(s32[2]{0:T(128)} %pad_add_fusion.where_ref.refs_0_, f32[3,16,3,192,384]{4,3,2,1,0:T(8,128)} %bitcast.73, f32[3,16,3,192,384]{4,3,2,1,0:T(8,128)} %bitcast.74, ...), custom_call_target="tpu_custom_call" | custom-call | tf_op jit(solution)/shard_map/pack/pallas_call | solution.py:80
  339.9 12.0 %collective-permute-done.28.refs_2_ = f32[4,4,2,3,8,384]{5,4,3,2,1,0:T(8,128)S(1)} collective-permute-done((f32[4,4,2,3,8,384]{5,4,3,2,1,0:T(8,128)}, f32[4,4,2,3,8,384]{5,4,3,2,1,0:T(8,128)S(1)}, u32[]{:S(2)}, u32[]{:S(2)}) %collective-permute-start.28) | collective-permute-done | bytes 1179680 | tf_op jit(solution)/shard_map/ppermute | solution.py:471
  351.9 14.5 %collective-permute-done.29.refs_3_ = f32[4,4,2,3,8,384]{5,4,3,2,1,0:T(8,128)S(1)} collective-permute-done((f32[4,4,2,3,8,384]{5,4,3,2,1,0:T(8,128)}, f32[4,4,2,3,8,384]{5,4,3,2,1,0:T(8,128)S(1)}, u32[]{:S(2)}, u32[]{:S(2)}) %collective-permute-start.29) | collective-permute-done | bytes 1179680 | tf_op jit(solution)/shard_map/ppermute | solution.py:471
  375.4 16.5 %multiply.7 = (f32[160,768]{1,0:T(8,128)}, f32[160,768]{1,0:T(8,128)}) custom-call(s32[11]{0:T(128)} %stack.58.refs_0_, f32[48,8,384]{2,1,0:T(8,128)} %get-tuple-element.201.refs_3_.refs_4_.refs_1_, f32[96,8,384]{2,1,0:T(8,128)} %copy-done.7, f32[84,8,384]{2,1,0:T(8,128)} %copy-done.12, f32[48,8,384]{2,1,0:T(8,128)} %get-tuple-element.216.refs_4_.refs_3_, ...), custom_call_target="tpu_custom_call" | custom-call | tf_op jit(solution)/shard_map/multiply/pallas_call | solution.py:356
  404.5 12.8 %pack.20 = (f32[4,4,2,3,8,384]{5,4,3,2,1,0:T(8,128)}, f32[4,4,2,3,8,384]{5,4,3,2,1,0:T(8,128)}, f32[4,4,2,3,8,384]{5,4,3,2,1,0:T(8,128)}, f32[4,4,2,3,8,384]{5,4,3,2,1,0:T(8,128)}) custom-call(s32[2]{0:T(128)} %pad_add_fusion.where_ref.refs_0_, f32[3,16,3,192,384]{4,3,2,1,0:T(8,128)} %bitcast.76, f32[3,16,3,192,384]{4,3,2,1,0:T(8,128)} %bitcast.77, ...), custom_call_target="tpu_custom_call" | custom-call | tf_op jit(solution)/shard_map/pack/pallas_call | solution.py:80
  417.3 10.9 %collective-permute-done.36.refs_2_ = f32[4,4,2,3,8,384]{5,4,3,2,1,0:T(8,128)S(1)} collective-permute-done((f32[4,4,2,3,8,384]{5,4,3,2,1,0:T(8,128)}, f32[4,4,2,3,8,384]{5,4,3,2,1,0:T(8,128)S(1)}, u32[]{:S(2)}, u32[]{:S(2)}) %collective-permute-start.36) | collective-permute-done | bytes 1179680 | tf_op jit(solution)/shard_map/ppermute | solution.py:471
  428.2 14.1 %collective-permute-done.37.refs_3_ = f32[4,4,2,3,8,384]{5,4,3,2,1,0:T(8,128)S(1)} collective-permute-done((f32[4,4,2,3,8,384]{5,4,3,2,1,0:T(8,128)}, f32[4,4,2,3,8,384]{5,4,3,2,1,0:T(8,128)S(1)}, u32[]{:S(2)}, u32[]{:S(2)}) %collective-permute-start.37) | collective-permute-done | bytes 1179680 | tf_op jit(solution)/shard_map/ppermute | solution.py:471
  451.2 35.2 %collective-permute-done.35.arrived_ref.refs_2_ = f32[168,8,384]{2,1,0:T(8,128)S(1)} collective-permute-done((f32[168,8,384]{2,1,0:T(8,128)}, f32[168,8,384]{2,1,0:T(8,128)S(1)}, u32[]{:S(2)}, u32[]{:S(2)}) %collective-permute-start.35) | collective-permute-done | bytes 2064416 | tf_op jit(solution)/shard_map/ppermute | solution.py:471
  500.4 12.7 %pack.21 = (f32[4,4,2,3,8,384]{5,4,3,2,1,0:T(8,128)}, f32[4,4,2,3,8,384]{5,4,3,2,1,0:T(8,128)}, f32[4,4,2,3,8,384]{5,4,3,2,1,0:T(8,128)}, f32[4,4,2,3,8,384]{5,4,3,2,1,0:T(8,128)}) custom-call(s32[2]{0:T(128)} %pad_add_fusion.where_ref.refs_0_, f32[3,16,3,192,384]{4,3,2,1,0:T(8,128)} %bitcast.79, f32[3,16,3,192,384]{4,3,2,1,0:T(8,128)} %bitcast.80, ...), custom_call_target="tpu_custom_call" | custom-call | tf_op jit(solution)/shard_map/pack/pallas_call | solution.py:80
  513.2 14.7 %collective-permute-done.40.refs_3_ = f32[4,4,2,3,8,384]{5,4,3,2,1,0:T(8,128)S(1)} collective-permute-done((f32[4,4,2,3,8,384]{5,4,3,2,1,0:T(8,128)}, f32[4,4,2,3,8,384]{5,4,3,2,1,0:T(8,128)S(1)}, u32[]{:S(2)}, u32[]{:S(2)}) %collective-permute-start.40) | collective-permute-done | bytes 1179680 | tf_op jit(solution)/shard_map/ppermute | solution.py:471
  536.8 20.4 %multiply.8 = (f32[256,768]{1,0:T(8,128)}, f32[256,768]{1,0:T(8,128)}) custom-call(s32[11]{0:T(128)} %stack.65.refs_0_, f32[84,8,384]{2,1,0:T(8,128)} %get-tuple-element.221.refs_8_.refs_3_.refs_4_.refs_1_, f32[168,8,384]{2,1,0:T(8,128)} %copy-done.3, f32[144,8,384]{2,1,0:T(8,128)} %collective-permute-done.32.rest_0_.refs_3_, ...), custom_call_target="tpu_custom_call" | custom-call | tf_op jit(solution)/shard_map/multiply/pallas_call | solution.py:356
  563.4 7.2 collective-permute-start.50
  573.0 12.1 %collective-permute-done.50.refs_2_ = f32[4,4,2,3,8,384]{5,4,3,2,1,0:T(8,128)S(1)} collective-permute-done((f32[4,4,2,3,8,384]{5,4,3,2,1,0:T(8,128)}, f32[4,4,2,3,8,384]{5,4,3,2,1,0:T(8,128)S(1)}, u32[]{:S(2)}, u32[]{:S(2)}) %collective-permute-start.50) | collective-permute-done | bytes 1179680 | tf_op jit(solution)/shard_map/ppermute | solution.py:471
  585.1 14.9 %collective-permute-done.51.refs_3_ = f32[4,4,2,3,8,384]{5,4,3,2,1,0:T(8,128)S(1)} collective-permute-done((f32[4,4,2,3,8,384]{5,4,3,2,1,0:T(8,128)}, f32[4,4,2,3,8,384]{5,4,3,2,1,0:T(8,128)S(1)}, u32[]{:S(2)}, u32[]{:S(2)}) %collective-permute-start.51) | collective-permute-done | bytes 1179680 | tf_op jit(solution)/shard_map/ppermute | solution.py:471
  600.5 7.7 pack.22
  608.3 6.7 orient.21
  615.0 7.0 collective-permute-done.49.arrived_ref.refs_2_
  622.0 13.1 %collective-permute-done.48.rest_0_.refs_6_ = f32[144,8,384]{2,1,0:T(8,128)S(1)} collective-permute-done((f32[144,8,384]{2,1,0:T(8,128)}, f32[144,8,384]{2,1,0:T(8,128)S(1)}, u32[]{:S(2)}, u32[]{:S(2)}) %collective-permute-start.48) | collective-permute-done | bytes 1769504 | tf_op jit(solution)/shard_map/ppermute | solution.py:471
  649.3 9.5 spread.4
  664.2 12.3 %collective-permute-done.54.refs_3_ = f32[4,4,1,3,8,384]{5,4,3,2,1,0:T(8,128)S(1)} collective-permute-done((f32[4,4,1,3,8,384]{5,4,3,2,1,0:T(8,128)}, f32[4,4,1,3,8,384]{5,4,3,2,1,0:T(8,128)S(1)}, u32[]{:S(2)}, u32[]{:S(2)}) %collective-permute-start.54) | collective-permute-done | bytes 589856 | tf_op jit(solution)/shard_map/ppermute | solution.py:471
  677.4 7.7 pack.23
  690.4 6.7 collective-permute-done.44
  698.0 20.3 %multiply.9 = (f32[256,768]{1,0:T(8,128)}, f32[256,768]{1,0:T(8,128)}) custom-call(s32[11]{0:T(128)} %stack.65.refs_0_, f32[84,8,384]{2,1,0:T(8,128)} %get-tuple-element.247.refs_8_.rest_1_.refs_3_.refs_4_.refs_1_, f32[168,8,384]{2,1,0:T(8,128)} %copy-done.5, f32[144,8,384]{2,1,0:T(8,128)} %collective-permute-done.46.rest_0_.refs_3_, ...), custom_call_target="tpu_custom_call" | custom-call | tf_op jit(solution)/shard_map/multiply/pallas_call | solution.py:356
  732.9 7.1 collective-permute-done.57.refs_2_.arrived_ref
  746.9 9.2 collective-permute-start.58
  773.3 53.3 %collective-permute-done.63.refs_6_ = f32[144,8,384]{2,1,0:T(8,128)S(1)} collective-permute-done((f32[144,8,384]{2,1,0:T(8,128)}, f32[144,8,384]{2,1,0:T(8,128)S(1)}, u32[]{:S(2)}, u32[]{:S(2)}) %collective-permute-start.63) | collective-permute-done | bytes 1769504 | tf_op jit(solution)/shard_map/ppermute | solution.py:471
  827.8 20.4 %multiply.10 = (f32[256,768]{1,0:T(8,128)}, f32[256,768]{1,0:T(8,128)}) custom-call(s32[11]{0:T(128)} %stack.65.refs_0_, f32[84,8,384]{2,1,0:T(8,128)} %get-tuple-element.273.refs_8_.refs_6_.rest_1_.refs_3_.refs_4_.refs_1_, f32[168,8,384]{2,1,0:T(8,128)} %copy-done.4, f32[144,8,384]{2,1,0:T(8,128)} %copy-done.1, ...), custom_call_target="tpu_custom_call" | custom-call | tf_op jit(solution)/shard_map/multiply/pallas_call | solution.py:356
  869.7 9.2 collective-permute-done.70
  882.2 29.1 %collective-permute-done.76.refs_6_ = f32[84,8,384]{2,1,0:T(8,128)S(1)} collective-permute-done((f32[84,8,384]{2,1,0:T(8,128)}, f32[84,8,384]{2,1,0:T(8,128)S(1)}, u32[]{:S(2)}, u32[]{:S(2)}) %collective-permute-start.76) | collective-permute-done | bytes 1032224 | tf_op jit(solution)/shard_map/ppermute | solution.py:471
  912.3 16.5 %multiply.11 = (f32[160,768]{1,0:T(8,128)}, f32[160,768]{1,0:T(8,128)}) custom-call(s32[11]{0:T(128)} %stack.58.refs_0_, f32[48,8,384]{2,1,0:T(8,128)} %get-tuple-element.303.refs_9_.rest_1_.refs_4_.refs_1_, f32[96,8,384]{2,1,0:T(8,128)} %copy-done.2, f32[84,8,384]{2,1,0:T(8,128)} %copy-done.14, f32[48,8,384]{2,1,0:T(8,128)} %get-tuple-element.322.rest_1_.refs_9_.refs_4_, ...), custom_call_target="tpu_custom_call" | custom-call | tf_op jit(solution)/shard_map/multiply/pallas_call | solution.py:356
  957.0 14.4 %collective-permute-done.73.refs_2_ = f32[128,768]{1,0:T(8,128)S(1)} collective-permute-done((f32[128,768]{1,0:T(8,128)S(1)}, f32[128,768]{1,0:T(8,128)S(1)}, u32[]{:S(2)}, u32[]{:S(2)}) %collective-permute-start.73) | collective-permute-done | bytes 393248 | tf_op jit(solution)/shard_map/ppermute | solution.py:471
  971.5 8.8 collective-permute-done.82.refs_6_
  (331 shorter events, 315.7 us)
Async XLA Ops:
  11.2 27.6 %collective-permute-start.1 = (f32[4,4,1,3,8,384]{5,4,3,2,1,0:T(8,128)}, f32[4,4,1,3,8,384]{5,4,3,2,1,0:T(8,128)S(1)}, u32[]{:S(2)}, u32[]{:S(2)}) collective-permute-start(f32[4,4,1,3,8,384]{5,4,3,2,1,0:T(8,128)} %get-tuple-element.175), channel_id=1, source_target_pairs={{0,4},{2,6},{4,0},{6,2},{8,12},{10,14},{12,8},{14,10},{16,20},{18,... | collective-permute-start | bytes 1769480 | tf_op jit(solution)/shard_map/ppermute | solution.py:471
  45.1 35.8 %collective-permute-start.3 = (f32[96,8,384]{2,1,0:T(8,128)}, f32[96,8,384]{2,1,0:T(8,128)S(1)}, u32[]{:S(2)}, u32[]{:S(2)}) collective-permute-start(f32[96,8,384]{2,1,0:T(8,128)} %get-tuple-element.179), channel_id=1, source_target_pairs={{0,8},{2,10},{4,12},{6,14},{8,0},{10,2},{12,4},{14,6},{16,24},{18,... | collective-permute-start | bytes 3538952 | tf_op jit(solution)/shard_map/ppermute | solution.py:471
  80.4 62.3 %collective-permute-start.8 = (f32[96,8,384]{2,1,0:T(8,128)}, f32[96,8,384]{2,1,0:T(8,128)S(1)}, u32[]{:S(2)}, u32[]{:S(2)}) collective-permute-start(f32[96,8,384]{2,1,0:T(8,128)} %get-tuple-element.190), channel_id=1, source_target_pairs={{0,8},{2,10},{4,12},{6,14},{8,0},{10,2},{12,4},{14,6},{16,24},{18,... | collective-permute-start | bytes 3538952 | tf_op jit(solution)/shard_map/ppermute | solution.py:471
  85.1 57.6 %collective-permute-start.4 = (f32[84,8,384]{2,1,0:T(8,128)}, f32[84,8,384]{2,1,0:T(8,128)}, u32[]{:S(2)}, u32[]{:S(2)}) collective-permute-start(f32[84,8,384]{2,1,0:T(8,128)} %get-tuple-element.181), channel_id=1, source_target_pairs={{0,16},{2,18},{4,20},{6,22},{8,24},{10,26},{12,28},{14,30},{16,0},... | collective-permute-start | bytes 3096584 | tf_op jit(solution)/shard_map/ppermute | solution.py:471
  119.0 51.9 %collective-permute-start.13 = (f32[96,8,384]{2,1,0:T(8,128)}, f32[96,8,384]{2,1,0:T(8,128)S(1)}, u32[]{:S(2)}, u32[]{:S(2)}) collective-permute-start(f32[96,8,384]{2,1,0:T(8,128)} %get-tuple-element.207), channel_id=1, source_target_pairs={{0,8},{2,10},{4,12},{6,14},{8,0},{10,2},{12,4},{14,6},{16,24},{18,... | collective-permute-start | bytes 3538952 | tf_op jit(solution)/shard_map/ppermute | solution.py:471
  146.9 36.2 %collective-permute-start.9 = (f32[84,8,384]{2,1,0:T(8,128)}, f32[84,8,384]{2,1,0:T(8,128)S(1)}, u32[]{:S(2)}, u32[]{:S(2)}) collective-permute-start(f32[84,8,384]{2,1,0:T(8,128)} %get-tuple-element.192), channel_id=1, source_target_pairs={{0,16},{2,18},{4,20},{6,22},{8,24},{10,26},{12,28},{14,30},{16,0},... | collective-permute-start | bytes 3096584 | tf_op jit(solution)/shard_map/ppermute | solution.py:471
  187.5 42.7 %collective-permute-start.18 = (f32[4,4,2,3,8,384]{5,4,3,2,1,0:T(8,128)}, f32[4,4,2,3,8,384]{5,4,3,2,1,0:T(8,128)S(1)}, u32[]{:S(2)}, u32[]{:S(2)}) collective-permute-start(f32[4,4,2,3,8,384]{5,4,3,2,1,0:T(8,128)} %get-tuple-element.218), channel_id=1, source_target_pairs={{0,4},{2,6},{4,0},{6,2},{8,12},{10,14},{12,8},{14,10},{16,20},{18,... | collective-permute-start | bytes 3538952 | tf_op jit(solution)/shard_map/ppermute | solution.py:471
  187.6 42.6 %collective-permute-start.19 = (f32[4,4,2,3,8,384]{5,4,3,2,1,0:T(8,128)}, f32[4,4,2,3,8,384]{5,4,3,2,1,0:T(8,128)S(1)}, u32[]{:S(2)}, u32[]{:S(2)}) collective-permute-start(f32[4,4,2,3,8,384]{5,4,3,2,1,0:T(8,128)} %get-tuple-element.219), channel_id=1, source_target_pairs={{0,6},{2,4},{4,2},{6,0},{8,14},{10,12},{12,10},{14,8},{16,22},{18,... | collective-permute-start | bytes 3538952 | tf_op jit(solution)/shard_map/ppermute | solution.py:471
  190.9 49.7 %collective-permute-start.22 = (f32[96,8,384]{2,1,0:T(8,128)}, f32[96,8,384]{2,1,0:T(8,128)S(1)}, u32[]{:S(2)}, u32[]{:S(2)}) collective-permute-start(f32[96,8,384]{2,1,0:T(8,128)} %get-tuple-element.225), channel_id=1, source_target_pairs={{0,8},{2,10},{4,12},{6,14},{8,0},{10,2},{12,4},{14,6},{16,24},{18,... | collective-permute-start | bytes 3538952 | tf_op jit(solution)/shard_map/ppermute | solution.py:471
  190.9 49.7 %collective-permute-start.21 = (f32[84,8,384]{2,1,0:T(8,128)S(1)}, f32[84,8,384]{2,1,0:T(8,128)S(1)}, u32[]{:S(2)}, u32[]{:S(2)}) collective-permute-start(f32[84,8,384]{2,1,0:T(8,128)S(1)} %copy-done.38), channel_id=1, source_target_pairs={{0,16},{2,18},{4,20},{6,22},{8,24},{10,26},{12,28},{14,30},{16,0},... | collective-permute-start | bytes 3096584 | tf_op jit(solution)/shard_map/ppermute | solution.py:471
  238.1 78.2 %collective-permute-start.24 = (f32[168,8,384]{2,1,0:T(8,128)}, f32[168,8,384]{2,1,0:T(8,128)S(1)}, u32[]{:S(2)}, u32[]{:S(2)}) collective-permute-start(f32[168,8,384]{2,1,0:T(8,128)} %get-tuple-element.233), channel_id=1, source_target_pairs={{0,8},{2,10},{4,12},{6,14},{8,0},{10,2},{12,4},{14,6},{16,24},{18,... | collective-permute-start | bytes 6193160 | tf_op jit(solution)/shard_map/ppermute | solution.py:471
  245.3 29.1 %collective-permute-start.25 = (f32[4,4,2,3,8,384]{5,4,3,2,1,0:T(8,128)}, f32[4,4,2,3,8,384]{5,4,3,2,1,0:T(8,128)S(1)}, u32[]{:S(2)}, u32[]{:S(2)}) collective-permute-start(f32[4,4,2,3,8,384]{5,4,3,2,1,0:T(8,128)} %get-tuple-element.238), channel_id=1, source_target_pairs={{0,2},{2,0},{4,6},{6,4},{8,10},{10,8},{12,14},{14,12},{16,18},{18,... | collective-permute-start | bytes 3538952 | tf_op jit(solution)/shard_map/ppermute | solution.py:471
  246.3 44.5 %collective-permute-start.26 = (f32[4,4,2,3,8,384]{5,4,3,2,1,0:T(8,128)}, f32[4,4,2,3,8,384]{5,4,3,2,1,0:T(8,128)S(1)}, u32[]{:S(2)}, u32[]{:S(2)}) collective-permute-start(f32[4,4,2,3,8,384]{5,4,3,2,1,0:T(8,128)} %get-tuple-element.239), channel_id=1, source_target_pairs={{0,4},{2,6},{4,0},{6,2},{8,12},{10,14},{12,8},{14,10},{16,20},{18,... | collective-permute-start | bytes 3538952 | tf_op jit(solution)/shard_map/ppermute | solution.py:471
  247.4 43.4 %collective-permute-start.27 = (f32[4,4,2,3,8,384]{5,4,3,2,1,0:T(8,128)}, f32[4,4,2,3,8,384]{5,4,3,2,1,0:T(8,128)S(1)}, u32[]{:S(2)}, u32[]{:S(2)}) collective-permute-start(f32[4,4,2,3,8,384]{5,4,3,2,1,0:T(8,128)} %get-tuple-element.240), channel_id=1, source_target_pairs={{0,6},{2,4},{4,2},{6,0},{8,14},{10,12},{12,10},{14,8},{16,22},{18,... | collective-permute-start | bytes 3538952 | tf_op jit(solution)/shard_map/ppermute | solution.py:471
  248.8 67.6 %collective-permute-start.23 = (f32[84,8,384]{2,1,0:T(8,128)}, f32[84,8,384]{2,1,0:T(8,128)S(1)}, u32[]{:S(2)}, u32[]{:S(2)}) collective-permute-start(f32[84,8,384]{2,1,0:T(8,128)} %get-tuple-element.227), channel_id=1, source_target_pairs={{0,16},{2,18},{4,20},{6,22},{8,24},{10,26},{12,28},{14,30},{16,0},... | collective-permute-start | bytes 3096584 | tf_op jit(solution)/shard_map/ppermute | solution.py:471
  298.7 93.2 %collective-permute-start.33 = (f32[168,8,384]{2,1,0:T(8,128)}, f32[168,8,384]{2,1,0:T(8,128)}, u32[]{:S(2)}, u32[]{:S(2)}) collective-permute-start(f32[168,8,384]{2,1,0:T(8,128)} %get-tuple-element.251), channel_id=1, source_target_pairs={{0,8},{2,10},{4,12},{6,14},{8,0},{10,2},{12,4},{14,6},{16,24},{18,... | collective-permute-start | bytes 6193160 | tf_op jit(solution)/shard_map/ppermute | solution.py:471
  322.9 69.7 %collective-permute-start.32 = (f32[144,8,384]{2,1,0:T(8,128)}, f32[144,8,384]{2,1,0:T(8,128)}, u32[]{:S(2)}, u32[]{:S(2)}) collective-permute-start(f32[144,8,384]{2,1,0:T(8,128)} %get-tuple-element.250), channel_id=1, source_target_pairs={{0,16},{2,18},{4,20},{6,22},{8,24},{10,26},{12,28},{14,30},{16,0},... | collective-permute-start | bytes 5308424 | tf_op jit(solution)/shard_map/ppermute | solution.py:471
  323.6 28.2 %collective-permute-start.28 = (f32[4,4,2,3,8,384]{5,4,3,2,1,0:T(8,128)}, f32[4,4,2,3,8,384]{5,4,3,2,1,0:T(8,128)S(1)}, u32[]{:S(2)}, u32[]{:S(2)}) collective-permute-start(f32[4,4,2,3,8,384]{5,4,3,2,1,0:T(8,128)} %get-tuple-element.243), channel_id=1, source_target_pairs={{0,2},{2,0},{4,6},{6,4},{8,10},{10,8},{12,14},{14,12},{16,18},{18,... | collective-permute-start | bytes 3538952 | tf_op jit(solution)/shard_map/ppermute | solution.py:471
  324.0 42.4 %collective-permute-start.29 = (f32[4,4,2,3,8,384]{5,4,3,2,1,0:T(8,128)}, f32[4,4,2,3,8,384]{5,4,3,2,1,0:T(8,128)S(1)}, u32[]{:S(2)}, u32[]{:S(2)}) collective-permute-start(f32[4,4,2,3,8,384]{5,4,3,2,1,0:T(8,128)} %get-tuple-element.244), channel_id=1, source_target_pairs={{0,4},{2,6},{4,0},{6,2},{8,12},{10,14},{12,8},{14,10},{16,20},{18,... | collective-permute-start | bytes 3538952 | tf_op jit(solution)/shard_map/ppermute | solution.py:471
  325.0 41.4 %collective-permute-start.30 = (f32[4,4,2,3,8,384]{5,4,3,2,1,0:T(8,128)}, f32[4,4,2,3,8,384]{5,4,3,2,1,0:T(8,128)S(1)}, u32[]{:S(2)}, u32[]{:S(2)}) collective-permute-start(f32[4,4,2,3,8,384]{5,4,3,2,1,0:T(8,128)} %get-tuple-element.245), channel_id=1, source_target_pairs={{0,6},{2,4},{4,2},{6,0},{8,14},{10,12},{12,10},{14,8},{16,22},{18,... | collective-permute-start | bytes 3538952 | tf_op jit(solution)/shard_map/ppermute | solution.py:471
  374.2 112.2 %collective-permute-start.35 = (f32[168,8,384]{2,1,0:T(8,128)}, f32[168,8,384]{2,1,0:T(8,128)S(1)}, u32[]{:S(2)}, u32[]{:S(2)}) collective-permute-start(f32[168,8,384]{2,1,0:T(8,128)} %get-tuple-element.259), channel_id=1, source_target_pairs={{0,8},{2,10},{4,12},{6,14},{8,0},{10,2},{12,4},{14,6},{16,24},{18,... | collective-permute-start | bytes 6193160 | tf_op jit(solution)/shard_map/ppermute | solution.py:471
  397.5 88.8 %collective-permute-start.34 = (f32[144,8,384]{2,1,0:T(8,128)}, f32[144,8,384]{2,1,0:T(8,128)}, u32[]{:S(2)}, u32[]{:S(2)}) collective-permute-start(f32[144,8,384]{2,1,0:T(8,128)} %get-tuple-element.253), channel_id=1, source_target_pairs={{0,16},{2,18},{4,20},{6,22},{8,24},{10,26},{12,28},{14,30},{16,0},... | collective-permute-start | bytes 5308424 | tf_op jit(solution)/shard_map/ppermute | solution.py:471
  399.6 28.6 %collective-permute-start.36 = (f32[4,4,2,3,8,384]{5,4,3,2,1,0:T(8,128)}, f32[4,4,2,3,8,384]{5,4,3,2,1,0:T(8,128)S(1)}, u32[]{:S(2)}, u32[]{:S(2)}) collective-permute-start(f32[4,4,2,3,8,384]{5,4,3,2,1,0:T(8,128)} %get-tuple-element.264), channel_id=1, source_target_pairs={{0,2},{2,0},{4,6},{6,4},{8,10},{10,8},{12,14},{14,12},{16,18},{18,... | collective-permute-start | bytes 3538952 | tf_op jit(solution)/shard_map/ppermute | solution.py:471
  400.7 41.6 %collective-permute-start.37 = (f32[4,4,2,3,8,384]{5,4,3,2,1,0:T(8,128)}, f32[4,4,2,3,8,384]{5,4,3,2,1,0:T(8,128)S(1)}, u32[]{:S(2)}, u32[]{:S(2)}) collective-permute-start(f32[4,4,2,3,8,384]{5,4,3,2,1,0:T(8,128)} %get-tuple-element.265), channel_id=1, source_target_pairs={{0,4},{2,6},{4,0},{6,2},{8,12},{10,14},{12,8},{14,10},{16,20},{18,... | collective-permute-start | bytes 3538952 | tf_op jit(solution)/shard_map/ppermute | solution.py:471
  404.5 37.8 %collective-permute-start.38 = (f32[4,4,2,3,8,384]{5,4,3,2,1,0:T(8,128)}, f32[4,4,2,3,8,384]{5,4,3,2,1,0:T(8,128)S(1)}, u32[]{:S(2)}, u32[]{:S(2)}) collective-permute-start(f32[4,4,2,3,8,384]{5,4,3,2,1,0:T(8,128)} %get-tuple-element.266), channel_id=1, source_target_pairs={{0,6},{2,4},{4,2},{6,0},{8,14},{10,12},{12,10},{14,8},{16,22},{18,... | collective-permute-start | bytes 3538952 | tf_op jit(solution)/shard_map/ppermute | solution.py:471
  450.3 106.8 %collective-permute-start.47 = (f32[168,8,384]{2,1,0:T(8,128)}, f32[168,8,384]{2,1,0:T(8,128)}, u32[]{:S(2)}, u32[]{:S(2)}) collective-permute-start(f32[168,8,384]{2,1,0:T(8,128)} %get-tuple-element.281), channel_id=1, source_target_pairs={{0,8},{2,10},{4,12},{6,14},{8,0},{10,2},{12,4},{14,6},{16,24},{18,... | collective-permute-start | bytes 6193160 | tf_op jit(solution)/shard_map/ppermute | solution.py:471
  492.7 65.9 %collective-permute-start.46 = (f32[144,8,384]{2,1,0:T(8,128)}, f32[144,8,384]{2,1,0:T(8,128)}, u32[]{:S(2)}, u32[]{:S(2)}) collective-permute-start(f32[144,8,384]{2,1,0:T(8,128)} %get-tuple-element.280), channel_id=1, source_target_pairs={{0,16},{2,18},{4,20},{6,22},{8,24},{10,26},{12,28},{14,30},{16,0},... | collective-permute-start | bytes 5308424 | tf_op jit(solution)/shard_map/ppermute | solution.py:471
  498.8 29.1 %collective-permute-start.40 = (f32[4,4,2,3,8,384]{5,4,3,2,1,0:T(8,128)}, f32[4,4,2,3,8,384]{5,4,3,2,1,0:T(8,128)S(1)}, u32[]{:S(2)}, u32[]{:S(2)}) collective-permute-start(f32[4,4,2,3,8,384]{5,4,3,2,1,0:T(8,128)} %get-tuple-element.270), channel_id=1, source_target_pairs={{0,4},{2,6},{4,0},{6,2},{8,12},{10,14},{12,8},{14,10},{16,20},{18,... | collective-permute-start | bytes 3538952 | tf_op jit(solution)/shard_map/ppermute | solution.py:471
  498.8 29.1 %collective-permute-start.41 = (f32[4,4,2,3,8,384]{5,4,3,2,1,0:T(8,128)}, f32[4,4,2,3,8,384]{5,4,3,2,1,0:T(8,128)S(1)}, u32[]{:S(2)}, u32[]{:S(2)}) collective-permute-start(f32[4,4,2,3,8,384]{5,4,3,2,1,0:T(8,128)} %get-tuple-element.271), channel_id=1, source_target_pairs={{0,6},{2,4},{4,2},{6,0},{8,14},{10,12},{12,10},{14,8},{16,22},{18,... | collective-permute-start | bytes 3538952 | tf_op jit(solution)/shard_map/ppermute | solution.py:471
  535.8 86.2 %collective-permute-start.49 = (f32[168,8,384]{2,1,0:T(8,128)}, f32[168,8,384]{2,1,0:T(8,128)S(1)}, u32[]{:S(2)}, u32[]{:S(2)}) collective-permute-start(f32[168,8,384]{2,1,0:T(8,128)} %get-tuple-element.289), channel_id=1, source_target_pairs={{0,8},{2,10},{4,12},{6,14},{8,0},{10,2},{12,4},{14,6},{16,24},{18,... | collective-permute-start | bytes 6193160 | tf_op jit(solution)/shard_map/ppermute | solution.py:471
  570.7 64.4 %collective-permute-start.48 = (f32[144,8,384]{2,1,0:T(8,128)}, f32[144,8,384]{2,1,0:T(8,128)S(1)}, u32[]{:S(2)}, u32[]{:S(2)}) collective-permute-start(f32[144,8,384]{2,1,0:T(8,128)} %get-tuple-element.283), channel_id=1, source_target_pairs={{0,16},{2,18},{4,20},{6,22},{8,24},{10,26},{12,28},{14,30},{16,0},... | collective-permute-start | bytes 5308424 | tf_op jit(solution)/shard_map/ppermute | solution.py:471
  570.7 29.3 %collective-permute-start.51 = (f32[4,4,2,3,8,384]{5,4,3,2,1,0:T(8,128)}, f32[4,4,2,3,8,384]{5,4,3,2,1,0:T(8,128)S(1)}, u32[]{:S(2)}, u32[]{:S(2)}) collective-permute-start(f32[4,4,2,3,8,384]{5,4,3,2,1,0:T(8,128)} %get-tuple-element.295), channel_id=1, source_target_pairs={{0,4},{2,6},{4,0},{6,2},{8,12},{10,14},{12,8},{14,10},{16,20},{18,... | collective-permute-start | bytes 3538952 | tf_op jit(solution)/shard_map/ppermute | solution.py:471
  585.1 62.7 %collective-permute-start.42 = (f32[256,768]{1,0:T(8,128)}, f32[256,768]{1,0:T(8,128)}, u32[]{:S(2)}, u32[]{:S(2)}) collective-permute-start(f32[256,768]{1,0:T(8,128)} %get-tuple-element.275), channel_id=1, source_target_pairs={{0,1},{1,0},{2,3},{3,2},{4,5},{5,4},{6,7},{7,6},{8,9},{9,8},{10,11... | collective-permute-start | bytes 2359304 | tf_op jit(solution)/shard_map/ppermute | solution.py:515
  600.0 42.6 %collective-permute-start.20 = (f32[160,768]{1,0:T(8,128)}, f32[160,768]{1,0:T(8,128)}, u32[]{:S(2)}, u32[]{:S(2)}) collective-permute-start(f32[160,768]{1,0:T(8,128)} %get-tuple-element.223), channel_id=1, source_target_pairs={{0,1},{1,0},{2,3},{3,2},{4,5},{5,4},{6,7},{7,6},{8,9},{9,8},{10,11... | collective-permute-start | bytes 1474568 | tf_op jit(solution)/shard_map/ppermute | solution.py:515
  600.0 47.7 %collective-permute-start.31 = (f32[160,768]{1,0:T(8,128)}, f32[160,768]{1,0:T(8,128)}, u32[]{:S(2)}, u32[]{:S(2)}) collective-permute-start(f32[160,768]{1,0:T(8,128)} %get-tuple-element.249), channel_id=1, source_target_pairs={{0,1},{1,0},{2,3},{3,2},{4,5},{5,4},{6,7},{7,6},{8,9},{9,8},{10,11... | collective-permute-start | bytes 1474568 | tf_op jit(solution)/shard_map/ppermute | solution.py:515
  622.0 96.3 %collective-permute-start.62 = (f32[168,8,384]{2,1,0:T(8,128)}, f32[168,8,384]{2,1,0:T(8,128)}, u32[]{:S(2)}, u32[]{:S(2)}) collective-permute-start(f32[168,8,384]{2,1,0:T(8,128)} %get-tuple-element.312), channel_id=1, source_target_pairs={{0,8},{2,10},{4,12},{6,14},{8,0},{10,2},{12,4},{14,6},{16,24},{18,... | collective-permute-start | bytes 6193160 | tf_op jit(solution)/shard_map/ppermute | solution.py:471
  641.2 77.1 %collective-permute-start.61 = (f32[144,8,384]{2,1,0:T(8,128)}, f32[144,8,384]{2,1,0:T(8,128)S(1)}, u32[]{:S(2)}, u32[]{:S(2)}) collective-permute-start(f32[144,8,384]{2,1,0:T(8,128)} %get-tuple-element.311), channel_id=1, source_target_pairs={{0,16},{2,18},{4,20},{6,22},{8,24},{10,26},{12,28},{14,30},{16,0},... | collective-permute-start | bytes 5308424 | tf_op jit(solution)/shard_map/ppermute | solution.py:471
  647.7 28.8 %collective-permute-start.54 = (f32[4,4,1,3,8,384]{5,4,3,2,1,0:T(8,128)}, f32[4,4,1,3,8,384]{5,4,3,2,1,0:T(8,128)S(1)}, u32[]{:S(2)}, u32[]{:S(2)}) collective-permute-start(f32[4,4,1,3,8,384]{5,4,3,2,1,0:T(8,128)} %get-tuple-element.300), channel_id=1, source_target_pairs={{0,4},{2,6},{4,0},{6,2},{8,12},{10,14},{12,8},{14,10},{16,20},{18,... | collective-permute-start | bytes 1769480 | tf_op jit(solution)/shard_map/ppermute | solution.py:471
  647.8 29.6 %collective-permute-start.55 = (f32[4,4,1,3,8,384]{5,4,3,2,1,0:T(8,128)}, f32[4,4,1,3,8,384]{5,4,3,2,1,0:T(8,128)S(1)}, u32[]{:S(2)}, u32[]{:S(2)}) collective-permute-start(f32[4,4,1,3,8,384]{5,4,3,2,1,0:T(8,128)} %get-tuple-element.301), channel_id=1, source_target_pairs={{0,6},{2,4},{4,2},{6,0},{8,14},{10,12},{12,10},{14,8},{16,22},{18,... | collective-permute-start | bytes 1769480 | tf_op jit(solution)/shard_map/ppermute | solution.py:471
  662.2 28.2 %collective-permute-start.43 = (f32[4,64,768]{2,1,0:T(8,128)}, f32[4,64,768]{2,1,0:T(8,128)S(1)}, u32[]{:S(2)}, u32[]{:S(2)}) collective-permute-start(f32[4,64,768]{2,1,0:T(8,128)} %get-tuple-element.277), channel_id=1, source_target_pairs={{0,2},{2,0},{4,6},{6,4},{8,10},{10,8},{12,14},{14,12},{16,18},{18,... | collective-permute-start | bytes 2359304 | tf_op jit(solution)/shard_map/ppermute | solution.py:471
  690.4 49.6 %collective-permute-start.57 = (f32[96,8,384]{2,1,0:T(8,128)}, f32[96,8,384]{2,1,0:T(8,128)S(1)}, u32[]{:S(2)}, u32[]{:S(2)}) collective-permute-start(f32[96,8,384]{2,1,0:T(8,128)} %get-tuple-element.306), channel_id=1, source_target_pairs={{0,8},{2,10},{4,12},{6,14},{8,0},{10,2},{12,4},{14,6},{16,24},{18,... | collective-permute-start | bytes 3538952 | tf_op jit(solution)/shard_map/ppermute | solution.py:471
  724.5 102.0 %collective-permute-start.63 = (f32[144,8,384]{2,1,0:T(8,128)}, f32[144,8,384]{2,1,0:T(8,128)S(1)}, u32[]{:S(2)}, u32[]{:S(2)}) collective-permute-start(f32[144,8,384]{2,1,0:T(8,128)} %get-tuple-element.314), channel_id=1, source_target_pairs={{0,16},{2,18},{4,20},{6,22},{8,24},{10,26},{12,28},{14,30},{16,0},... | collective-permute-start | bytes 5308424 | tf_op jit(solution)/shard_map/ppermute | solution.py:471
  724.9 31.3 %collective-permute-start.64 = (f32[4,4,1,3,8,384]{5,4,3,2,1,0:T(8,128)}, f32[4,4,1,3,8,384]{5,4,3,2,1,0:T(8,128)S(1)}, u32[]{:S(2)}, u32[]{:S(2)}) collective-permute-start(f32[4,4,1,3,8,384]{5,4,3,2,1,0:T(8,128)} %get-tuple-element.319), channel_id=1, source_target_pairs={{0,2},{2,0},{4,6},{6,4},{8,10},{10,8},{12,14},{14,12},{16,18},{18,... | collective-permute-start | bytes 1769480 | tf_op jit(solution)/shard_map/ppermute | solution.py:471
  763.7 84.6 %collective-permute-start.68 = (f32[96,8,384]{2,1,0:T(8,128)}, f32[96,8,384]{2,1,0:T(8,128)S(1)}, u32[]{:S(2)}, u32[]{:S(2)}) collective-permute-start(f32[96,8,384]{2,1,0:T(8,128)} %get-tuple-element.327), channel_id=1, source_target_pairs={{0,8},{2,10},{4,12},{6,14},{8,0},{10,2},{12,4},{14,6},{16,24},{18,... | collective-permute-start | bytes 3538952 | tf_op jit(solution)/shard_map/ppermute | solution.py:471
  767.4 93.6 %collective-permute-start.75 = (f32[84,8,384]{2,1,0:T(8,128)}, f32[84,8,384]{2,1,0:T(8,128)S(1)}, u32[]{:S(2)}, u32[]{:S(2)}) collective-permute-start(f32[84,8,384]{2,1,0:T(8,128)} %get-tuple-element.332), channel_id=1, source_target_pairs={{0,16},{2,18},{4,20},{6,22},{8,24},{10,26},{12,28},{14,30},{16,0},... | collective-permute-start | bytes 3096584 | tf_op jit(solution)/shard_map/ppermute | solution.py:471
  865.4 45.9 %collective-permute-start.76 = (f32[84,8,384]{2,1,0:T(8,128)}, f32[84,8,384]{2,1,0:T(8,128)S(1)}, u32[]{:S(2)}, u32[]{:S(2)}) collective-permute-start(f32[84,8,384]{2,1,0:T(8,128)} %get-tuple-element.334), channel_id=1, source_target_pairs={{0,16},{2,18},{4,20},{6,22},{8,24},{10,26},{12,28},{14,30},{16,0},... | collective-permute-start | bytes 3096584 | tf_op jit(solution)/shard_map/ppermute | solution.py:471
  939.2 32.2 %collective-permute-start.73 = (f32[128,768]{1,0:T(8,128)S(1)}, f32[128,768]{1,0:T(8,128)S(1)}, u32[]{:S(2)}, u32[]{:S(2)}) collective-permute-start(f32[128,768]{1,0:T(8,128)S(1)} %copy-done.18), channel_id=1, source_target_pairs={{0,16},{2,18},{4,20},{6,22},{8,24},{10,26},{12,28},{14,30},{16,0},... | collective-permute-start | bytes 1179656 | tf_op jit(solution)/shard_map/ppermute | solution.py:471
  943.7 27.8 %collective-permute-start.74 = (f32[128,768]{1,0:T(8,128)S(1)}, f32[128,768]{1,0:T(8,128)S(1)}, u32[]{:S(2)}, u32[]{:S(2)}) collective-permute-start(f32[128,768]{1,0:T(8,128)S(1)} %copy-done.17), channel_id=1, source_target_pairs={{0,24},{2,26},{4,28},{6,30},{8,16},{10,18},{12,20},{14,22},{16,8},... | collective-permute-start | bytes 1179656 | tf_op jit(solution)/shard_map/ppermute | solution.py:471
  (107 other events, 1089.3 us)

commit v2 on v1

--- a/solution.py
+++ b/solution.py
@@ -267,8 +267,9 @@
     return jnp.stack(own + pairs + [lax.axis_index("vir")]).astype(jnp.int32)
 
 
-def multiply_kernel(spans, place_ref, *refs):
-    b_ref, mine, theirs, hi, lo = refs[3 * len(spans)], *refs[-4:]
+def multiply_kernel(parts, add, place_ref, *refs):
+    b_ref, mine_in, theirs_in = refs[3 * len(parts) : 3 * len(parts) + 3]
+    mine, theirs, hi, lo = refs[-4:]
     lanes = refs[0].shape[-1]
 
     def gather(sizes, begin, kept, near, far):
@@ -313,8 +314,10 @@
 
     @pl.when(pl.program_id(0) == 0)
     def _():
-        for at, (sizes, begin) in enumerate(spans):
+        begin = 0
+        for at, sizes in enumerate(parts):
             gather(sizes, begin, *refs[3 * at : 3 * at + 3])
+            begin += sizes.deep
 
     b = b_ref[...].reshape(b_ref.shape[0] * b_ref.shape[1], b_ref.shape[2])
     b_hi = b.astype(jnp.bfloat16)
@@ -325,34 +328,39 @@
 
     @pl.when(pl.program_id(0) < half)
     def _():
-        theirs[...] = c
+        theirs[...] = c + theirs_in[...] if add else c
 
     @pl.when(pl.program_id(0) >= half)
     def _():
-        mine[...] = c
-
-
-def multiply(place, parts, integrals, after):
+        mine[...] = c + mine_in[...] if add else c
+
+
+def multiply(place, begin, parts, integrals, earlier, after):
     cs, ds, columns = integrals.shape
-    rows = parts[0][0].rows
+    lanes = parts[0][1][0].shape[-1]
+    rows, deep = parts[0][0].rows, sum(sizes.deep for sizes, _ in parts)
+    depth = deep * CHUNK
     wide = 256
     half = columns // wide // 2
-    arrays = [x for _, _, three in parts for x in three]
-    lanes = arrays[0].shape[-1]
+
+    def kernel(*refs):
+        multiply_kernel([sizes for sizes, _ in parts], len(earlier) > 0, *refs)
+
+    def column(n, w):
+        return lax.rem(n + (1 - w[PLANES + 6]) * half, 2 * half)
+
+    out_specs = [
+        pl.BlockSpec((rows, wide), lambda n, w: (0, jnp.maximum(n - half, 0))),
+        pl.BlockSpec((rows, wide), lambda n, w: (0, jnp.minimum(n, half - 1))),
+    ]
     in_specs = []
-    for sizes, _, _ in parts:
+    for sizes, _ in parts:
         in_specs += [
             pl.BlockSpec((sizes.full, SUB, lanes), lambda n, w: (0, 0, 0)),
             pl.BlockSpec((sizes.full, SUB, lanes), lambda n, w: (1, 0, 0)),
             pl.BlockSpec((sizes.far, SUB, lanes), lambda n, w: (0, 0, 0)),
         ]
-
-    def kernel(*refs):
-        multiply_kernel([(sizes, begin) for sizes, begin, _ in parts], *refs)
-
-    def column(n, w):
-        return lax.rem(n + (1 - w[PLANES + 6]) * half, 2 * half)
-
+    in_specs.append(pl.BlockSpec((depth, ds, wide), lambda n, w: (begin // deep, 0, column(n, w))))
     return pl.pallas_call(
         kernel,
         out_shape=[jax.ShapeDtypeStruct((rows, columns // 2), jnp.float32)] * 2,
@@ -360,22 +368,15 @@
             num_scalar_prefetch=1,
             grid=(2 * half,),
             in_specs=in_specs
-            + [pl.BlockSpec((cs, ds, wide), lambda n, w: (0, 0, column(n, w)))]
+            + out_specs[: len(earlier)]
             + [pl.BlockSpec(memory_space=pl.ANY)] * len(after),
-            out_specs=[
-                pl.BlockSpec((rows, wide), lambda n, w: (0, jnp.maximum(n - half, 0))),
-                pl.BlockSpec((rows, wide), lambda n, w: (0, jnp.minimum(n, half - 1))),
-            ],
-            scratch_shapes=[pltpu.VMEM((rows, cs * ds), jnp.bfloat16)] * 2,
+            out_specs=out_specs,
+            scratch_shapes=[pltpu.VMEM((rows, depth * ds), jnp.bfloat16)] * 2,
         ),
         compiler_params=pltpu.CompilerParams(vmem_limit_bytes=VMEM),
-        cost_estimate=pl.CostEstimate(
-            flops=0,
-            transcendentals=0,
-            bytes_accessed=0
-        ),
+        cost_estimate=pl.CostEstimate(flops=0, transcendentals=0, bytes_accessed=0),
         name="multiply",
-    )(place, *arrays, integrals, *after)
+    )(place, *[x for _, arrays in parts for x in arrays], integrals, *earlier, *after)
 
 
 def row_table(sizes):
@@ -450,12 +451,15 @@
 
     def kernel(*refs):
         out = refs[-1]
-        for at, (pairs, _) in enumerate(batches):
-            a, b, c, d = refs[PLANES * at : PLANES * (at + 1)]
+        begin = 0
+        for pairs, parts in batches:
             for n, (r, s) in enumerate(pairs):
                 rows = pl.ds(n * OWNERS, OWNERS)
-                total = (a[rows, :] + b[rows, :]) + (c[rows, :] + d[rows, :])
+                total = refs[begin][rows, :]
+                for at in range(1, len(parts)):
+                    total = total + refs[begin + at][rows, :]
                 out[pl.ds(r * O + s, OWNERS, stride=SHARE), :] = total
+            begin += len(parts)
 
     return pl.pallas_call(
         kernel,
@@ -480,7 +484,7 @@
     for pair in CLASSES:
         chunks += [(pair, (0, deep // 2), False), (pair, (deep // 2, deep), True)]
     kepts, nears, tokens, fars, products = [], [], [], [], []
-    parts, batch, batches, ready = [], [], [], []
+    parts, earlier, batch, batches, ready = [], [], [], [], []
 
     def last(arrays, back=1):
         return arrays[-back:][:1] if len(arrays) >= back else []
@@ -489,38 +493,47 @@
         pair, span, _ = chunks[at]
         return pack(where, amplitudes, pair, span, last(kepts))
 
+    def sizes_of(at):
+        (r, s), span, _ = chunks[at]
+        return Sizes(1 if r == s else 2, span[1] - span[0])
+
     def first_half(at):
         own, *others = coming
         if kepts:
-            others = hold(others, last(tokens, 1) + last(kepts))
+            others = hold(others, last(tokens) + last(kepts))
         ys = [own] + [exchange(x, m) for m, x in enumerate(others, 1)]
-        upcoming = packed(at + 1) if at + 1 < len(chunks) else []
+        upcoming = packed(at + 1) if at + 1 < count else []
         kept, near, far = orient(where, ys, sizes_of(at), list(upcoming[:1]))
         kepts.append(kept)
         nears.append((exchange(near, SPOTS), far))
         return upcoming
 
-    def sizes_of(at):
-        (r, s), span, _ = chunks[at]
-        return Sizes(1 if r == s else 2, span[1] - span[0])
-
-    def second_half(at, after):
-        nonlocal parts, batch, ready
+    def second_half(at, after, until=[]):
+        nonlocal earlier, parts, batch, ready
         (r, s), span, ends = chunks[at]
-        parts.append((sizes_of(at), span[0], (kepts[at], nears[at][0], fars[at])))
+        sizes = sizes_of(at)
+        parts.append((sizes, (kepts[at], nears[at][0], fars[at])))
+        if not ends and (r, s) != CLASSES[-1]:
+            return
+        begin = span[1] - sum(part.deep for part, _ in parts)
+        after = ready + after
+        earlier = multiply(place_of(z, sizes), begin, parts, integrals, earlier, after)
+        parts = []
         if not ends:
             return
-        mine, theirs = multiply(place_of(z, sizes_of(at)), parts, integrals, ready + after)
+        mine, theirs = earlier
         products.append(mine)
-        theirs = lax.ppermute(theirs, "vir", [(0, 1), (1, 0)])
-        batch.append((sizes_of(at), mine, theirs, [(r, s)] if r == s else [(r, s), (s, r)]))
-        parts = []
+        earlier = []
+        pairs = [(r, s)] if r == s else [(r, s), (s, r)]
+        batch.append((sizes, mine, lax.ppermute(theirs, "vir", [(0, 1), (1, 0)]), pairs))
         if (r, s) not in BATCH_ENDS:
             return
-        before = nears[-1][:1] if batches else kepts[-1:]
-        rows = spread(where, [x[:3] for x in batch], list(before))
+        before = list(nears[-1][:1] if batches else kepts[-1:])
+        rows = spread(where, [x[:3] for x in batch], before)
         rows = [rows[0]] + [exchange(rows[m], m) for m in range(1, SPOTS)]
-        plane = [rows[0][dr] + rows[1][dr] + rows[2][dr] + rows[3][dr] for dr in range(PLANES)]
+        if until:
+            rows = hold(rows, until)
+        plane = [rows[0][n] + rows[1][n] + rows[2][n] + rows[3][n] for n in range(PLANES)]
         ready = plane[:1]
         batches.append(([pair for x in batch for pair in x[3]], plane))
         batch = []
@@ -528,14 +541,15 @@
     def over_planes(plane):
         return plane[:1] + [exchange(plane[dr], dr * SPOTS) for dr in range(1, PLANES)]
 
+    count = len(chunks)
     coming = packed(0)
     coming = first_half(0)
-    count = len(chunks)
     for at in range(count):
         if at + 1 < count:
             coming = first_half(at + 1)
         if at >= 2:
-            second_half(at - 2, kepts[-1:] + (tokens[-1:] if at + 1 == count else []))
+            after = tokens[-1:] if at + 1 == count else []
+            second_half(at - 2, kepts[-1:] + after)
         before = last(fars, 2 if at + 2 == count else 1)
         if at >= 4:
             before = before + last(kepts) + last(products)
@@ -545,9 +559,11 @@
         fars.append(exchange(far, 2 * SPOTS))
     second_half(count - 2, [])
     early = [pair for pairs, _ in batches for pair in pairs]
-    plane = [jnp.concatenate([x[dr] for _, x in batches]) for dr in range(PLANES)]
-    second_half(count - 1, plane)
-    return collect([(pairs, over_planes(x)) for pairs, x in [(early, plane), batches[-1]]])
+    plane = [jnp.concatenate([x[n] for _, x in batches]) for n in range(PLANES)]
+    sums = over_planes(plane)
+    second_half(count - 1, plane, sums[1:])
+    pairs, plane = batches[-1]
+    return collect([(early, sums), (pairs, over_planes(plane))])
 
 
 def regrouped(amplitudes, integrals):

time: 989 us -> 981 us (level)
  waiting for transfers between devices: 452 us -> 432 us
    ppermute x78, waiting for transfers between devices: 448 us -> 430 us  [exchange(): return lax.ppermute(x, 'occ', [(n, n ^ bits) for n in range(OWNERS)])]
    pallas_call x6 -> x7, Pallas kernels: 111 us -> 117 us  [multiply(): pl.pallas_call(kernel, out_shape=[jax.ShapeDtypeStruct((rows, columns //...]
    unnamed x142 -> x148, local copies, waits for them, and re-layouts: 28.8 us -> 30 us
  transfers between devices with their start and end apart: 84 -> 84, of which waited for: 42 -> 43; matrix products, arithmetic and copies ran while one was open for 1% -> 1% of each run, Pallas kernels for 35% -> 37%
where the time goes in v2:
time: 981 us; the launch traced here: 977 us
  waiting for transfers between devices  432 us (44%)
  Pallas kernels  389 us (40%)
  starting transfers between devices  117 us (12%)
  local copies, waits for them, and re-layouts  31.2 us (3%)
    ppermute x78, waiting for transfers between devices, exchange(): return lax.ppermute(x, 'occ', [(n, n ^ bits) for n in range(OWNERS)])  430 us
    pallas_call x12, Pallas kernels, pack(): pl.pallas_call(pack_kernel, out_shape=[jax.ShapeDtypeStruct(shape, jnp.fl...  123 us
    pallas_call x7, Pallas kernels, multiply(): pl.pallas_call(kernel, out_shape=[jax.ShapeDtypeStruct((rows, columns //...  117 us
    ppermute x78, starting transfers between devices, exchange(): return lax.ppermute(x, 'occ', [(n, n ^ bits) for n in range(OWNERS)])  116 us
    pallas_call x12, Pallas kernels, orient(): pl.pallas_call(kernel, out_shape=[jax.ShapeDtypeStruct((n, SUB, lanes), j...  70.7 us
    pallas_call x12, Pallas kernels, merge(): pl.pallas_call(kernel, out_shape=[jax.ShapeDtypeStruct(far.shape, jnp.flo...  49.2 us
    unnamed x148, local copies, waits for them, and re-layouts  30 us
    pallas_call x4, Pallas kernels, spread(): pl.pallas_call(kernel, out_shape=[jax.ShapeDtypeStruct((PLANES, rows, col...  25.2 us
  transfers between devices with their start and end apart: 84, of which 43 were waited for; matrix products, arithmetic and copies ran while one was open for 1% of the time, Pallas kernels for 37%

profile of v2, /device:TPU:0, one launch (start us, length us, event | category | flops | bytes accessed | tf_op | source)
XLA Modules:
  0.0 977.2 jit_solution(17966696233279969180)
XLA Ops:
  0.6 7.8 pack.12
  12.9 7.7 pack.13
  25.7 13.3 %collective-permute-done.1.refs_3_ = f32[4,4,1,3,8,384]{5,4,3,2,1,0:T(8,128)S(1)} collective-permute-done((f32[4,4,1,3,8,384]{5,4,3,2,1,0:T(8,128)}, f32[4,4,1,3,8,384]{5,4,3,2,1,0:T(8,128)S(1)}, u32[]{:S(2)}, u32[]{:S(2)}) %collective-permute-start.1) | collective-permute-done | bytes 589856 | tf_op jit(solution)/shard_map/ppermute | solution.py:475
  50.4 7.7 pack.14
  63.4 11.0 %collective-permute-done.6.refs_3_ = f32[4,4,1,3,8,384]{5,4,3,2,1,0:T(8,128)S(1)} collective-permute-done((f32[4,4,1,3,8,384]{5,4,3,2,1,0:T(8,128)}, f32[4,4,1,3,8,384]{5,4,3,2,1,0:T(8,128)S(1)}, u32[]{:S(2)}, u32[]{:S(2)}) %collective-permute-start.6) | collective-permute-done | bytes 589856 | tf_op jit(solution)/shard_map/ppermute | solution.py:475
  91.7 7.7 pack.15
  104.7 8.3 collective-permute-done.11.refs_3_
  120.9 22.0 %collective-permute-done.8.arrived_ref.refs_5_ = f32[96,8,384]{2,1,0:T(8,128)S(1)} collective-permute-done((f32[96,8,384]{2,1,0:T(8,128)}, f32[96,8,384]{2,1,0:T(8,128)S(1)}, u32[]{:S(2)}, u32[]{:S(2)}) %collective-permute-start.8) | collective-permute-done | bytes 1179680 | tf_op jit(solution)/shard_map/ppermute | solution.py:475
  151.6 12.8 %pack.16 = (f32[4,4,2,3,8,384]{5,4,3,2,1,0:T(8,128)}, f32[4,4,2,3,8,384]{5,4,3,2,1,0:T(8,128)}, f32[4,4,2,3,8,384]{5,4,3,2,1,0:T(8,128)}, f32[4,4,2,3,8,384]{5,4,3,2,1,0:T(8,128)}) custom-call(s32[2]{0:T(128)} %pad_add_fusion.where_ref.refs_0_, f32[3,16,3,192,384]{4,3,2,1,0:T(8,128)} %bitcast.64, f32[3,16,3,192,384]{4,3,2,1,0:T(8,128)} %bitcast.65, ...), custom_call_target="tpu_custom_call" | custom-call | tf_op jit(solution)/shard_map/pack/pallas_call | solution.py:80
  171.2 12.2 %collective-permute-done.9.rest_0_.refs_6_ = f32[84,8,384]{2,1,0:T(8,128)S(1)} collective-permute-done((f32[84,8,384]{2,1,0:T(8,128)}, f32[84,8,384]{2,1,0:T(8,128)S(1)}, u32[]{:S(2)}, u32[]{:S(2)}) %collective-permute-start.9) | collective-permute-done | bytes 1032224 | tf_op jit(solution)/shard_map/ppermute | solution.py:475
  193.7 12.8 %pack.17 = (f32[4,4,2,3,8,384]{5,4,3,2,1,0:T(8,128)}, f32[4,4,2,3,8,384]{5,4,3,2,1,0:T(8,128)}, f32[4,4,2,3,8,384]{5,4,3,2,1,0:T(8,128)}, f32[4,4,2,3,8,384]{5,4,3,2,1,0:T(8,128)}) custom-call(s32[2]{0:T(128)} %pad_add_fusion.where_ref.refs_0_, f32[3,16,3,192,384]{4,3,2,1,0:T(8,128)} %bitcast.69, f32[3,16,3,192,384]{4,3,2,1,0:T(8,128)} %bitcast.68, ...), custom_call_target="tpu_custom_call" | custom-call | tf_op jit(solution)/shard_map/pack/pallas_call | solution.py:80
  213.0 17.5 %collective-permute-done.18.refs_3_ = f32[4,4,2,3,8,384]{5,4,3,2,1,0:T(8,128)S(1)} collective-permute-done((f32[4,4,2,3,8,384]{5,4,3,2,1,0:T(8,128)}, f32[4,4,2,3,8,384]{5,4,3,2,1,0:T(8,128)S(1)}, u32[]{:S(2)}, u32[]{:S(2)}) %collective-permute-start.18) | collective-permute-done | bytes 1179680 | tf_op jit(solution)/shard_map/ppermute | solution.py:475
  249.2 12.8 %pack.18 = (f32[4,4,2,3,8,384]{5,4,3,2,1,0:T(8,128)}, f32[4,4,2,3,8,384]{5,4,3,2,1,0:T(8,128)}, f32[4,4,2,3,8,384]{5,4,3,2,1,0:T(8,128)}, f32[4,4,2,3,8,384]{5,4,3,2,1,0:T(8,128)}) custom-call(s32[2]{0:T(128)} %pad_add_fusion.where_ref.refs_0_, f32[3,16,3,192,384]{4,3,2,1,0:T(8,128)} %bitcast.70, f32[3,16,3,192,384]{4,3,2,1,0:T(8,128)} %bitcast.71, ...), custom_call_target="tpu_custom_call" | custom-call | tf_op jit(solution)/shard_map/pack/pallas_call | solution.py:80
  262.0 12.9 %collective-permute-done.25.refs_2_ = f32[4,4,2,3,8,384]{5,4,3,2,1,0:T(8,128)S(1)} collective-permute-done((f32[4,4,2,3,8,384]{5,4,3,2,1,0:T(8,128)}, f32[4,4,2,3,8,384]{5,4,3,2,1,0:T(8,128)S(1)}, u32[]{:S(2)}, u32[]{:S(2)}) %collective-permute-start.25) | collective-permute-done | bytes 1179680 | tf_op jit(solution)/shard_map/ppermute | solution.py:475
  274.9 16.5 %collective-permute-done.26.refs_3_ = f32[4,4,2,3,8,384]{5,4,3,2,1,0:T(8,128)S(1)} collective-permute-done((f32[4,4,2,3,8,384]{5,4,3,2,1,0:T(8,128)}, f32[4,4,2,3,8,384]{5,4,3,2,1,0:T(8,128)S(1)}, u32[]{:S(2)}, u32[]{:S(2)}) %collective-permute-start.26) | collective-permute-done | bytes 1179680 | tf_op jit(solution)/shard_map/ppermute | solution.py:475
  300.2 16.6 %multiply.7 = (f32[160,768]{1,0:T(8,128)}, f32[160,768]{1,0:T(8,128)}) custom-call(s32[11]{0:T(128)} %stack.58.refs_0_, f32[48,8,384]{2,1,0:T(8,128)} %get-tuple-element.184.refs_3_.refs_1_, f32[96,8,384]{2,1,0:T(8,128)} %copy-done.10, f32[84,8,384]{2,1,0:T(8,128)} %collective-permute-done.4.rest_0_.refs_3_, ...), custom_call_target="tpu_custom_call" | custom-call | tf_op jit(solution)/shard_map/multiply/pallas_call | solution.py:364
  327.6 12.8 %pack.19 = (f32[4,4,2,3,8,384]{5,4,3,2,1,0:T(8,128)}, f32[4,4,2,3,8,384]{5,4,3,2,1,0:T(8,128)}, f32[4,4,2,3,8,384]{5,4,3,2,1,0:T(8,128)}, f32[4,4,2,3,8,384]{5,4,3,2,1,0:T(8,128)}) custom-call(s32[2]{0:T(128)} %pad_add_fusion.where_ref.refs_0_, f32[3,16,3,192,384]{4,3,2,1,0:T(8,128)} %bitcast.73, f32[3,16,3,192,384]{4,3,2,1,0:T(8,128)} %bitcast.74, ...), custom_call_target="tpu_custom_call" | custom-call | tf_op jit(solution)/shard_map/pack/pallas_call | solution.py:80
  340.4 12.0 %collective-permute-done.28.refs_2_ = f32[4,4,2,3,8,384]{5,4,3,2,1,0:T(8,128)S(1)} collective-permute-done((f32[4,4,2,3,8,384]{5,4,3,2,1,0:T(8,128)}, f32[4,4,2,3,8,384]{5,4,3,2,1,0:T(8,128)S(1)}, u32[]{:S(2)}, u32[]{:S(2)}) %collective-permute-start.28) | collective-permute-done | bytes 1179680 | tf_op jit(solution)/shard_map/ppermute | solution.py:475
  352.3 14.5 %collective-permute-done.29.refs_3_ = f32[4,4,2,3,8,384]{5,4,3,2,1,0:T(8,128)S(1)} collective-permute-done((f32[4,4,2,3,8,384]{5,4,3,2,1,0:T(8,128)}, f32[4,4,2,3,8,384]{5,4,3,2,1,0:T(8,128)S(1)}, u32[]{:S(2)}, u32[]{:S(2)}) %collective-permute-start.29) | collective-permute-done | bytes 1179680 | tf_op jit(solution)/shard_map/ppermute | solution.py:475
  376.2 16.5 %multiply.8 = (f32[160,768]{1,0:T(8,128)}, f32[160,768]{1,0:T(8,128)}) custom-call(s32[11]{0:T(128)} %stack.58.refs_0_, f32[48,8,384]{2,1,0:T(8,128)} %get-tuple-element.207.refs_3_.refs_4_.refs_1_, f32[96,8,384]{2,1,0:T(8,128)} %copy-done.7, f32[84,8,384]{2,1,0:T(8,128)} %copy-done.12, f32[48,8,384]{2,1,0:T(8,128)} %get-tuple-element.222.refs_4_.refs_3_, ...), custom_call_target="tpu_custom_call" | custom-call | tf_op jit(solution)/shard_map/multiply/pallas_call | solution.py:364
  404.4 12.7 %pack.20 = (f32[4,4,2,3,8,384]{5,4,3,2,1,0:T(8,128)}, f32[4,4,2,3,8,384]{5,4,3,2,1,0:T(8,128)}, f32[4,4,2,3,8,384]{5,4,3,2,1,0:T(8,128)}, f32[4,4,2,3,8,384]{5,4,3,2,1,0:T(8,128)}) custom-call(s32[2]{0:T(128)} %pad_add_fusion.where_ref.refs_0_, f32[3,16,3,192,384]{4,3,2,1,0:T(8,128)} %bitcast.76, f32[3,16,3,192,384]{4,3,2,1,0:T(8,128)} %bitcast.77, ...), custom_call_target="tpu_custom_call" | custom-call | tf_op jit(solution)/shard_map/pack/pallas_call | solution.py:80
  417.1 11.8 %collective-permute-done.36.refs_2_ = f32[4,4,2,3,8,384]{5,4,3,2,1,0:T(8,128)S(1)} collective-permute-done((f32[4,4,2,3,8,384]{5,4,3,2,1,0:T(8,128)}, f32[4,4,2,3,8,384]{5,4,3,2,1,0:T(8,128)S(1)}, u32[]{:S(2)}, u32[]{:S(2)}) %collective-permute-start.36) | collective-permute-done | bytes 1179680 | tf_op jit(solution)/shard_map/ppermute | solution.py:475
  429.0 14.1 %collective-permute-done.37.refs_3_ = f32[4,4,2,3,8,384]{5,4,3,2,1,0:T(8,128)S(1)} collective-permute-done((f32[4,4,2,3,8,384]{5,4,3,2,1,0:T(8,128)}, f32[4,4,2,3,8,384]{5,4,3,2,1,0:T(8,128)S(1)}, u32[]{:S(2)}, u32[]{:S(2)}) %collective-permute-start.37) | collective-permute-done | bytes 1179680 | tf_op jit(solution)/shard_map/ppermute | solution.py:475
  451.9 35.1 %collective-permute-done.35.arrived_ref.refs_2_ = f32[168,8,384]{2,1,0:T(8,128)S(1)} collective-permute-done((f32[168,8,384]{2,1,0:T(8,128)}, f32[168,8,384]{2,1,0:T(8,128)S(1)}, u32[]{:S(2)}, u32[]{:S(2)}) %collective-permute-start.35) | collective-permute-done | bytes 2064416 | tf_op jit(solution)/shard_map/ppermute | solution.py:475
  500.9 12.7 %pack.21 = (f32[4,4,2,3,8,384]{5,4,3,2,1,0:T(8,128)}, f32[4,4,2,3,8,384]{5,4,3,2,1,0:T(8,128)}, f32[4,4,2,3,8,384]{5,4,3,2,1,0:T(8,128)}, f32[4,4,2,3,8,384]{5,4,3,2,1,0:T(8,128)}) custom-call(s32[2]{0:T(128)} %pad_add_fusion.where_ref.refs_0_, f32[3,16,3,192,384]{4,3,2,1,0:T(8,128)} %bitcast.79, f32[3,16,3,192,384]{4,3,2,1,0:T(8,128)} %bitcast.80, ...), custom_call_target="tpu_custom_call" | custom-call | tf_op jit(solution)/shard_map/pack/pallas_call | solution.py:80
  513.8 14.7 %collective-permute-done.40.refs_3_ = f32[4,4,2,3,8,384]{5,4,3,2,1,0:T(8,128)S(1)} collective-permute-done((f32[4,4,2,3,8,384]{5,4,3,2,1,0:T(8,128)}, f32[4,4,2,3,8,384]{5,4,3,2,1,0:T(8,128)S(1)}, u32[]{:S(2)}, u32[]{:S(2)}) %collective-permute-start.40) | collective-permute-done | bytes 1179680 | tf_op jit(solution)/shard_map/ppermute | solution.py:475
  536.9 20.4 %multiply.9 = (f32[256,768]{1,0:T(8,128)}, f32[256,768]{1,0:T(8,128)}) custom-call(s32[11]{0:T(128)} %stack.65.refs_0_, f32[84,8,384]{2,1,0:T(8,128)} %get-tuple-element.227.refs_8_.refs_3_.refs_4_.refs_1_, f32[168,8,384]{2,1,0:T(8,128)} %copy-done.3, f32[144,8,384]{2,1,0:T(8,128)} %collective-permute-done.32.rest_0_.refs_3_, ...), custom_call_target="tpu_custom_call" | custom-call | tf_op jit(solution)/shard_map/multiply/pallas_call | solution.py:364
  564.1 7.1 collective-permute-start.50
  574.1 11.5 %collective-permute-done.50.refs_2_ = f32[4,4,2,3,8,384]{5,4,3,2,1,0:T(8,128)S(1)} collective-permute-done((f32[4,4,2,3,8,384]{5,4,3,2,1,0:T(8,128)}, f32[4,4,2,3,8,384]{5,4,3,2,1,0:T(8,128)S(1)}, u32[]{:S(2)}, u32[]{:S(2)}) %collective-permute-start.50) | collective-permute-done | bytes 1179680 | tf_op jit(solution)/shard_map/ppermute | solution.py:475
  585.6 15.5 %collective-permute-done.51.refs_3_ = f32[4,4,2,3,8,384]{5,4,3,2,1,0:T(8,128)S(1)} collective-permute-done((f32[4,4,2,3,8,384]{5,4,3,2,1,0:T(8,128)}, f32[4,4,2,3,8,384]{5,4,3,2,1,0:T(8,128)S(1)}, u32[]{:S(2)}, u32[]{:S(2)}) %collective-permute-start.51) | collective-permute-done | bytes 1179680 | tf_op jit(solution)/shard_map/ppermute | solution.py:475
  601.6 7.7 pack.22
  609.3 6.8 orient.21
  620.6 14.6 %collective-permute-done.48.rest_0_.refs_6_ = f32[144,8,384]{2,1,0:T(8,128)S(1)} collective-permute-done((f32[144,8,384]{2,1,0:T(8,128)}, f32[144,8,384]{2,1,0:T(8,128)S(1)}, u32[]{:S(2)}, u32[]{:S(2)}) %collective-permute-start.48) | collective-permute-done | bytes 1769504 | tf_op jit(solution)/shard_map/ppermute | solution.py:475
  649.7 9.5 spread.4
  664.7 12.5 %collective-permute-done.54.refs_3_ = f32[4,4,1,3,8,384]{5,4,3,2,1,0:T(8,128)S(1)} collective-permute-done((f32[4,4,1,3,8,384]{5,4,3,2,1,0:T(8,128)}, f32[4,4,1,3,8,384]{5,4,3,2,1,0:T(8,128)S(1)}, u32[]{:S(2)}, u32[]{:S(2)}) %collective-permute-start.54) | collective-permute-done | bytes 589856 | tf_op jit(solution)/shard_map/ppermute | solution.py:475
  678.1 7.7 pack.23
  698.6 20.3 %multiply.10 = (f32[256,768]{1,0:T(8,128)}, f32[256,768]{1,0:T(8,128)}) custom-call(s32[11]{0:T(128)} %stack.65.refs_0_, f32[84,8,384]{2,1,0:T(8,128)} %get-tuple-element.253.refs_8_.rest_1_.refs_3_.refs_4_.refs_1_, f32[168,8,384]{2,1,0:T(8,128)} %copy-done.5, f32[144,8,384]{2,1,0:T(8,128)} %collective-permute-done.46.rest_0_.refs_3_, ...), custom_call_target="tpu_custom_call" | custom-call | tf_op jit(solution)/shard_map/multiply/pallas_call | solution.py:364
  732.0 7.8 collective-permute-done.57.refs_2_.arrived_ref
  746.7 7.8 collective-permute-start.58
  771.8 55.6 %collective-permute-done.63.refs_6_ = f32[144,8,384]{2,1,0:T(8,128)S(1)} collective-permute-done((f32[144,8,384]{2,1,0:T(8,128)}, f32[144,8,384]{2,1,0:T(8,128)S(1)}, u32[]{:S(2)}, u32[]{:S(2)}) %collective-permute-start.63) | collective-permute-done | bytes 1769504 | tf_op jit(solution)/shard_map/ppermute | solution.py:475
  828.7 20.4 %multiply.11 = (f32[256,768]{1,0:T(8,128)}, f32[256,768]{1,0:T(8,128)}) custom-call(s32[11]{0:T(128)} %stack.65.refs_0_, f32[84,8,384]{2,1,0:T(8,128)} %get-tuple-element.279.refs_8_.refs_6_.rest_1_.refs_3_.refs_4_.refs_1_, f32[168,8,384]{2,1,0:T(8,128)} %copy-done.4, f32[144,8,384]{2,1,0:T(8,128)} %copy-done.1, ...), custom_call_target="tpu_custom_call" | custom-call | tf_op jit(solution)/shard_map/multiply/pallas_call | solution.py:364
  871.3 7.6 collective-permute-done.71
  879.7 11.2 %multiply.12 = (f32[160,768]{1,0:T(8,128)}, f32[160,768]{1,0:T(8,128)}) custom-call(s32[11]{0:T(128)} %stack.58.refs_0_, f32[48,8,384]{2,1,0:T(8,128)} %get-tuple-element.309.refs_9_.rest_1_.refs_4_.refs_1_, f32[96,8,384]{2,1,0:T(8,128)} %copy-done.2, f32[84,8,384]{2,1,0:T(8,128)} %copy-done.14, f32[192,24,1536]{2,1,0:T(8,128)} %refs_4_.3, ...), custom_call_target="tpu_custom_call" | custom-call | tf_op jit(solution)/shard_map/multiply/pallas_call | solution.py:364
  893.9 18.2 %collective-permute-done.76.refs_3_ = f32[84,8,384]{2,1,0:T(8,128)S(1)} collective-permute-done((f32[84,8,384]{2,1,0:T(8,128)}, f32[84,8,384]{2,1,0:T(8,128)S(1)}, u32[]{:S(2)}, u32[]{:S(2)}) %collective-permute-start.76) | collective-permute-done | bytes 1032224 | tf_op jit(solution)/shard_map/ppermute | solution.py:475
  913.1 11.4 %multiply.13 = (f32[160,768]{1,0:T(8,128)}, f32[160,768]{1,0:T(8,128)}) custom-call(s32[11]{0:T(128)} %stack.58.refs_0_, f32[48,8,384]{2,1,0:T(8,128)} %get-tuple-element.328.rest_1_.refs_9_.refs_1_, f32[96,8,384]{2,1,0:T(8,128)} %copy-done, f32[84,8,384]{2,1,0:T(8,128)} %copy-done.43, f32[192,24,1536]{2,1,0:T(8,128)} %refs_4_.3, ...), custom_call_target="tpu_custom_call" | custom-call | tf_op jit(solution)/shard_map/multiply/pallas_call | solution.py:364
  935.8 8.3 collective-permute-done.72.refs_4_.refs_1_
  945.3 9.2 collective-permute-done.73.refs_5_.refs_2_
  959.7 8.5 collective-permute-start.82
  (339 shorter events, 320.9 us)
Async XLA Ops:
  11.4 27.6 %collective-permute-start.1 = (f32[4,4,1,3,8,384]{5,4,3,2,1,0:T(8,128)}, f32[4,4,1,3,8,384]{5,4,3,2,1,0:T(8,128)S(1)}, u32[]{:S(2)}, u32[]{:S(2)}) collective-permute-start(f32[4,4,1,3,8,384]{5,4,3,2,1,0:T(8,128)} %get-tuple-element.181), channel_id=1, source_target_pairs={{0,4},{2,6},{4,0},{6,2},{8,12},{10,14},{12,8},{14,10},{16,20},{18,... | collective-permute-start | bytes 1769480 | tf_op jit(solution)/shard_map/ppermute | solution.py:475
  45.3 35.8 %collective-permute-start.3 = (f32[96,8,384]{2,1,0:T(8,128)}, f32[96,8,384]{2,1,0:T(8,128)S(1)}, u32[]{:S(2)}, u32[]{:S(2)}) collective-permute-start(f32[96,8,384]{2,1,0:T(8,128)} %get-tuple-element.185), channel_id=1, source_target_pairs={{0,8},{2,10},{4,12},{6,14},{8,0},{10,2},{12,4},{14,6},{16,24},{18,... | collective-permute-start | bytes 3538952 | tf_op jit(solution)/shard_map/ppermute | solution.py:475
  80.7 62.3 %collective-permute-start.8 = (f32[96,8,384]{2,1,0:T(8,128)}, f32[96,8,384]{2,1,0:T(8,128)S(1)}, u32[]{:S(2)}, u32[]{:S(2)}) collective-permute-start(f32[96,8,384]{2,1,0:T(8,128)} %get-tuple-element.196), channel_id=1, source_target_pairs={{0,8},{2,10},{4,12},{6,14},{8,0},{10,2},{12,4},{14,6},{16,24},{18,... | collective-permute-start | bytes 3538952 | tf_op jit(solution)/shard_map/ppermute | solution.py:475
  85.4 57.5 %collective-permute-start.4 = (f32[84,8,384]{2,1,0:T(8,128)}, f32[84,8,384]{2,1,0:T(8,128)}, u32[]{:S(2)}, u32[]{:S(2)}) collective-permute-start(f32[84,8,384]{2,1,0:T(8,128)} %get-tuple-element.187), channel_id=1, source_target_pairs={{0,16},{2,18},{4,20},{6,22},{8,24},{10,26},{12,28},{14,30},{16,0},... | collective-permute-start | bytes 3096584 | tf_op jit(solution)/shard_map/ppermute | solution.py:475
  119.3 51.9 %collective-permute-start.13 = (f32[96,8,384]{2,1,0:T(8,128)}, f32[96,8,384]{2,1,0:T(8,128)S(1)}, u32[]{:S(2)}, u32[]{:S(2)}) collective-permute-start(f32[96,8,384]{2,1,0:T(8,128)} %get-tuple-element.213), channel_id=1, source_target_pairs={{0,8},{2,10},{4,12},{6,14},{8,0},{10,2},{12,4},{14,6},{16,24},{18,... | collective-permute-start | bytes 3538952 | tf_op jit(solution)/shard_map/ppermute | solution.py:475
  147.2 36.2 %collective-permute-start.9 = (f32[84,8,384]{2,1,0:T(8,128)}, f32[84,8,384]{2,1,0:T(8,128)S(1)}, u32[]{:S(2)}, u32[]{:S(2)}) collective-permute-start(f32[84,8,384]{2,1,0:T(8,128)} %get-tuple-element.198), channel_id=1, source_target_pairs={{0,16},{2,18},{4,20},{6,22},{8,24},{10,26},{12,28},{14,30},{16,0},... | collective-permute-start | bytes 3096584 | tf_op jit(solution)/shard_map/ppermute | solution.py:475
  187.8 42.6 %collective-permute-start.18 = (f32[4,4,2,3,8,384]{5,4,3,2,1,0:T(8,128)}, f32[4,4,2,3,8,384]{5,4,3,2,1,0:T(8,128)S(1)}, u32[]{:S(2)}, u32[]{:S(2)}) collective-permute-start(f32[4,4,2,3,8,384]{5,4,3,2,1,0:T(8,128)} %get-tuple-element.224), channel_id=1, source_target_pairs={{0,4},{2,6},{4,0},{6,2},{8,12},{10,14},{12,8},{14,10},{16,20},{18,... | collective-permute-start | bytes 3538952 | tf_op jit(solution)/shard_map/ppermute | solution.py:475
  187.9 42.5 %collective-permute-start.19 = (f32[4,4,2,3,8,384]{5,4,3,2,1,0:T(8,128)}, f32[4,4,2,3,8,384]{5,4,3,2,1,0:T(8,128)S(1)}, u32[]{:S(2)}, u32[]{:S(2)}) collective-permute-start(f32[4,4,2,3,8,384]{5,4,3,2,1,0:T(8,128)} %get-tuple-element.225), channel_id=1, source_target_pairs={{0,6},{2,4},{4,2},{6,0},{8,14},{10,12},{12,10},{14,8},{16,22},{18,... | collective-permute-start | bytes 3538952 | tf_op jit(solution)/shard_map/ppermute | solution.py:475
  191.2 49.9 %collective-permute-start.22 = (f32[96,8,384]{2,1,0:T(8,128)}, f32[96,8,384]{2,1,0:T(8,128)S(1)}, u32[]{:S(2)}, u32[]{:S(2)}) collective-permute-start(f32[96,8,384]{2,1,0:T(8,128)} %get-tuple-element.231), channel_id=1, source_target_pairs={{0,8},{2,10},{4,12},{6,14},{8,0},{10,2},{12,4},{14,6},{16,24},{18,... | collective-permute-start | bytes 3538952 | tf_op jit(solution)/shard_map/ppermute | solution.py:475
  191.2 49.9 %collective-permute-start.21 = (f32[84,8,384]{2,1,0:T(8,128)S(1)}, f32[84,8,384]{2,1,0:T(8,128)S(1)}, u32[]{:S(2)}, u32[]{:S(2)}) collective-permute-start(f32[84,8,384]{2,1,0:T(8,128)S(1)} %copy-done.42), channel_id=1, source_target_pairs={{0,16},{2,18},{4,20},{6,22},{8,24},{10,26},{12,28},{14,30},{16,0},... | collective-permute-start | bytes 3096584 | tf_op jit(solution)/shard_map/ppermute | solution.py:475
  238.6 78.3 %collective-permute-start.24 = (f32[168,8,384]{2,1,0:T(8,128)}, f32[168,8,384]{2,1,0:T(8,128)S(1)}, u32[]{:S(2)}, u32[]{:S(2)}) collective-permute-start(f32[168,8,384]{2,1,0:T(8,128)} %get-tuple-element.239), channel_id=1, source_target_pairs={{0,8},{2,10},{4,12},{6,14},{8,0},{10,2},{12,4},{14,6},{16,24},{18,... | collective-permute-start | bytes 6193160 | tf_op jit(solution)/shard_map/ppermute | solution.py:475
  245.7 29.1 %collective-permute-start.25 = (f32[4,4,2,3,8,384]{5,4,3,2,1,0:T(8,128)}, f32[4,4,2,3,8,384]{5,4,3,2,1,0:T(8,128)S(1)}, u32[]{:S(2)}, u32[]{:S(2)}) collective-permute-start(f32[4,4,2,3,8,384]{5,4,3,2,1,0:T(8,128)} %get-tuple-element.244), channel_id=1, source_target_pairs={{0,2},{2,0},{4,6},{6,4},{8,10},{10,8},{12,14},{14,12},{16,18},{18,... | collective-permute-start | bytes 3538952 | tf_op jit(solution)/shard_map/ppermute | solution.py:475
  246.8 44.6 %collective-permute-start.26 = (f32[4,4,2,3,8,384]{5,4,3,2,1,0:T(8,128)}, f32[4,4,2,3,8,384]{5,4,3,2,1,0:T(8,128)S(1)}, u32[]{:S(2)}, u32[]{:S(2)}) collective-permute-start(f32[4,4,2,3,8,384]{5,4,3,2,1,0:T(8,128)} %get-tuple-element.245), channel_id=1, source_target_pairs={{0,4},{2,6},{4,0},{6,2},{8,12},{10,14},{12,8},{14,10},{16,20},{18,... | collective-permute-start | bytes 3538952 | tf_op jit(solution)/shard_map/ppermute | solution.py:475
  247.9 43.5 %collective-permute-start.27 = (f32[4,4,2,3,8,384]{5,4,3,2,1,0:T(8,128)}, f32[4,4,2,3,8,384]{5,4,3,2,1,0:T(8,128)S(1)}, u32[]{:S(2)}, u32[]{:S(2)}) collective-permute-start(f32[4,4,2,3,8,384]{5,4,3,2,1,0:T(8,128)} %get-tuple-element.246), channel_id=1, source_target_pairs={{0,6},{2,4},{4,2},{6,0},{8,14},{10,12},{12,10},{14,8},{16,22},{18,... | collective-permute-start | bytes 3538952 | tf_op jit(solution)/shard_map/ppermute | solution.py:475
  249.2 67.7 %collective-permute-start.23 = (f32[84,8,384]{2,1,0:T(8,128)}, f32[84,8,384]{2,1,0:T(8,128)S(1)}, u32[]{:S(2)}, u32[]{:S(2)}) collective-permute-start(f32[84,8,384]{2,1,0:T(8,128)} %get-tuple-element.233), channel_id=1, source_target_pairs={{0,16},{2,18},{4,20},{6,22},{8,24},{10,26},{12,28},{14,30},{16,0},... | collective-permute-start | bytes 3096584 | tf_op jit(solution)/shard_map/ppermute | solution.py:475
  299.3 93.3 %collective-permute-start.33 = (f32[168,8,384]{2,1,0:T(8,128)}, f32[168,8,384]{2,1,0:T(8,128)}, u32[]{:S(2)}, u32[]{:S(2)}) collective-permute-start(f32[168,8,384]{2,1,0:T(8,128)} %get-tuple-element.257), channel_id=1, source_target_pairs={{0,8},{2,10},{4,12},{6,14},{8,0},{10,2},{12,4},{14,6},{16,24},{18,... | collective-permute-start | bytes 6193160 | tf_op jit(solution)/shard_map/ppermute | solution.py:475
  323.5 69.7 %collective-permute-start.32 = (f32[144,8,384]{2,1,0:T(8,128)}, f32[144,8,384]{2,1,0:T(8,128)}, u32[]{:S(2)}, u32[]{:S(2)}) collective-permute-start(f32[144,8,384]{2,1,0:T(8,128)} %get-tuple-element.256), channel_id=1, source_target_pairs={{0,16},{2,18},{4,20},{6,22},{8,24},{10,26},{12,28},{14,30},{16,0},... | collective-permute-start | bytes 5308424 | tf_op jit(solution)/shard_map/ppermute | solution.py:475
  324.1 28.2 %collective-permute-start.28 = (f32[4,4,2,3,8,384]{5,4,3,2,1,0:T(8,128)}, f32[4,4,2,3,8,384]{5,4,3,2,1,0:T(8,128)S(1)}, u32[]{:S(2)}, u32[]{:S(2)}) collective-permute-start(f32[4,4,2,3,8,384]{5,4,3,2,1,0:T(8,128)} %get-tuple-element.249), channel_id=1, source_target_pairs={{0,2},{2,0},{4,6},{6,4},{8,10},{10,8},{12,14},{14,12},{16,18},{18,... | collective-permute-start | bytes 3538952 | tf_op jit(solution)/shard_map/ppermute | solution.py:475
  324.4 42.4 %collective-permute-start.29 = (f32[4,4,2,3,8,384]{5,4,3,2,1,0:T(8,128)}, f32[4,4,2,3,8,384]{5,4,3,2,1,0:T(8,128)S(1)}, u32[]{:S(2)}, u32[]{:S(2)}) collective-permute-start(f32[4,4,2,3,8,384]{5,4,3,2,1,0:T(8,128)} %get-tuple-element.250), channel_id=1, source_target_pairs={{0,4},{2,6},{4,0},{6,2},{8,12},{10,14},{12,8},{14,10},{16,20},{18,... | collective-permute-start | bytes 3538952 | tf_op jit(solution)/shard_map/ppermute | solution.py:475
  325.5 41.4 %collective-permute-start.30 = (f32[4,4,2,3,8,384]{5,4,3,2,1,0:T(8,128)}, f32[4,4,2,3,8,384]{5,4,3,2,1,0:T(8,128)S(1)}, u32[]{:S(2)}, u32[]{:S(2)}) collective-permute-start(f32[4,4,2,3,8,384]{5,4,3,2,1,0:T(8,128)} %get-tuple-element.251), channel_id=1, source_target_pairs={{0,6},{2,4},{4,2},{6,0},{8,14},{10,12},{12,10},{14,8},{16,22},{18,... | collective-permute-start | bytes 3538952 | tf_op jit(solution)/shard_map/ppermute | solution.py:475
  374.8 112.3 %collective-permute-start.35 = (f32[168,8,384]{2,1,0:T(8,128)}, f32[168,8,384]{2,1,0:T(8,128)S(1)}, u32[]{:S(2)}, u32[]{:S(2)}) collective-permute-start(f32[168,8,384]{2,1,0:T(8,128)} %get-tuple-element.265), channel_id=1, source_target_pairs={{0,8},{2,10},{4,12},{6,14},{8,0},{10,2},{12,4},{14,6},{16,24},{18,... | collective-permute-start | bytes 6193160 | tf_op jit(solution)/shard_map/ppermute | solution.py:475
  398.1 88.9 %collective-permute-start.34 = (f32[144,8,384]{2,1,0:T(8,128)}, f32[144,8,384]{2,1,0:T(8,128)}, u32[]{:S(2)}, u32[]{:S(2)}) collective-permute-start(f32[144,8,384]{2,1,0:T(8,128)} %get-tuple-element.259), channel_id=1, source_target_pairs={{0,16},{2,18},{4,20},{6,22},{8,24},{10,26},{12,28},{14,30},{16,0},... | collective-permute-start | bytes 5308424 | tf_op jit(solution)/shard_map/ppermute | solution.py:475
  400.3 28.7 %collective-permute-start.36 = (f32[4,4,2,3,8,384]{5,4,3,2,1,0:T(8,128)}, f32[4,4,2,3,8,384]{5,4,3,2,1,0:T(8,128)S(1)}, u32[]{:S(2)}, u32[]{:S(2)}) collective-permute-start(f32[4,4,2,3,8,384]{5,4,3,2,1,0:T(8,128)} %get-tuple-element.270), channel_id=1, source_target_pairs={{0,2},{2,0},{4,6},{6,4},{8,10},{10,8},{12,14},{14,12},{16,18},{18,... | collective-permute-start | bytes 3538952 | tf_op jit(solution)/shard_map/ppermute | solution.py:475
  401.4 41.7 %collective-permute-start.37 = (f32[4,4,2,3,8,384]{5,4,3,2,1,0:T(8,128)}, f32[4,4,2,3,8,384]{5,4,3,2,1,0:T(8,128)S(1)}, u32[]{:S(2)}, u32[]{:S(2)}) collective-permute-start(f32[4,4,2,3,8,384]{5,4,3,2,1,0:T(8,128)} %get-tuple-element.271), channel_id=1, source_target_pairs={{0,4},{2,6},{4,0},{6,2},{8,12},{10,14},{12,8},{14,10},{16,20},{18,... | collective-permute-start | bytes 3538952 | tf_op jit(solution)/shard_map/ppermute | solution.py:475
  404.4 38.7 %collective-permute-start.38 = (f32[4,4,2,3,8,384]{5,4,3,2,1,0:T(8,128)}, f32[4,4,2,3,8,384]{5,4,3,2,1,0:T(8,128)S(1)}, u32[]{:S(2)}, u32[]{:S(2)}) collective-permute-start(f32[4,4,2,3,8,384]{5,4,3,2,1,0:T(8,128)} %get-tuple-element.272), channel_id=1, source_target_pairs={{0,6},{2,4},{4,2},{6,0},{8,14},{10,12},{12,10},{14,8},{16,22},{18,... | collective-permute-start | bytes 3538952 | tf_op jit(solution)/shard_map/ppermute | solution.py:475
  451.0 106.2 %collective-permute-start.47 = (f32[168,8,384]{2,1,0:T(8,128)}, f32[168,8,384]{2,1,0:T(8,128)}, u32[]{:S(2)}, u32[]{:S(2)}) collective-permute-start(f32[168,8,384]{2,1,0:T(8,128)} %get-tuple-element.287), channel_id=1, source_target_pairs={{0,8},{2,10},{4,12},{6,14},{8,0},{10,2},{12,4},{14,6},{16,24},{18,... | collective-permute-start | bytes 6193160 | tf_op jit(solution)/shard_map/ppermute | solution.py:475
  493.4 65.8 %collective-permute-start.46 = (f32[144,8,384]{2,1,0:T(8,128)}, f32[144,8,384]{2,1,0:T(8,128)}, u32[]{:S(2)}, u32[]{:S(2)}) collective-permute-start(f32[144,8,384]{2,1,0:T(8,128)} %get-tuple-element.286), channel_id=1, source_target_pairs={{0,16},{2,18},{4,20},{6,22},{8,24},{10,26},{12,28},{14,30},{16,0},... | collective-permute-start | bytes 5308424 | tf_op jit(solution)/shard_map/ppermute | solution.py:475
  499.4 29.1 %collective-permute-start.40 = (f32[4,4,2,3,8,384]{5,4,3,2,1,0:T(8,128)}, f32[4,4,2,3,8,384]{5,4,3,2,1,0:T(8,128)S(1)}, u32[]{:S(2)}, u32[]{:S(2)}) collective-permute-start(f32[4,4,2,3,8,384]{5,4,3,2,1,0:T(8,128)} %get-tuple-element.276), channel_id=1, source_target_pairs={{0,4},{2,6},{4,0},{6,2},{8,12},{10,14},{12,8},{14,10},{16,20},{18,... | collective-permute-start | bytes 3538952 | tf_op jit(solution)/shard_map/ppermute | solution.py:475
  499.4 29.1 %collective-permute-start.41 = (f32[4,4,2,3,8,384]{5,4,3,2,1,0:T(8,128)}, f32[4,4,2,3,8,384]{5,4,3,2,1,0:T(8,128)S(1)}, u32[]{:S(2)}, u32[]{:S(2)}) collective-permute-start(f32[4,4,2,3,8,384]{5,4,3,2,1,0:T(8,128)} %get-tuple-element.277), channel_id=1, source_target_pairs={{0,6},{2,4},{4,2},{6,0},{8,14},{10,12},{12,10},{14,8},{16,22},{18,... | collective-permute-start | bytes 3538952 | tf_op jit(solution)/shard_map/ppermute | solution.py:475
  536.3 84.3 %collective-permute-start.49 = (f32[168,8,384]{2,1,0:T(8,128)}, f32[168,8,384]{2,1,0:T(8,128)S(1)}, u32[]{:S(2)}, u32[]{:S(2)}) collective-permute-start(f32[168,8,384]{2,1,0:T(8,128)} %get-tuple-element.295), channel_id=1, source_target_pairs={{0,8},{2,10},{4,12},{6,14},{8,0},{10,2},{12,4},{14,6},{16,24},{18,... | collective-permute-start | bytes 6193160 | tf_op jit(solution)/shard_map/ppermute | solution.py:475
  571.2 64.0 %collective-permute-start.48 = (f32[144,8,384]{2,1,0:T(8,128)}, f32[144,8,384]{2,1,0:T(8,128)S(1)}, u32[]{:S(2)}, u32[]{:S(2)}) collective-permute-start(f32[144,8,384]{2,1,0:T(8,128)} %get-tuple-element.289), channel_id=1, source_target_pairs={{0,16},{2,18},{4,20},{6,22},{8,24},{10,26},{12,28},{14,30},{16,0},... | collective-permute-start | bytes 5308424 | tf_op jit(solution)/shard_map/ppermute | solution.py:475
  571.2 29.9 %collective-permute-start.51 = (f32[4,4,2,3,8,384]{5,4,3,2,1,0:T(8,128)}, f32[4,4,2,3,8,384]{5,4,3,2,1,0:T(8,128)S(1)}, u32[]{:S(2)}, u32[]{:S(2)}) collective-permute-start(f32[4,4,2,3,8,384]{5,4,3,2,1,0:T(8,128)} %get-tuple-element.301), channel_id=1, source_target_pairs={{0,4},{2,6},{4,0},{6,2},{8,12},{10,14},{12,8},{14,10},{16,20},{18,... | collective-permute-start | bytes 3538952 | tf_op jit(solution)/shard_map/ppermute | solution.py:475
  574.1 27.0 %collective-permute-start.52 = (f32[4,4,2,3,8,384]{5,4,3,2,1,0:T(8,128)}, f32[4,4,2,3,8,384]{5,4,3,2,1,0:T(8,128)S(1)}, u32[]{:S(2)}, u32[]{:S(2)}) collective-permute-start(f32[4,4,2,3,8,384]{5,4,3,2,1,0:T(8,128)} %get-tuple-element.302), channel_id=1, source_target_pairs={{0,6},{2,4},{4,2},{6,0},{8,14},{10,12},{12,10},{14,8},{16,22},{18,... | collective-permute-start | bytes 3538952 | tf_op jit(solution)/shard_map/ppermute | solution.py:475
  585.5 62.6 %collective-permute-start.42 = (f32[256,768]{1,0:T(8,128)}, f32[256,768]{1,0:T(8,128)}, u32[]{:S(2)}, u32[]{:S(2)}) collective-permute-start(f32[256,768]{1,0:T(8,128)} %get-tuple-element.281), channel_id=1, source_target_pairs={{0,1},{1,0},{2,3},{3,2},{4,5},{5,4},{6,7},{7,6},{8,9},{9,8},{10,11... | collective-permute-start | bytes 2359304 | tf_op jit(solution)/shard_map/ppermute | solution.py:528
  601.1 40.7 %collective-permute-start.20 = (f32[160,768]{1,0:T(8,128)}, f32[160,768]{1,0:T(8,128)}, u32[]{:S(2)}, u32[]{:S(2)}) collective-permute-start(f32[160,768]{1,0:T(8,128)} %get-tuple-element.229), channel_id=1, source_target_pairs={{0,1},{1,0},{2,3},{3,2},{4,5},{5,4},{6,7},{7,6},{8,9},{9,8},{10,11... | collective-permute-start | bytes 1474568 | tf_op jit(solution)/shard_map/ppermute | solution.py:528
  601.1 47.1 %collective-permute-start.31 = (f32[160,768]{1,0:T(8,128)}, f32[160,768]{1,0:T(8,128)}, u32[]{:S(2)}, u32[]{:S(2)}) collective-permute-start(f32[160,768]{1,0:T(8,128)} %get-tuple-element.255), channel_id=1, source_target_pairs={{0,1},{1,0},{2,3},{3,2},{4,5},{5,4},{6,7},{7,6},{8,9},{9,8},{10,11... | collective-permute-start | bytes 1474568 | tf_op jit(solution)/shard_map/ppermute | solution.py:528
  620.6 98.4 %collective-permute-start.62 = (f32[168,8,384]{2,1,0:T(8,128)}, f32[168,8,384]{2,1,0:T(8,128)}, u32[]{:S(2)}, u32[]{:S(2)}) collective-permute-start(f32[168,8,384]{2,1,0:T(8,128)} %get-tuple-element.318), channel_id=1, source_target_pairs={{0,8},{2,10},{4,12},{6,14},{8,0},{10,2},{12,4},{14,6},{16,24},{18,... | collective-permute-start | bytes 6193160 | tf_op jit(solution)/shard_map/ppermute | solution.py:475
  641.3 77.7 %collective-permute-start.61 = (f32[144,8,384]{2,1,0:T(8,128)}, f32[144,8,384]{2,1,0:T(8,128)S(1)}, u32[]{:S(2)}, u32[]{:S(2)}) collective-permute-start(f32[144,8,384]{2,1,0:T(8,128)} %get-tuple-element.317), channel_id=1, source_target_pairs={{0,16},{2,18},{4,20},{6,22},{8,24},{10,26},{12,28},{14,30},{16,0},... | collective-permute-start | bytes 5308424 | tf_op jit(solution)/shard_map/ppermute | solution.py:475
  648.2 29.0 %collective-permute-start.54 = (f32[4,4,1,3,8,384]{5,4,3,2,1,0:T(8,128)}, f32[4,4,1,3,8,384]{5,4,3,2,1,0:T(8,128)S(1)}, u32[]{:S(2)}, u32[]{:S(2)}) collective-permute-start(f32[4,4,1,3,8,384]{5,4,3,2,1,0:T(8,128)} %get-tuple-element.306), channel_id=1, source_target_pairs={{0,4},{2,6},{4,0},{6,2},{8,12},{10,14},{12,8},{14,10},{16,20},{18,... | collective-permute-start | bytes 1769480 | tf_op jit(solution)/shard_map/ppermute | solution.py:475
  648.2 29.9 %collective-permute-start.55 = (f32[4,4,1,3,8,384]{5,4,3,2,1,0:T(8,128)}, f32[4,4,1,3,8,384]{5,4,3,2,1,0:T(8,128)S(1)}, u32[]{:S(2)}, u32[]{:S(2)}) collective-permute-start(f32[4,4,1,3,8,384]{5,4,3,2,1,0:T(8,128)} %get-tuple-element.307), channel_id=1, source_target_pairs={{0,6},{2,4},{4,2},{6,0},{8,14},{10,12},{12,10},{14,8},{16,22},{18,... | collective-permute-start | bytes 1769480 | tf_op jit(solution)/shard_map/ppermute | solution.py:475
  662.6 28.5 %collective-permute-start.43 = (f32[4,64,768]{2,1,0:T(8,128)}, f32[4,64,768]{2,1,0:T(8,128)S(1)}, u32[]{:S(2)}, u32[]{:S(2)}) collective-permute-start(f32[4,64,768]{2,1,0:T(8,128)} %get-tuple-element.283), channel_id=1, source_target_pairs={{0,2},{2,0},{4,6},{6,4},{8,10},{10,8},{12,14},{14,12},{16,18},{18,... | collective-permute-start | bytes 2359304 | tf_op jit(solution)/shard_map/ppermute | solution.py:475
  691.2 48.7 %collective-permute-start.57 = (f32[96,8,384]{2,1,0:T(8,128)}, f32[96,8,384]{2,1,0:T(8,128)S(1)}, u32[]{:S(2)}, u32[]{:S(2)}) collective-permute-start(f32[96,8,384]{2,1,0:T(8,128)} %get-tuple-element.312), channel_id=1, source_target_pairs={{0,8},{2,10},{4,12},{6,14},{8,0},{10,2},{12,4},{14,6},{16,24},{18,... | collective-permute-start | bytes 3538952 | tf_op jit(solution)/shard_map/ppermute | solution.py:475
  725.2 102.2 %collective-permute-start.63 = (f32[144,8,384]{2,1,0:T(8,128)}, f32[144,8,384]{2,1,0:T(8,128)S(1)}, u32[]{:S(2)}, u32[]{:S(2)}) collective-permute-start(f32[144,8,384]{2,1,0:T(8,128)} %get-tuple-element.320), channel_id=1, source_target_pairs={{0,16},{2,18},{4,20},{6,22},{8,24},{10,26},{12,28},{14,30},{16,0},... | collective-permute-start | bytes 5308424 | tf_op jit(solution)/shard_map/ppermute | solution.py:475
  725.5 29.0 %collective-permute-start.64 = (f32[4,4,1,3,8,384]{5,4,3,2,1,0:T(8,128)}, f32[4,4,1,3,8,384]{5,4,3,2,1,0:T(8,128)S(1)}, u32[]{:S(2)}, u32[]{:S(2)}) collective-permute-start(f32[4,4,1,3,8,384]{5,4,3,2,1,0:T(8,128)} %get-tuple-element.325), channel_id=1, source_target_pairs={{0,2},{2,0},{4,6},{6,4},{8,10},{10,8},{12,14},{14,12},{16,18},{18,... | collective-permute-start | bytes 1769480 | tf_op jit(solution)/shard_map/ppermute | solution.py:475
  763.4 85.7 %collective-permute-start.68 = (f32[96,8,384]{2,1,0:T(8,128)}, f32[96,8,384]{2,1,0:T(8,128)S(1)}, u32[]{:S(2)}, u32[]{:S(2)}) collective-permute-start(f32[96,8,384]{2,1,0:T(8,128)} %get-tuple-element.333), channel_id=1, source_target_pairs={{0,8},{2,10},{4,12},{6,14},{8,0},{10,2},{12,4},{14,6},{16,24},{18,... | collective-permute-start | bytes 3538952 | tf_op jit(solution)/shard_map/ppermute | solution.py:475
  766.7 95.1 %collective-permute-start.75 = (f32[84,8,384]{2,1,0:T(8,128)}, f32[84,8,384]{2,1,0:T(8,128)S(1)}, u32[]{:S(2)}, u32[]{:S(2)}) collective-permute-start(f32[84,8,384]{2,1,0:T(8,128)} %get-tuple-element.339), channel_id=1, source_target_pairs={{0,16},{2,18},{4,20},{6,22},{8,24},{10,26},{12,28},{14,30},{16,0},... | collective-permute-start | bytes 3096584 | tf_op jit(solution)/shard_map/ppermute | solution.py:475
  866.2 45.9 %collective-permute-start.76 = (f32[84,8,384]{2,1,0:T(8,128)}, f32[84,8,384]{2,1,0:T(8,128)S(1)}, u32[]{:S(2)}, u32[]{:S(2)}) collective-permute-start(f32[84,8,384]{2,1,0:T(8,128)} %get-tuple-element.340), channel_id=1, source_target_pairs={{0,16},{2,18},{4,20},{6,22},{8,24},{10,26},{12,28},{14,30},{16,0},... | collective-permute-start | bytes 3096584 | tf_op jit(solution)/shard_map/ppermute | solution.py:475
  924.6 29.8 %collective-permute-start.73 = (f32[128,768]{1,0:T(8,128)S(1)}, f32[128,768]{1,0:T(8,128)S(1)}, u32[]{:S(2)}, u32[]{:S(2)}) collective-permute-start(f32[128,768]{1,0:T(8,128)S(1)} %copy-done.18), channel_id=1, source_target_pairs={{0,16},{2,18},{4,20},{6,22},{8,24},{10,26},{12,28},{14,30},{16,0},... | collective-permute-start | bytes 1179656 | tf_op jit(solution)/shard_map/ppermute | solution.py:475
  (110 other events, 1035.9 us)

commit v3 on v2

--- a/solution.py
+++ b/solution.py
@@ -500,7 +500,7 @@
     def first_half(at):
         own, *others = coming
         if kepts:
-            others = hold(others, last(tokens) + last(kepts))
+            others = hold(others, last(tokens, 2 if at in (3, 4) else 1) + last(kepts))
         ys = [own] + [exchange(x, m) for m, x in enumerate(others, 1)]
         upcoming = packed(at + 1) if at + 1 < count else []
         kept, near, far = orient(where, ys, sizes_of(at), list(upcoming[:1]))
@@ -513,7 +513,7 @@
         (r, s), span, ends = chunks[at]
         sizes = sizes_of(at)
         parts.append((sizes, (kepts[at], nears[at][0], fars[at])))
-        if not ends and (r, s) != CLASSES[-1]:
+        if not ends and (r, s) not in CLASSES[-2:]:
             return
         begin = span[1] - sum(part.deep for part, _ in parts)
         after = ready + after

time: 981 us -> 975 us (level); the launches traced: 977 us -> 960 us
  starting transfers between devices: 117 us -> 99.6 us
    ppermute x78, starting transfers between devices: 116 us -> 99 us  [exchange(): return lax.ppermute(x, 'occ', [(n, n ^ bits) for n in range(OWNERS)])]
    pallas_call x7 -> x8, Pallas kernels: 117 us -> 123 us  [multiply(): pl.pallas_call(kernel, out_shape=[jax.ShapeDtypeStruct((rows, columns //...]
    unnamed x148 -> x146, local copies, waits for them, and re-layouts: 30 us -> 30 us
  transfers between devices with their start and end apart: 84 -> 84, of which waited for: 43 -> 39; matrix products, arithmetic and copies ran while one was open for 1% -> 1% of each run, Pallas kernels for 37% -> 38%
where the time goes in v3:
time: 975 us; the launch traced here: 960 us
  waiting for transfers between devices  426 us (44%)
  Pallas kernels  395 us (41%)
  starting transfers between devices  99.6 us (10%)
  local copies, waits for them, and re-layouts  31.3 us (3%)
    ppermute x78, waiting for transfers between devices, exchange(): return lax.ppermute(x, 'occ', [(n, n ^ bits) for n in range(OWNERS)])  423 us
    pallas_call x8, Pallas kernels, multiply(): pl.pallas_call(kernel, out_shape=[jax.ShapeDtypeStruct((rows, columns //...  123 us
    pallas_call x12, Pallas kernels, pack(): pl.pallas_call(pack_kernel, out_shape=[jax.ShapeDtypeStruct(shape, jnp.fl...  123 us
    ppermute x78, starting transfers between devices, exchange(): return lax.ppermute(x, 'occ', [(n, n ^ bits) for n in range(OWNERS)])  99 us
    pallas_call x12, Pallas kernels, orient(): pl.pallas_call(kernel, out_shape=[jax.ShapeDtypeStruct((n, SUB, lanes), j...  70.9 us
    pallas_call x12, Pallas kernels, merge(): pl.pallas_call(kernel, out_shape=[jax.ShapeDtypeStruct(far.shape, jnp.flo...  49.2 us
    unnamed x146, local copies, waits for them, and re-layouts  30 us
    pallas_call x4, Pallas kernels, spread(): pl.pallas_call(kernel, out_shape=[jax.ShapeDtypeStruct((PLANES, rows, col...  25.1 us
  transfers between devices with their start and end apart: 84, of which 39 were waited for; matrix products, arithmetic and copies ran while one was open for 1% of the time, Pallas kernels for 38%

profile of v3, /device:TPU:0, one launch (start us, length us, event | category | flops | bytes accessed | tf_op | source)
XLA Modules:
  0.0 960.4 jit_solution(6161124144203110950)
XLA Ops:
  0.7 7.7 pack.12
  12.8 7.7 pack.13
  25.6 13.3 %collective-permute-done.1.refs_3_ = f32[4,4,1,3,8,384]{5,4,3,2,1,0:T(8,128)S(1)} collective-permute-done((f32[4,4,1,3,8,384]{5,4,3,2,1,0:T(8,128)}, f32[4,4,1,3,8,384]{5,4,3,2,1,0:T(8,128)S(1)}, u32[]{:S(2)}, u32[]{:S(2)}) %collective-permute-start.1) | collective-permute-done | bytes 589856 | tf_op jit(solution)/shard_map/ppermute | solution.py:475
  50.3 7.7 pack.14
  63.3 11.0 %collective-permute-done.6.refs_3_ = f32[4,4,1,3,8,384]{5,4,3,2,1,0:T(8,128)S(1)} collective-permute-done((f32[4,4,1,3,8,384]{5,4,3,2,1,0:T(8,128)}, f32[4,4,1,3,8,384]{5,4,3,2,1,0:T(8,128)S(1)}, u32[]{:S(2)}, u32[]{:S(2)}) %collective-permute-start.6) | collective-permute-done | bytes 589856 | tf_op jit(solution)/shard_map/ppermute | solution.py:475
  91.5 7.7 pack.15
  104.5 8.4 collective-permute-done.11.refs_3_
  133.9 12.7 %pack.16 = (f32[4,4,2,3,8,384]{5,4,3,2,1,0:T(8,128)}, f32[4,4,2,3,8,384]{5,4,3,2,1,0:T(8,128)}, f32[4,4,2,3,8,384]{5,4,3,2,1,0:T(8,128)}, f32[4,4,2,3,8,384]{5,4,3,2,1,0:T(8,128)}) custom-call(s32[2]{0:T(128)} %pad_add_fusion.where_ref.refs_0_, f32[3,16,3,192,384]{4,3,2,1,0:T(8,128)} %bitcast.64, f32[3,16,3,192,384]{4,3,2,1,0:T(8,128)} %bitcast.65, ...), custom_call_target="tpu_custom_call" | custom-call | tf_op jit(solution)/shard_map/pack/pallas_call | solution.py:80
  156.5 18.6 %collective-permute-done.20.arrived_ref.refs_2_ = f32[96,8,384]{2,1,0:T(8,128)S(1)} collective-permute-done((f32[96,8,384]{2,1,0:T(8,128)S(1)}, f32[96,8,384]{2,1,0:T(8,128)S(1)}, u32[]{:S(2)}, u32[]{:S(2)}) %collective-permute-start.20) | collective-permute-done | bytes 1179680 | tf_op jit(solution)/shard_map/ppermute | solution.py:475
  181.0 12.8 %pack.17 = (f32[4,4,2,3,8,384]{5,4,3,2,1,0:T(8,128)}, f32[4,4,2,3,8,384]{5,4,3,2,1,0:T(8,128)}, f32[4,4,2,3,8,384]{5,4,3,2,1,0:T(8,128)}, f32[4,4,2,3,8,384]{5,4,3,2,1,0:T(8,128)}) custom-call(s32[2]{0:T(128)} %pad_add_fusion.where_ref.refs_0_, f32[3,16,3,192,384]{4,3,2,1,0:T(8,128)} %bitcast.69, f32[3,16,3,192,384]{4,3,2,1,0:T(8,128)} %bitcast.68, ...), custom_call_target="tpu_custom_call" | custom-call | tf_op jit(solution)/shard_map/pack/pallas_call | solution.py:80
  193.8 8.1 collective-permute-done.17.refs_3_
  214.7 10.5 %collective-permute-done.22.arrived_ref.refs_5_ = f32[96,8,384]{2,1,0:T(8,128)S(1)} collective-permute-done((f32[96,8,384]{2,1,0:T(8,128)}, f32[96,8,384]{2,1,0:T(8,128)S(1)}, u32[]{:S(2)}, u32[]{:S(2)}) %collective-permute-start.22) | collective-permute-done | bytes 1179680 | tf_op jit(solution)/shard_map/ppermute | solution.py:475
  235.1 12.8 %pack.18 = (f32[4,4,2,3,8,384]{5,4,3,2,1,0:T(8,128)}, f32[4,4,2,3,8,384]{5,4,3,2,1,0:T(8,128)}, f32[4,4,2,3,8,384]{5,4,3,2,1,0:T(8,128)}, f32[4,4,2,3,8,384]{5,4,3,2,1,0:T(8,128)}) custom-call(s32[2]{0:T(128)} %pad_add_fusion.where_ref.refs_0_, f32[3,16,3,192,384]{4,3,2,1,0:T(8,128)} %bitcast.70, f32[3,16,3,192,384]{4,3,2,1,0:T(8,128)} %bitcast.71, ...), custom_call_target="tpu_custom_call" | custom-call | tf_op jit(solution)/shard_map/pack/pallas_call | solution.py:80
  247.8 11.1 %collective-permute-done.25.refs_2_ = f32[4,4,2,3,8,384]{5,4,3,2,1,0:T(8,128)S(1)} collective-permute-done((f32[4,4,2,3,8,384]{5,4,3,2,1,0:T(8,128)}, f32[4,4,2,3,8,384]{5,4,3,2,1,0:T(8,128)S(1)}, u32[]{:S(2)}, u32[]{:S(2)}) %collective-permute-start.25) | collective-permute-done | bytes 1179680 | tf_op jit(solution)/shard_map/ppermute | solution.py:475
  259.0 17.6 %collective-permute-done.26.refs_3_ = f32[4,4,2,3,8,384]{5,4,3,2,1,0:T(8,128)S(1)} collective-permute-done((f32[4,4,2,3,8,384]{5,4,3,2,1,0:T(8,128)}, f32[4,4,2,3,8,384]{5,4,3,2,1,0:T(8,128)S(1)}, u32[]{:S(2)}, u32[]{:S(2)}) %collective-permute-start.26) | collective-permute-done | bytes 1179680 | tf_op jit(solution)/shard_map/ppermute | solution.py:475
  288.8 16.7 %multiply.8 = (f32[160,768]{1,0:T(8,128)}, f32[160,768]{1,0:T(8,128)}) custom-call(s32[11]{0:T(128)} %stack.58.refs_0_, f32[48,8,384]{2,1,0:T(8,128)} %get-tuple-element.185.refs_3_.refs_1_, f32[96,8,384]{2,1,0:T(8,128)} %copy-done.10, f32[84,8,384]{2,1,0:T(8,128)} %collective-permute-done.4.rest_0_.refs_3_, ...), custom_call_target="tpu_custom_call" | custom-call | tf_op jit(solution)/shard_map/multiply/pallas_call | solution.py:364
  316.1 12.8 %pack.19 = (f32[4,4,2,3,8,384]{5,4,3,2,1,0:T(8,128)}, f32[4,4,2,3,8,384]{5,4,3,2,1,0:T(8,128)}, f32[4,4,2,3,8,384]{5,4,3,2,1,0:T(8,128)}, f32[4,4,2,3,8,384]{5,4,3,2,1,0:T(8,128)}) custom-call(s32[2]{0:T(128)} %pad_add_fusion.where_ref.refs_0_, f32[3,16,3,192,384]{4,3,2,1,0:T(8,128)} %bitcast.73, f32[3,16,3,192,384]{4,3,2,1,0:T(8,128)} %bitcast.74, ...), custom_call_target="tpu_custom_call" | custom-call | tf_op jit(solution)/shard_map/pack/pallas_call | solution.py:80
  328.8 12.9 %collective-permute-done.28.refs_2_ = f32[4,4,2,3,8,384]{5,4,3,2,1,0:T(8,128)S(1)} collective-permute-done((f32[4,4,2,3,8,384]{5,4,3,2,1,0:T(8,128)}, f32[4,4,2,3,8,384]{5,4,3,2,1,0:T(8,128)S(1)}, u32[]{:S(2)}, u32[]{:S(2)}) %collective-permute-start.28) | collective-permute-done | bytes 1179680 | tf_op jit(solution)/shard_map/ppermute | solution.py:475
  341.7 16.9 %collective-permute-done.29.refs_3_ = f32[4,4,2,3,8,384]{5,4,3,2,1,0:T(8,128)S(1)} collective-permute-done((f32[4,4,2,3,8,384]{5,4,3,2,1,0:T(8,128)}, f32[4,4,2,3,8,384]{5,4,3,2,1,0:T(8,128)S(1)}, u32[]{:S(2)}, u32[]{:S(2)}) %collective-permute-start.29) | collective-permute-done | bytes 1179680 | tf_op jit(solution)/shard_map/ppermute | solution.py:475
  367.0 16.5 %multiply.9 = (f32[160,768]{1,0:T(8,128)}, f32[160,768]{1,0:T(8,128)}) custom-call(s32[11]{0:T(128)} %stack.58.refs_0_, f32[48,8,384]{2,1,0:T(8,128)} %get-tuple-element.208.refs_3_.refs_4_.refs_1_, f32[96,8,384]{2,1,0:T(8,128)} %copy-done.8, f32[84,8,384]{2,1,0:T(8,128)} %copy-done.11, f32[48,8,384]{2,1,0:T(8,128)} %get-tuple-element.220.refs_4_.refs_3_, ...), custom_call_target="tpu_custom_call" | custom-call | tf_op jit(solution)/shard_map/multiply/pallas_call | solution.py:364
  394.6 12.7 %pack.20 = (f32[4,4,2,3,8,384]{5,4,3,2,1,0:T(8,128)}, f32[4,4,2,3,8,384]{5,4,3,2,1,0:T(8,128)}, f32[4,4,2,3,8,384]{5,4,3,2,1,0:T(8,128)}, f32[4,4,2,3,8,384]{5,4,3,2,1,0:T(8,128)}) custom-call(s32[2]{0:T(128)} %pad_add_fusion.where_ref.refs_0_, f32[3,16,3,192,384]{4,3,2,1,0:T(8,128)} %bitcast.76, f32[3,16,3,192,384]{4,3,2,1,0:T(8,128)} %bitcast.77, ...), custom_call_target="tpu_custom_call" | custom-call | tf_op jit(solution)/shard_map/pack/pallas_call | solution.py:80
  407.4 12.9 %collective-permute-done.36.refs_2_ = f32[4,4,2,3,8,384]{5,4,3,2,1,0:T(8,128)S(1)} collective-permute-done((f32[4,4,2,3,8,384]{5,4,3,2,1,0:T(8,128)}, f32[4,4,2,3,8,384]{5,4,3,2,1,0:T(8,128)S(1)}, u32[]{:S(2)}, u32[]{:S(2)}) %collective-permute-start.36) | collective-permute-done | bytes 1179680 | tf_op jit(solution)/shard_map/ppermute | solution.py:475
  420.3 14.6 %collective-permute-done.37.refs_3_ = f32[4,4,2,3,8,384]{5,4,3,2,1,0:T(8,128)S(1)} collective-permute-done((f32[4,4,2,3,8,384]{5,4,3,2,1,0:T(8,128)}, f32[4,4,2,3,8,384]{5,4,3,2,1,0:T(8,128)S(1)}, u32[]{:S(2)}, u32[]{:S(2)}) %collective-permute-start.37) | collective-permute-done | bytes 1179680 | tf_op jit(solution)/shard_map/ppermute | solution.py:475
  444.1 38.5 %collective-permute-done.35.arrived_ref.refs_2_ = f32[168,8,384]{2,1,0:T(8,128)S(1)} collective-permute-done((f32[168,8,384]{2,1,0:T(8,128)}, f32[168,8,384]{2,1,0:T(8,128)S(1)}, u32[]{:S(2)}, u32[]{:S(2)}) %collective-permute-start.35) | collective-permute-done | bytes 2064416 | tf_op jit(solution)/shard_map/ppermute | solution.py:475
  492.4 12.7 %pack.21 = (f32[4,4,2,3,8,384]{5,4,3,2,1,0:T(8,128)}, f32[4,4,2,3,8,384]{5,4,3,2,1,0:T(8,128)}, f32[4,4,2,3,8,384]{5,4,3,2,1,0:T(8,128)}, f32[4,4,2,3,8,384]{5,4,3,2,1,0:T(8,128)}) custom-call(s32[2]{0:T(128)} %pad_add_fusion.where_ref.refs_0_, f32[3,16,3,192,384]{4,3,2,1,0:T(8,128)} %bitcast.79, f32[3,16,3,192,384]{4,3,2,1,0:T(8,128)} %bitcast.80, ...), custom_call_target="tpu_custom_call" | custom-call | tf_op jit(solution)/shard_map/pack/pallas_call | solution.py:80
  505.3 13.4 %collective-permute-done.40.refs_3_ = f32[4,4,2,3,8,384]{5,4,3,2,1,0:T(8,128)S(1)} collective-permute-done((f32[4,4,2,3,8,384]{5,4,3,2,1,0:T(8,128)}, f32[4,4,2,3,8,384]{5,4,3,2,1,0:T(8,128)S(1)}, u32[]{:S(2)}, u32[]{:S(2)}) %collective-permute-start.40) | collective-permute-done | bytes 1179680 | tf_op jit(solution)/shard_map/ppermute | solution.py:475
  528.4 20.4 %multiply.10 = (f32[256,768]{1,0:T(8,128)}, f32[256,768]{1,0:T(8,128)}) custom-call(s32[11]{0:T(128)} %stack.65.refs_0_, f32[84,8,384]{2,1,0:T(8,128)} %get-tuple-element.225.refs_8_.refs_3_.refs_4_.refs_1_, f32[168,8,384]{2,1,0:T(8,128)} %copy-done.4, f32[144,8,384]{2,1,0:T(8,128)} %collective-permute-done.32.rest_0_.refs_3_, ...), custom_call_target="tpu_custom_call" | custom-call | tf_op jit(solution)/shard_map/multiply/pallas_call | solution.py:364
  548.7 13.4 %collective-permute-done.46.rest_0_.refs_3_ = f32[144,8,384]{2,1,0:T(8,128)} collective-permute-done((f32[144,8,384]{2,1,0:T(8,128)}, f32[144,8,384]{2,1,0:T(8,128)}, u32[]{:S(2)}, u32[]{:S(2)}) %collective-permute-start.46) | collective-permute-done | bytes 1769504 | tf_op jit(solution)/shard_map/ppermute | solution.py:475
  570.6 12.9 %collective-permute-done.50.refs_2_ = f32[4,4,2,3,8,384]{5,4,3,2,1,0:T(8,128)S(1)} collective-permute-done((f32[4,4,2,3,8,384]{5,4,3,2,1,0:T(8,128)}, f32[4,4,2,3,8,384]{5,4,3,2,1,0:T(8,128)S(1)}, u32[]{:S(2)}, u32[]{:S(2)}) %collective-permute-start.50) | collective-permute-done | bytes 1179680 | tf_op jit(solution)/shard_map/ppermute | solution.py:475
  583.5 13.1 %collective-permute-done.51.refs_3_ = f32[4,4,2,3,8,384]{5,4,3,2,1,0:T(8,128)S(1)} collective-permute-done((f32[4,4,2,3,8,384]{5,4,3,2,1,0:T(8,128)}, f32[4,4,2,3,8,384]{5,4,3,2,1,0:T(8,128)S(1)}, u32[]{:S(2)}, u32[]{:S(2)}) %collective-permute-start.51) | collective-permute-done | bytes 1179680 | tf_op jit(solution)/shard_map/ppermute | solution.py:475
  597.1 7.7 pack.22
  604.8 6.7 orient.21
  612.3 23.6 %collective-permute-done.48.rest_0_.refs_6_ = f32[144,8,384]{2,1,0:T(8,128)S(1)} collective-permute-done((f32[144,8,384]{2,1,0:T(8,128)}, f32[144,8,384]{2,1,0:T(8,128)S(1)}, u32[]{:S(2)}, u32[]{:S(2)}) %collective-permute-start.48) | collective-permute-done | bytes 1769504 | tf_op jit(solution)/shard_map/ppermute | solution.py:475
  645.6 9.5 spread.4
  660.2 10.2 %collective-permute-done.54.refs_3_ = f32[4,4,1,3,8,384]{5,4,3,2,1,0:T(8,128)S(1)} collective-permute-done((f32[4,4,1,3,8,384]{5,4,3,2,1,0:T(8,128)}, f32[4,4,1,3,8,384]{5,4,3,2,1,0:T(8,128)S(1)}, u32[]{:S(2)}, u32[]{:S(2)}) %collective-permute-start.54) | collective-permute-done | bytes 589856 | tf_op jit(solution)/shard_map/ppermute | solution.py:475
  672.3 7.7 pack.23
  691.9 20.3 %multiply.11 = (f32[256,768]{1,0:T(8,128)}, f32[256,768]{1,0:T(8,128)}) custom-call(s32[11]{0:T(128)} %stack.65.refs_0_, f32[84,8,384]{2,1,0:T(8,128)} %get-tuple-element.253.refs_8_.rest_1_.refs_3_.refs_4_.refs_1_, f32[168,8,384]{2,1,0:T(8,128)} %copy-done.5, f32[144,8,384]{2,1,0:T(8,128)} %collective-permute-done.46.rest_0_.refs_3_, ...), custom_call_target="tpu_custom_call" | custom-call | tf_op jit(solution)/shard_map/multiply/pallas_call | solution.py:364
  722.4 13.6 %collective-permute-done.57.refs_2_.arrived_ref = f32[96,8,384]{2,1,0:T(8,128)S(1)} collective-permute-done((f32[96,8,384]{2,1,0:T(8,128)}, f32[96,8,384]{2,1,0:T(8,128)S(1)}, u32[]{:S(2)}, u32[]{:S(2)}) %collective-permute-start.57) | collective-permute-done | bytes 1179680 | tf_op jit(solution)/shard_map/ppermute | solution.py:475
  765.3 13.2 %multiply.12 = (f32[256,768]{1,0:T(8,128)}, f32[256,768]{1,0:T(8,128)}) custom-call(s32[11]{0:T(128)} %stack.65.refs_0_, f32[84,8,384]{2,1,0:T(8,128)} %get-tuple-element.279.refs_8_.refs_6_.rest_1_.refs_3_.refs_4_.refs_1_, f32[168,8,384]{2,1,0:T(8,128)} %copy-done.3, f32[144,8,384]{2,1,0:T(8,128)} %copy-done.1, f32[192,24,1536]{2,1,0:T(8,128)} %refs_4_.7, ...), custom_call_target="tpu_custom_call" | custom-call | tf_op jit(solution)/shard_map/multiply/pallas_call | solution.py:364
  778.4 42.6 %collective-permute-done.63.refs_3_ = f32[144,8,384]{2,1,0:T(8,128)S(1)} collective-permute-done((f32[144,8,384]{2,1,0:T(8,128)}, f32[144,8,384]{2,1,0:T(8,128)S(1)}, u32[]{:S(2)}, u32[]{:S(2)}) %collective-permute-start.63) | collective-permute-done | bytes 1769504 | tf_op jit(solution)/shard_map/ppermute | solution.py:475
  822.2 13.5 %multiply.13 = (f32[256,768]{1,0:T(8,128)}, f32[256,768]{1,0:T(8,128)}) custom-call(s32[11]{0:T(128)} %stack.65.refs_0_, f32[84,8,384]{2,1,0:T(8,128)} %get-tuple-element.303.rest_1_.refs_4_.refs_3_.refs_1_, f32[168,8,384]{2,1,0:T(8,128)} %collective-permute-done.61.arrived_ref.refs_2_, f32[144,8,384]{2,1,0:T(8,128)} %copy-done.15, ...), custom_call_target="tpu_custom_call" | custom-call | tf_op jit(solution)/shard_map/multiply/pallas_call | solution.py:364
  857.1 7.8 collective-permute-done.70
  865.7 11.2 %multiply.14 = (f32[160,768]{1,0:T(8,128)}, f32[160,768]{1,0:T(8,128)}) custom-call(s32[11]{0:T(128)} %stack.58.refs_0_, f32[48,8,384]{2,1,0:T(8,128)} %get-tuple-element.309.refs_9_.rest_1_.refs_4_.refs_1_, f32[96,8,384]{2,1,0:T(8,128)} %copy-done.2, f32[84,8,384]{2,1,0:T(8,128)} %copy-done.13, f32[192,24,1536]{2,1,0:T(8,128)} %refs_4_.7, ...), custom_call_target="tpu_custom_call" | custom-call | tf_op jit(solution)/shard_map/multiply/pallas_call | solution.py:364
  880.0 14.7 %collective-permute-done.76.refs_3_ = f32[84,8,384]{2,1,0:T(8,128)S(1)} collective-permute-done((f32[84,8,384]{2,1,0:T(8,128)}, f32[84,8,384]{2,1,0:T(8,128)S(1)}, u32[]{:S(2)}, u32[]{:S(2)}) %collective-permute-start.76) | collective-permute-done | bytes 1032224 | tf_op jit(solution)/shard_map/ppermute | solution.py:475
  895.8 11.4 %multiply.15 = (f32[160,768]{1,0:T(8,128)}, f32[160,768]{1,0:T(8,128)}) custom-call(s32[11]{0:T(128)} %stack.58.refs_0_, f32[48,8,384]{2,1,0:T(8,128)} %get-tuple-element.328.refs_6_.rest_1_.refs_8_.refs_1_, f32[96,8,384]{2,1,0:T(8,128)} %copy-done, f32[84,8,384]{2,1,0:T(8,128)} %copy-done.42, f32[192,24,1536]{2,1,0:T(8,128)} %refs_4_.7, ...), custom_call_target="tpu_custom_call" | custom-call | tf_op jit(solution)/shard_map/multiply/pallas_call | solution.py:364
  918.5 8.3 collective-permute-done.72.refs_4_.refs_1_
  928.2 9.0 collective-permute-done.73.refs_5_.refs_2_
  942.5 8.5 collective-permute-start.82
  (338 shorter events, 312.2 us)
Async XLA Ops:
  11.3 27.6 %collective-permute-start.1 = (f32[4,4,1,3,8,384]{5,4,3,2,1,0:T(8,128)}, f32[4,4,1,3,8,384]{5,4,3,2,1,0:T(8,128)S(1)}, u32[]{:S(2)}, u32[]{:S(2)}) collective-permute-start(f32[4,4,1,3,8,384]{5,4,3,2,1,0:T(8,128)} %get-tuple-element.182), channel_id=1, source_target_pairs={{0,4},{2,6},{4,0},{6,2},{8,12},{10,14},{12,8},{14,10},{16,20},{18,... | collective-permute-start | bytes 1769480 | tf_op jit(solution)/shard_map/ppermute | solution.py:475
  45.2 35.7 %collective-permute-start.3 = (f32[96,8,384]{2,1,0:T(8,128)}, f32[96,8,384]{2,1,0:T(8,128)S(1)}, u32[]{:S(2)}, u32[]{:S(2)}) collective-permute-start(f32[96,8,384]{2,1,0:T(8,128)} %get-tuple-element.186), channel_id=1, source_target_pairs={{0,8},{2,10},{4,12},{6,14},{8,0},{10,2},{12,4},{14,6},{16,24},{18,... | collective-permute-start | bytes 3538952 | tf_op jit(solution)/shard_map/ppermute | solution.py:475
  80.5 48.6 %collective-permute-start.8 = (f32[96,8,384]{2,1,0:T(8,128)}, f32[96,8,384]{2,1,0:T(8,128)S(1)}, u32[]{:S(2)}, u32[]{:S(2)}) collective-permute-start(f32[96,8,384]{2,1,0:T(8,128)} %get-tuple-element.197), channel_id=1, source_target_pairs={{0,8},{2,10},{4,12},{6,14},{8,0},{10,2},{12,4},{14,6},{16,24},{18,... | collective-permute-start | bytes 3538952 | tf_op jit(solution)/shard_map/ppermute | solution.py:475
  85.2 43.8 %collective-permute-start.4 = (f32[84,8,384]{2,1,0:T(8,128)}, f32[84,8,384]{2,1,0:T(8,128)}, u32[]{:S(2)}, u32[]{:S(2)}) collective-permute-start(f32[84,8,384]{2,1,0:T(8,128)} %get-tuple-element.188), channel_id=1, source_target_pairs={{0,16},{2,18},{4,20},{6,22},{8,24},{10,26},{12,28},{14,30},{16,0},... | collective-permute-start | bytes 3096584 | tf_op jit(solution)/shard_map/ppermute | solution.py:475
  119.1 27.5 %collective-permute-start.13 = (f32[4,4,1,3,8,384]{5,4,3,2,1,0:T(8,128)}, f32[4,4,1,3,8,384]{5,4,3,2,1,0:T(8,128)S(1)}, u32[]{:S(2)}, u32[]{:S(2)}) collective-permute-start(f32[4,4,1,3,8,384]{5,4,3,2,1,0:T(8,128)} %get-tuple-element.217), channel_id=1, source_target_pairs={{0,2},{2,0},{4,6},{6,4},{8,10},{10,8},{12,14},{14,12},{16,18},{18,... | collective-permute-start | bytes 1769480 | tf_op jit(solution)/shard_map/ppermute | solution.py:475
  129.0 46.1 %collective-permute-start.20 = (f32[96,8,384]{2,1,0:T(8,128)S(1)}, f32[96,8,384]{2,1,0:T(8,128)S(1)}, u32[]{:S(2)}, u32[]{:S(2)}) collective-permute-start(f32[96,8,384]{2,1,0:T(8,128)S(1)} %copy-done.72), channel_id=1, source_target_pairs={{0,8},{2,10},{4,12},{6,14},{8,0},{10,2},{12,4},{14,6},{16,24},{18,... | collective-permute-start | bytes 3538952 | tf_op jit(solution)/shard_map/ppermute | solution.py:475
  133.3 41.8 %collective-permute-start.9 = (f32[84,8,384]{2,1,0:T(8,128)}, f32[84,8,384]{2,1,0:T(8,128)}, u32[]{:S(2)}, u32[]{:S(2)}) collective-permute-start(f32[84,8,384]{2,1,0:T(8,128)} %get-tuple-element.199), channel_id=1, source_target_pairs={{0,16},{2,18},{4,20},{6,22},{8,24},{10,26},{12,28},{14,30},{16,0},... | collective-permute-start | bytes 3096584 | tf_op jit(solution)/shard_map/ppermute | solution.py:475
  153.1 40.8 %collective-permute-start.16 = (f32[4,4,2,3,8,384]{5,4,3,2,1,0:T(8,128)}, f32[4,4,2,3,8,384]{5,4,3,2,1,0:T(8,128)S(1)}, u32[]{:S(2)}, u32[]{:S(2)}) collective-permute-start(f32[4,4,2,3,8,384]{5,4,3,2,1,0:T(8,128)} %get-tuple-element.221), channel_id=1, source_target_pairs={{0,2},{2,0},{4,6},{6,4},{8,10},{10,8},{12,14},{14,12},{16,18},{18,... | collective-permute-start | bytes 3538952 | tf_op jit(solution)/shard_map/ppermute | solution.py:475
  153.6 48.4 %collective-permute-start.17 = (f32[4,4,2,3,8,384]{5,4,3,2,1,0:T(8,128)}, f32[4,4,2,3,8,384]{5,4,3,2,1,0:T(8,128)S(1)}, u32[]{:S(2)}, u32[]{:S(2)}) collective-permute-start(f32[4,4,2,3,8,384]{5,4,3,2,1,0:T(8,128)} %get-tuple-element.222), channel_id=1, source_target_pairs={{0,4},{2,6},{4,0},{6,2},{8,12},{10,14},{12,8},{14,10},{16,20},{18,... | collective-permute-start | bytes 3538952 | tf_op jit(solution)/shard_map/ppermute | solution.py:475
  154.7 47.2 %collective-permute-start.18 = (f32[4,4,2,3,8,384]{5,4,3,2,1,0:T(8,128)}, f32[4,4,2,3,8,384]{5,4,3,2,1,0:T(8,128)S(1)}, u32[]{:S(2)}, u32[]{:S(2)}) collective-permute-start(f32[4,4,2,3,8,384]{5,4,3,2,1,0:T(8,128)} %get-tuple-element.223), channel_id=1, source_target_pairs={{0,6},{2,4},{4,2},{6,0},{8,14},{10,12},{12,10},{14,8},{16,22},{18,... | collective-permute-start | bytes 3538952 | tf_op jit(solution)/shard_map/ppermute | solution.py:475
  175.1 50.1 %collective-permute-start.22 = (f32[96,8,384]{2,1,0:T(8,128)}, f32[96,8,384]{2,1,0:T(8,128)S(1)}, u32[]{:S(2)}, u32[]{:S(2)}) collective-permute-start(f32[96,8,384]{2,1,0:T(8,128)} %get-tuple-element.231), channel_id=1, source_target_pairs={{0,8},{2,10},{4,12},{6,14},{8,0},{10,2},{12,4},{14,6},{16,24},{18,... | collective-permute-start | bytes 3538952 | tf_op jit(solution)/shard_map/ppermute | solution.py:475
  179.4 45.8 %collective-permute-start.21 = (f32[84,8,384]{2,1,0:T(8,128)}, f32[84,8,384]{2,1,0:T(8,128)S(1)}, u32[]{:S(2)}, u32[]{:S(2)}) collective-permute-start(f32[84,8,384]{2,1,0:T(8,128)} %get-tuple-element.230), channel_id=1, source_target_pairs={{0,16},{2,18},{4,20},{6,22},{8,24},{10,26},{12,28},{14,30},{16,0},... | collective-permute-start | bytes 3096584 | tf_op jit(solution)/shard_map/ppermute | solution.py:475
  210.1 95.3 %collective-permute-start.24 = (f32[168,8,384]{2,1,0:T(8,128)}, f32[168,8,384]{2,1,0:T(8,128)S(1)}, u32[]{:S(2)}, u32[]{:S(2)}) collective-permute-start(f32[168,8,384]{2,1,0:T(8,128)} %get-tuple-element.239), channel_id=1, source_target_pairs={{0,8},{2,10},{4,12},{6,14},{8,0},{10,2},{12,4},{14,6},{16,24},{18,... | collective-permute-start | bytes 6193160 | tf_op jit(solution)/shard_map/ppermute | solution.py:475
  229.8 29.1 %collective-permute-start.25 = (f32[4,4,2,3,8,384]{5,4,3,2,1,0:T(8,128)}, f32[4,4,2,3,8,384]{5,4,3,2,1,0:T(8,128)S(1)}, u32[]{:S(2)}, u32[]{:S(2)}) collective-permute-start(f32[4,4,2,3,8,384]{5,4,3,2,1,0:T(8,128)} %get-tuple-element.244), channel_id=1, source_target_pairs={{0,2},{2,0},{4,6},{6,4},{8,10},{10,8},{12,14},{14,12},{16,18},{18,... | collective-permute-start | bytes 3538952 | tf_op jit(solution)/shard_map/ppermute | solution.py:475
  231.7 44.8 %collective-permute-start.26 = (f32[4,4,2,3,8,384]{5,4,3,2,1,0:T(8,128)}, f32[4,4,2,3,8,384]{5,4,3,2,1,0:T(8,128)S(1)}, u32[]{:S(2)}, u32[]{:S(2)}) collective-permute-start(f32[4,4,2,3,8,384]{5,4,3,2,1,0:T(8,128)} %get-tuple-element.245), channel_id=1, source_target_pairs={{0,4},{2,6},{4,0},{6,2},{8,12},{10,14},{12,8},{14,10},{16,20},{18,... | collective-permute-start | bytes 3538952 | tf_op jit(solution)/shard_map/ppermute | solution.py:475
  233.9 42.6 %collective-permute-start.27 = (f32[4,4,2,3,8,384]{5,4,3,2,1,0:T(8,128)}, f32[4,4,2,3,8,384]{5,4,3,2,1,0:T(8,128)S(1)}, u32[]{:S(2)}, u32[]{:S(2)}) collective-permute-start(f32[4,4,2,3,8,384]{5,4,3,2,1,0:T(8,128)} %get-tuple-element.246), channel_id=1, source_target_pairs={{0,6},{2,4},{4,2},{6,0},{8,14},{10,12},{12,10},{14,8},{16,22},{18,... | collective-permute-start | bytes 3538952 | tf_op jit(solution)/shard_map/ppermute | solution.py:475
  234.0 71.5 %collective-permute-start.23 = (f32[84,8,384]{2,1,0:T(8,128)}, f32[84,8,384]{2,1,0:T(8,128)S(1)}, u32[]{:S(2)}, u32[]{:S(2)}) collective-permute-start(f32[84,8,384]{2,1,0:T(8,128)} %get-tuple-element.233), channel_id=1, source_target_pairs={{0,16},{2,18},{4,20},{6,22},{8,24},{10,26},{12,28},{14,30},{16,0},... | collective-permute-start | bytes 3096584 | tf_op jit(solution)/shard_map/ppermute | solution.py:475
  284.5 99.7 %collective-permute-start.33 = (f32[168,8,384]{2,1,0:T(8,128)}, f32[168,8,384]{2,1,0:T(8,128)}, u32[]{:S(2)}, u32[]{:S(2)}) collective-permute-start(f32[168,8,384]{2,1,0:T(8,128)} %get-tuple-element.257), channel_id=1, source_target_pairs={{0,8},{2,10},{4,12},{6,14},{8,0},{10,2},{12,4},{14,6},{16,24},{18,... | collective-permute-start | bytes 6193160 | tf_op jit(solution)/shard_map/ppermute | solution.py:475
  312.0 72.2 %collective-permute-start.32 = (f32[144,8,384]{2,1,0:T(8,128)}, f32[144,8,384]{2,1,0:T(8,128)}, u32[]{:S(2)}, u32[]{:S(2)}) collective-permute-start(f32[144,8,384]{2,1,0:T(8,128)} %get-tuple-element.256), channel_id=1, source_target_pairs={{0,16},{2,18},{4,20},{6,22},{8,24},{10,26},{12,28},{14,30},{16,0},... | collective-permute-start | bytes 5308424 | tf_op jit(solution)/shard_map/ppermute | solution.py:475
  312.6 29.1 %collective-permute-start.28 = (f32[4,4,2,3,8,384]{5,4,3,2,1,0:T(8,128)}, f32[4,4,2,3,8,384]{5,4,3,2,1,0:T(8,128)S(1)}, u32[]{:S(2)}, u32[]{:S(2)}) collective-permute-start(f32[4,4,2,3,8,384]{5,4,3,2,1,0:T(8,128)} %get-tuple-element.249), channel_id=1, source_target_pairs={{0,2},{2,0},{4,6},{6,4},{8,10},{10,8},{12,14},{14,12},{16,18},{18,... | collective-permute-start | bytes 3538952 | tf_op jit(solution)/shard_map/ppermute | solution.py:475
  313.7 44.9 %collective-permute-start.29 = (f32[4,4,2,3,8,384]{5,4,3,2,1,0:T(8,128)}, f32[4,4,2,3,8,384]{5,4,3,2,1,0:T(8,128)S(1)}, u32[]{:S(2)}, u32[]{:S(2)}) collective-permute-start(f32[4,4,2,3,8,384]{5,4,3,2,1,0:T(8,128)} %get-tuple-element.250), channel_id=1, source_target_pairs={{0,4},{2,6},{4,0},{6,2},{8,12},{10,14},{12,8},{14,10},{16,20},{18,... | collective-permute-start | bytes 3538952 | tf_op jit(solution)/shard_map/ppermute | solution.py:475
  314.7 43.9 %collective-permute-start.30 = (f32[4,4,2,3,8,384]{5,4,3,2,1,0:T(8,128)}, f32[4,4,2,3,8,384]{5,4,3,2,1,0:T(8,128)S(1)}, u32[]{:S(2)}, u32[]{:S(2)}) collective-permute-start(f32[4,4,2,3,8,384]{5,4,3,2,1,0:T(8,128)} %get-tuple-element.251), channel_id=1, source_target_pairs={{0,6},{2,4},{4,2},{6,0},{8,14},{10,12},{12,10},{14,8},{16,22},{18,... | collective-permute-start | bytes 3538952 | tf_op jit(solution)/shard_map/ppermute | solution.py:475
  366.5 116.0 %collective-permute-start.35 = (f32[168,8,384]{2,1,0:T(8,128)}, f32[168,8,384]{2,1,0:T(8,128)S(1)}, u32[]{:S(2)}, u32[]{:S(2)}) collective-permute-start(f32[168,8,384]{2,1,0:T(8,128)} %get-tuple-element.265), channel_id=1, source_target_pairs={{0,8},{2,10},{4,12},{6,14},{8,0},{10,2},{12,4},{14,6},{16,24},{18,... | collective-permute-start | bytes 6193160 | tf_op jit(solution)/shard_map/ppermute | solution.py:475
  389.1 93.4 %collective-permute-start.34 = (f32[144,8,384]{2,1,0:T(8,128)}, f32[144,8,384]{2,1,0:T(8,128)}, u32[]{:S(2)}, u32[]{:S(2)}) collective-permute-start(f32[144,8,384]{2,1,0:T(8,128)} %get-tuple-element.259), channel_id=1, source_target_pairs={{0,16},{2,18},{4,20},{6,22},{8,24},{10,26},{12,28},{14,30},{16,0},... | collective-permute-start | bytes 5308424 | tf_op jit(solution)/shard_map/ppermute | solution.py:475
  391.2 29.1 %collective-permute-start.36 = (f32[4,4,2,3,8,384]{5,4,3,2,1,0:T(8,128)}, f32[4,4,2,3,8,384]{5,4,3,2,1,0:T(8,128)S(1)}, u32[]{:S(2)}, u32[]{:S(2)}) collective-permute-start(f32[4,4,2,3,8,384]{5,4,3,2,1,0:T(8,128)} %get-tuple-element.270), channel_id=1, source_target_pairs={{0,2},{2,0},{4,6},{6,4},{8,10},{10,8},{12,14},{14,12},{16,18},{18,... | collective-permute-start | bytes 3538952 | tf_op jit(solution)/shard_map/ppermute | solution.py:475
  391.8 43.1 %collective-permute-start.37 = (f32[4,4,2,3,8,384]{5,4,3,2,1,0:T(8,128)}, f32[4,4,2,3,8,384]{5,4,3,2,1,0:T(8,128)S(1)}, u32[]{:S(2)}, u32[]{:S(2)}) collective-permute-start(f32[4,4,2,3,8,384]{5,4,3,2,1,0:T(8,128)} %get-tuple-element.271), channel_id=1, source_target_pairs={{0,4},{2,6},{4,0},{6,2},{8,12},{10,14},{12,8},{14,10},{16,20},{18,... | collective-permute-start | bytes 3538952 | tf_op jit(solution)/shard_map/ppermute | solution.py:475
  392.6 42.3 %collective-permute-start.38 = (f32[4,4,2,3,8,384]{5,4,3,2,1,0:T(8,128)}, f32[4,4,2,3,8,384]{5,4,3,2,1,0:T(8,128)S(1)}, u32[]{:S(2)}, u32[]{:S(2)}) collective-permute-start(f32[4,4,2,3,8,384]{5,4,3,2,1,0:T(8,128)} %get-tuple-element.272), channel_id=1, source_target_pairs={{0,6},{2,4},{4,2},{6,0},{8,14},{10,12},{12,10},{14,8},{16,22},{18,... | collective-permute-start | bytes 3538952 | tf_op jit(solution)/shard_map/ppermute | solution.py:475
  442.8 105.9 %collective-permute-start.47 = (f32[168,8,384]{2,1,0:T(8,128)}, f32[168,8,384]{2,1,0:T(8,128)}, u32[]{:S(2)}, u32[]{:S(2)}) collective-permute-start(f32[168,8,384]{2,1,0:T(8,128)} %get-tuple-element.287), channel_id=1, source_target_pairs={{0,8},{2,10},{4,12},{6,14},{8,0},{10,2},{12,4},{14,6},{16,24},{18,... | collective-permute-start | bytes 6193160 | tf_op jit(solution)/shard_map/ppermute | solution.py:475
  488.8 73.3 %collective-permute-start.46 = (f32[144,8,384]{2,1,0:T(8,128)}, f32[144,8,384]{2,1,0:T(8,128)}, u32[]{:S(2)}, u32[]{:S(2)}) collective-permute-start(f32[144,8,384]{2,1,0:T(8,128)} %get-tuple-element.286), channel_id=1, source_target_pairs={{0,16},{2,18},{4,20},{6,22},{8,24},{10,26},{12,28},{14,30},{16,0},... | collective-permute-start | bytes 5308424 | tf_op jit(solution)/shard_map/ppermute | solution.py:475
  489.7 29.1 %collective-permute-start.40 = (f32[4,4,2,3,8,384]{5,4,3,2,1,0:T(8,128)}, f32[4,4,2,3,8,384]{5,4,3,2,1,0:T(8,128)S(1)}, u32[]{:S(2)}, u32[]{:S(2)}) collective-permute-start(f32[4,4,2,3,8,384]{5,4,3,2,1,0:T(8,128)} %get-tuple-element.276), channel_id=1, source_target_pairs={{0,4},{2,6},{4,0},{6,2},{8,12},{10,14},{12,8},{14,10},{16,20},{18,... | collective-permute-start | bytes 3538952 | tf_op jit(solution)/shard_map/ppermute | solution.py:475
  489.7 29.1 %collective-permute-start.41 = (f32[4,4,2,3,8,384]{5,4,3,2,1,0:T(8,128)}, f32[4,4,2,3,8,384]{5,4,3,2,1,0:T(8,128)S(1)}, u32[]{:S(2)}, u32[]{:S(2)}) collective-permute-start(f32[4,4,2,3,8,384]{5,4,3,2,1,0:T(8,128)} %get-tuple-element.277), channel_id=1, source_target_pairs={{0,6},{2,4},{4,2},{6,0},{8,14},{10,12},{12,10},{14,8},{16,22},{18,... | collective-permute-start | bytes 3538952 | tf_op jit(solution)/shard_map/ppermute | solution.py:475
  526.6 84.9 %collective-permute-start.49 = (f32[168,8,384]{2,1,0:T(8,128)}, f32[168,8,384]{2,1,0:T(8,128)S(1)}, u32[]{:S(2)}, u32[]{:S(2)}) collective-permute-start(f32[168,8,384]{2,1,0:T(8,128)} %get-tuple-element.295), channel_id=1, source_target_pairs={{0,8},{2,10},{4,12},{6,14},{8,0},{10,2},{12,4},{14,6},{16,24},{18,... | collective-permute-start | bytes 6193160 | tf_op jit(solution)/shard_map/ppermute | solution.py:475
  567.5 68.4 %collective-permute-start.48 = (f32[144,8,384]{2,1,0:T(8,128)}, f32[144,8,384]{2,1,0:T(8,128)S(1)}, u32[]{:S(2)}, u32[]{:S(2)}) collective-permute-start(f32[144,8,384]{2,1,0:T(8,128)} %get-tuple-element.289), channel_id=1, source_target_pairs={{0,16},{2,18},{4,20},{6,22},{8,24},{10,26},{12,28},{14,30},{16,0},... | collective-permute-start | bytes 5308424 | tf_op jit(solution)/shard_map/ppermute | solution.py:475
  567.5 29.1 %collective-permute-start.51 = (f32[4,4,2,3,8,384]{5,4,3,2,1,0:T(8,128)}, f32[4,4,2,3,8,384]{5,4,3,2,1,0:T(8,128)S(1)}, u32[]{:S(2)}, u32[]{:S(2)}) collective-permute-start(f32[4,4,2,3,8,384]{5,4,3,2,1,0:T(8,128)} %get-tuple-element.301), channel_id=1, source_target_pairs={{0,4},{2,6},{4,0},{6,2},{8,12},{10,14},{12,8},{14,10},{16,20},{18,... | collective-permute-start | bytes 3538952 | tf_op jit(solution)/shard_map/ppermute | solution.py:475
  567.5 29.1 %collective-permute-start.52 = (f32[4,4,2,3,8,384]{5,4,3,2,1,0:T(8,128)}, f32[4,4,2,3,8,384]{5,4,3,2,1,0:T(8,128)S(1)}, u32[]{:S(2)}, u32[]{:S(2)}) collective-permute-start(f32[4,4,2,3,8,384]{5,4,3,2,1,0:T(8,128)} %get-tuple-element.302), channel_id=1, source_target_pairs={{0,6},{2,4},{4,2},{6,0},{8,14},{10,12},{12,10},{14,8},{16,22},{18,... | collective-permute-start | bytes 3538952 | tf_op jit(solution)/shard_map/ppermute | solution.py:475
  583.5 60.2 %collective-permute-start.42 = (f32[256,768]{1,0:T(8,128)}, f32[256,768]{1,0:T(8,128)}, u32[]{:S(2)}, u32[]{:S(2)}) collective-permute-start(f32[256,768]{1,0:T(8,128)} %get-tuple-element.281), channel_id=1, source_target_pairs={{0,1},{1,0},{2,3},{3,2},{4,5},{5,4},{6,7},{7,6},{8,9},{9,8},{10,11... | collective-permute-start | bytes 2359304 | tf_op jit(solution)/shard_map/ppermute | solution.py:528
  596.6 45.4 %collective-permute-start.19 = (f32[160,768]{1,0:T(8,128)}, f32[160,768]{1,0:T(8,128)}, u32[]{:S(2)}, u32[]{:S(2)}) collective-permute-start(f32[160,768]{1,0:T(8,128)} %get-tuple-element.227), channel_id=1, source_target_pairs={{0,1},{1,0},{2,3},{3,2},{4,5},{5,4},{6,7},{7,6},{8,9},{9,8},{10,11... | collective-permute-start | bytes 1474568 | tf_op jit(solution)/shard_map/ppermute | solution.py:528
  596.6 47.0 %collective-permute-start.31 = (f32[160,768]{1,0:T(8,128)}, f32[160,768]{1,0:T(8,128)}, u32[]{:S(2)}, u32[]{:S(2)}) collective-permute-start(f32[160,768]{1,0:T(8,128)} %get-tuple-element.255), channel_id=1, source_target_pairs={{0,1},{1,0},{2,3},{3,2},{4,5},{5,4},{6,7},{7,6},{8,9},{9,8},{10,11... | collective-permute-start | bytes 1474568 | tf_op jit(solution)/shard_map/ppermute | solution.py:528
  611.5 100.7 %collective-permute-start.61 = (f32[168,8,384]{2,1,0:T(8,128)}, f32[168,8,384]{2,1,0:T(8,128)}, u32[]{:S(2)}, u32[]{:S(2)}) collective-permute-start(f32[168,8,384]{2,1,0:T(8,128)} %get-tuple-element.317), channel_id=1, source_target_pairs={{0,8},{2,10},{4,12},{6,14},{8,0},{10,2},{12,4},{14,6},{16,24},{18,... | collective-permute-start | bytes 6193160 | tf_op jit(solution)/shard_map/ppermute | solution.py:475
  642.0 70.2 %collective-permute-start.62 = (f32[144,8,384]{2,1,0:T(8,128)}, f32[144,8,384]{2,1,0:T(8,128)S(1)}, u32[]{:S(2)}, u32[]{:S(2)}) collective-permute-start(f32[144,8,384]{2,1,0:T(8,128)} %get-tuple-element.319), channel_id=1, source_target_pairs={{0,16},{2,18},{4,20},{6,22},{8,24},{10,26},{12,28},{14,30},{16,0},... | collective-permute-start | bytes 5308424 | tf_op jit(solution)/shard_map/ppermute | solution.py:475
  685.4 50.6 %collective-permute-start.57 = (f32[96,8,384]{2,1,0:T(8,128)}, f32[96,8,384]{2,1,0:T(8,128)S(1)}, u32[]{:S(2)}, u32[]{:S(2)}) collective-permute-start(f32[96,8,384]{2,1,0:T(8,128)} %get-tuple-element.312), channel_id=1, source_target_pairs={{0,8},{2,10},{4,12},{6,14},{8,0},{10,2},{12,4},{14,6},{16,24},{18,... | collective-permute-start | bytes 3538952 | tf_op jit(solution)/shard_map/ppermute | solution.py:475
  718.4 102.6 %collective-permute-start.63 = (f32[144,8,384]{2,1,0:T(8,128)}, f32[144,8,384]{2,1,0:T(8,128)S(1)}, u32[]{:S(2)}, u32[]{:S(2)}) collective-permute-start(f32[144,8,384]{2,1,0:T(8,128)} %get-tuple-element.320), channel_id=1, source_target_pairs={{0,16},{2,18},{4,20},{6,22},{8,24},{10,26},{12,28},{14,30},{16,0},... | collective-permute-start | bytes 5308424 | tf_op jit(solution)/shard_map/ppermute | solution.py:475
  719.7 28.2 %collective-permute-start.65 = (f32[4,4,1,3,8,384]{5,4,3,2,1,0:T(8,128)}, f32[4,4,1,3,8,384]{5,4,3,2,1,0:T(8,128)S(1)}, u32[]{:S(2)}, u32[]{:S(2)}) collective-permute-start(f32[4,4,1,3,8,384]{5,4,3,2,1,0:T(8,128)} %get-tuple-element.326), channel_id=1, source_target_pairs={{0,4},{2,6},{4,0},{6,2},{8,12},{10,14},{12,8},{14,10},{16,20},{18,... | collective-permute-start | bytes 1769480 | tf_op jit(solution)/shard_map/ppermute | solution.py:475
  719.7 29.4 %collective-permute-start.66 = (f32[4,4,1,3,8,384]{5,4,3,2,1,0:T(8,128)}, f32[4,4,1,3,8,384]{5,4,3,2,1,0:T(8,128)S(1)}, u32[]{:S(2)}, u32[]{:S(2)}) collective-permute-start(f32[4,4,1,3,8,384]{5,4,3,2,1,0:T(8,128)} %get-tuple-element.327), channel_id=1, source_target_pairs={{0,6},{2,4},{4,2},{6,0},{8,14},{10,12},{12,10},{14,8},{16,22},{18,... | collective-permute-start | bytes 1769480 | tf_op jit(solution)/shard_map/ppermute | solution.py:475
  755.3 80.5 %collective-permute-start.68 = (f32[96,8,384]{2,1,0:T(8,128)}, f32[96,8,384]{2,1,0:T(8,128)S(1)}, u32[]{:S(2)}, u32[]{:S(2)}) collective-permute-start(f32[96,8,384]{2,1,0:T(8,128)} %get-tuple-element.335), channel_id=1, source_target_pairs={{0,8},{2,10},{4,12},{6,14},{8,0},{10,2},{12,4},{14,6},{16,24},{18,... | collective-permute-start | bytes 3538952 | tf_op jit(solution)/shard_map/ppermute | solution.py:475
  758.6 89.8 %collective-permute-start.75 = (f32[84,8,384]{2,1,0:T(8,128)}, f32[84,8,384]{2,1,0:T(8,128)S(1)}, u32[]{:S(2)}, u32[]{:S(2)}) collective-permute-start(f32[84,8,384]{2,1,0:T(8,128)} %get-tuple-element.341), channel_id=1, source_target_pairs={{0,16},{2,18},{4,20},{6,22},{8,24},{10,26},{12,28},{14,30},{16,0},... | collective-permute-start | bytes 3096584 | tf_op jit(solution)/shard_map/ppermute | solution.py:475
  852.8 42.0 %collective-permute-start.76 = (f32[84,8,384]{2,1,0:T(8,128)}, f32[84,8,384]{2,1,0:T(8,128)S(1)}, u32[]{:S(2)}, u32[]{:S(2)}) collective-permute-start(f32[84,8,384]{2,1,0:T(8,128)} %get-tuple-element.342), channel_id=1, source_target_pairs={{0,16},{2,18},{4,20},{6,22},{8,24},{10,26},{12,28},{14,30},{16,0},... | collective-permute-start | bytes 3096584 | tf_op jit(solution)/shard_map/ppermute | solution.py:475
  907.2 30.0 %collective-permute-start.73 = (f32[128,768]{1,0:T(8,128)S(1)}, f32[128,768]{1,0:T(8,128)S(1)}, u32[]{:S(2)}, u32[]{:S(2)}) collective-permute-start(f32[128,768]{1,0:T(8,128)S(1)} %copy-done.17), channel_id=1, source_target_pairs={{0,16},{2,18},{4,20},{6,22},{8,24},{10,26},{12,28},{14,30},{16,0},... | collective-permute-start | bytes 1179656 | tf_op jit(solution)/shard_map/ppermute | solution.py:475
  (109 other events, 1055.5 us)
